TPU v7x, 32 devices: a whole 2x2x4 slice. The times are simulated.
32 devices in a mesh: snap: 8 (over z, y), space: 4 (over x, core).
Axes of the slice: x: 2, y: 2, z: 4, core: 2. Of those that a mesh axis runs over, the one named last changes fastest.
Arguments:
- snapshots: bfloat16 [1024, 2, 16, 720], P('snap', None, 'space'), may hold values from -6 to 6
- lon_coeff: float32 [2, 16, 720], P(None, 'space'), may hold values from 0.05 to 0.24
- lat_coeff: float32 [2, 16, 720], P(None, 'space'), may hold values from 0.1 to 0.24
Outputs:
- gram: float32 [1024, 1024], P('snap', 'space')
All inputs are finite; a program needn't handle non-finite values.
Results may differ from a plain program's by a relative error of at most 0.00062.
Values may be sent and summed in bfloat16 or wider, within the bound.
No kernel may reach another device: no remote copies, remote signals or barrier semaphores. Data moves between devices by JAX's collectives and lax.ppermute only.
A program may use at most 128 MiB of HBM per device.

v0:
```python
import math

import jax
import jax.numpy as jnp
from jax import lax
from jax.sharding import PartitionSpec as P


def padded_2(cells, sides, width):
    for axis, dim in sides:
        count = lax.axis_size(axis)
        ends = count - 1
        head = lax.slice_in_dim(cells, 0, width, axis=dim)
        tail = lax.slice_in_dim(cells, cells.shape[dim] - width, cells.shape[dim], axis=dim)
        cells = jnp.concatenate(
            [
                lax.ppermute(tail, axis, [(i, (i + 1) % count) for i in range(ends)]),
                cells,
                lax.ppermute(head, axis, [((i + 1) % count, i) for i in range(ends)]),
            ],
            axis=dim,
        )
    return cells


def inner_tile(left, right):
    return lax.dot_general(
        left, right, (((1,), (1,)), ((), ())), preferred_element_type=jnp.float32
    )


def shards(snapshots, lon_coeff, lat_coeff):
    snap_rows, fields, rows, nlon = snapshots.shape
    bands = lax.axis_size("space")
    padded = padded_2(snapshots, (("space", 2),), 1).astype(jnp.float32)
    values = snapshots.astype(jnp.float32)
    lon_part = jnp.roll(values, 1, axis=3) + jnp.roll(values, -1, axis=3) - 2.0 * values
    lat_part = padded[:, :, 2:] + padded[:, :, :-2] - 2.0 * values
    smooth = values + lon_coeff * lon_part + lat_coeff * lat_part
    nlat = bands * rows
    every_row = jnp.arange(nlat).astype(jnp.float32)
    every_cos = jnp.cos((45.0 + 0.5 * (every_row + 0.5 - nlat / 2.0)) * (math.pi / 180.0))
    total = fields * nlon * jnp.sum(every_cos)
    my_rows = (lax.axis_index("space") * rows + jnp.arange(rows)).astype(jnp.float32)
    cosine = jnp.cos((45.0 + 0.5 * (my_rows + 0.5 - nlat / 2.0)) * (math.pi / 180.0))
    factor = jnp.sqrt(cosine) * total ** (-0.25)
    scaled = (smooth * factor[:, None]).astype(jnp.bfloat16).reshape(snap_rows, -1)
    partial_value = inner_tile(scaled, lax.all_gather(scaled, "snap", axis=0, tiled=True))
    return lax.psum_scatter(partial_value, "space", scatter_dimension=1, tiled=True)


def solution(mesh):
    return jax.shard_map(
        shards,
        mesh=mesh,
        in_specs=(P("snap", None, "space", None), P(None, "space", None), P(None, "space", None)),
        out_specs=P("snap", "space"),
        check_vma=False,
    )
```

profile of v0, /device:TPU:0, one launch (start us, length us, event | category | flops | bytes accessed | tf_op | source)
XLA Modules:
  0.0 226.8 jit_solution(15903471929560043048)
XLA Ops:
  6.5 0.0 all-gather.2.cloned.1.call-start
  6.5 1.3 fusion.10
  7.8 2.4 %collective-permute-start = (bf16[128,2,1,720]{0,3,2,1:T(8,128)(2,1)S(1)}, bf16[128,2,1,720]{0,3,2,1:T(8,128)(2,1)S(1)}, u32[]{:S(2)}, u32[]{:S(2)}) collective-permute-start(bf16[128,2,1,720]{0,3,2,1:T(8,128)(2,1)S(1)} %get-tuple-element.9), channel_id=1, source_target_pairs={{0,1},{1,2},{2,3},{4,5},{5,6},{6,7},{8,9},{9,10},{10,11},{12,13},{... | collective-permute-start | bytes 1105928 | tf_op jit(solution)/shard_map/ppermute | solution.py:17
  10.2 1.3 collective-permute-start.1
  11.5 0.6 cosine_reduce_fusion
  12.1 0.8 fusion.9
  13.6 0.1 sqrt_multiply_fusion
  13.7 0.0 copy-done
  13.7 0.4 fusion.8
  14.1 0.0 copy-start.2
  14.1 0.0 copy-start.3
  14.1 0.0 collective-permute-done
  14.1 1.8 collective-permute-done.1
  15.9 0.3 maximum_convert_fusion
  16.2 0.0 copy-done.2
  16.2 0.0 copy-done.3
  16.2 4.0 %fusion.4 = bf16[128,2,4,720]{0,3,2,1:T(8,128)(2,1)} fusion(f32[128,2,6,720]{0,3,2,1:T(8,128)S(1)} %maximum_convert_fusion, f32[128,2,4,719]{0,3,2,1:T(8,128)S(1)} %get-tuple-element.6, f32[128,2,4,1]{0,3,2,1:T(1,128)S(1)} %get-tuple-element.8, f32[128,2,4,1]{0,3,2,1:T(1,128)S(1)} %get-tuple-element.7, f32[128,2,4,719]{0,3,2,1:T(8,128)S(1)} %get-tuple-element.5, ...), kind=kLoop, calls=%fused_computation.5 | loop fusion | flops 10321920 | bytes 14791696 | tf_op jit(solution)/shard_map/convert_element_type | solution.py:47
  20.2 0.0 all-gather.2.cloned.1.call-update
  20.2 0.0 reduce-scatter.2.cloned.1.call-start
  20.3 172.8 %all-gather.2.cloned.1.call-done = bf16[1024,5760]{0,1:T(8,128)(2,1)} async-done(((bf16[128,5760]{0,1:T(8,128)(2,1)}), bf16[1024,5760]{0,1:T(8,128)(2,1)}) %all-gather.2.cloned.1.call-update) | async-done | bytes 11796496 | tf_op jit(solution)/shard_map/all_gather | solution.py:48
  193.1 0.0 copy-done.1
  193.1 6.9 %fusion.11 = f32[128,1024]{1,0:T(8,128)} fusion(bf16[128,5760]{0,1:T(8,128)(2,1)S(1)} %bitcast.4, bf16[1024,5760]{0,1:T(8,128)(2,1)} %all-gather.2.cloned.1.call-done), kind=kOutput, calls=%fused_computation.16 | convolution fusion | flops 1509949440 | bytes 13795328 | tf_op jit(solution)/shard_map/dot_general | solution.py:27
  200.0 0.0 reduce-scatter.2.cloned.1.call-update
  200.0 20.0 %reduce-scatter.2.cloned.1.call-done = f32[128,256]{1,0:T(8,128)} async-done(((f32[128,1024]{1,0:T(8,128)}), f32[128,256]{1,0:T(8,128)}) %reduce-scatter.2.cloned.1.call-update) | async-done | bytes 131088 | tf_op jit(solution)/shard_map/reduce_scatter | solution.py:49
  (2 shorter events, 0.0 us)
Async XLA Ops:
  6.5 7.1 %copy-start = (bf16[128,2,4,720]{0,3,2,1:T(8,128)(2,1)S(1)}, bf16[128,2,4,720]{0,3,2,1:T(8,128)(2,1)}, u32[]{:S(2)}) copy-start(bf16[128,2,4,720]{0,3,2,1:T(8,128)(2,1)} %param.3) | copy-start | bytes 4423684
  6.5 186.6 %all-gather.2.cloned.1.call-start = ((), (), s32[]{:S(2)}) async-start(), calls=%async_computation.1 | async-start | bytes 13271040 | tf_op jit(solution)/shard_map/all_gather | solution.py:48
  7.8 6.3 %collective-permute-start = (bf16[128,2,1,720]{0,3,2,1:T(8,128)(2,1)S(1)}, bf16[128,2,1,720]{0,3,2,1:T(8,128)(2,1)S(1)}, u32[]{:S(2)}, u32[]{:S(2)}) collective-permute-start(bf16[128,2,1,720]{0,3,2,1:T(8,128)(2,1)S(1)} %get-tuple-element.9), channel_id=1, source_target_pairs={{0,1},{1,2},{2,3},{4,5},{5,6},{6,7},{8,9},{9,10},{10,11},{12,13},{... | collective-permute-start | bytes 1105928 | tf_op jit(solution)/shard_map/ppermute | solution.py:17
  10.2 5.7 %collective-permute-start.1 = (bf16[128,2,1,720]{0,3,2,1:T(8,128)(2,1)S(1)}, bf16[128,2,1,720]{0,3,2,1:T(8,128)(2,1)S(1)}, u32[]{:S(2)}, u32[]{:S(2)}) collective-permute-start(bf16[128,2,1,720]{0,3,2,1:T(8,128)(2,1)S(1)} %get-tuple-element.10), channel_id=1, source_target_pairs={{1,0},{2,1},{3,2},{5,4},{6,5},{7,6},{9,8},{10,9},{11,10},{13,12},{... | collective-permute-start | bytes 1105928 | tf_op jit(solution)/shard_map/ppermute | solution.py:19
  14.1 2.1 copy-start.2
  14.1 2.1 copy-start.3
  20.2 172.9 %copy-start.1 = (bf16[128,2,4,720]{0,3,2,1:T(8,128)(2,1)S(1)}, bf16[128,2,4,720]{0,3,2,1:T(8,128)(2,1)}, u32[]{:S(2)}) copy-start(bf16[128,2,4,720]{0,3,2,1:T(8,128)(2,1)} %fusion.4) | copy-start | bytes 4423684
  20.2 199.7 %reduce-scatter.2.cloned.1.call-start = ((), (), s32[]{:S(2)}) async-start(), calls=%async_computation.2 | async-start | bytes 655360 | tf_op jit(solution)/shard_map/reduce_scatter | solution.py:49
Sparse Core Ops, SparseCore 0:
  20.4 172.6 all-gather.1
  200.1 19.7 reduce-scatter.1
where the time goes:
time: 227 us
  waiting for transfers between devices  195 us (86%)
  between operations  14.2 us (6%)
  matrix products  6.89 us (3%)
  other arithmetic  5.04 us (2%)
  starting transfers between devices  3.72 us (2%)
  local copies, waits for them, and re-layouts  2.42 us (1%)
    all_gather x1, waiting for transfers between devices, shards(): lax.all_gather(scaled, 'snap', axis=0, tiled=True)  173 us
    reduce_scatter x1, waiting for transfers between devices, shards(): lax.psum_scatter(partial_value, 'space', scatter_dimension=1, tiled=True)  20 us
    dot_general x1, matrix products, inner_tile(): lax.dot_general(left, right, (((1,), (1,)), ((), ())), preferred_element_...  6.89 us
  transfers between devices with their start and end apart: 4, of which 3 were waited for; matrix products, arithmetic and copies ran while one was open for 1% of the time, Pallas kernels for 0%

commit v1 on v0

v1 whole, which is shorter than its diff:
```python
import math

import jax
import jax.numpy as jnp
from jax import lax
from jax.sharding import PartitionSpec as P


def flip(cells, axis, bits):
    count = lax.axis_size(axis)
    return lax.ppermute(cells, axis, [(i, i ^ bits) for i in range(count)])


def scaled_cells(cells, lon_coeff, lat_coeff):
    fields, rows, nlon, snaps = cells.shape
    bands = lax.axis_size("space")
    ends = bands - 1
    above = lax.ppermute(cells[:, rows - 1 :], "space", [(i, i + 1) for i in range(ends)])
    below = lax.ppermute(cells[:, :1], "space", [(i + 1, i) for i in range(ends)])
    padded = jnp.concatenate([above, cells, below], axis=1).astype(jnp.float32)
    values = cells.astype(jnp.float32)
    lon_part = jnp.roll(values, 1, axis=2) + jnp.roll(values, -1, axis=2) - 2.0 * values
    lat_part = padded[:, 2:] + padded[:, :-2] - 2.0 * values
    smooth = values + lon_coeff[..., None] * lon_part + lat_coeff[..., None] * lat_part
    nlat = bands * rows
    every_row = jnp.arange(nlat).astype(jnp.float32)
    every_cos = jnp.cos((45.0 + 0.5 * (every_row + 0.5 - nlat / 2.0)) * (math.pi / 180.0))
    total = fields * nlon * jnp.sum(every_cos)
    my_rows = (lax.axis_index("space") * rows + jnp.arange(rows)).astype(jnp.float32)
    cosine = jnp.cos((45.0 + 0.5 * (my_rows + 0.5 - nlat / 2.0)) * (math.pi / 180.0))
    factor = jnp.sqrt(cosine) * total ** (-0.25)
    return (smooth * factor[:, None, None]).astype(jnp.bfloat16)


def shards(snapshots, lon_coeff, lat_coeff):
    snaps, fields, rows, nlon = snapshots.shape
    groups, bands = lax.axis_size("snap"), lax.axis_size("space")
    layers, columns = groups // 2, bands // 2
    me, band = lax.axis_index("snap"), lax.axis_index("space")
    layer, column, core = me // 2, band // 2, band % 2
    scaled = scaled_cells(jnp.transpose(snapshots, (1, 2, 3, 0)), lon_coeff, lat_coeff)
    slices = scaled.reshape(layers, -1, snaps)
    held = []
    for j in range(layers):
        mine = lax.dynamic_index_in_dim(slices, layer ^ j, 0, keepdims=False)
        held.append(flip(mine, "snap", 2 * j) if j else mine)
    other = [flip(piece, "snap", 1) for piece in held]
    stack = jnp.stack([piece for pair in zip(held, other) for piece in pair])
    stack = jnp.concatenate([stack, flip(stack, "space", 1)], axis=1)
    left = jnp.concatenate([stack[2 * j] for j in range(layers)], axis=1)
    share = groups // bands
    right = []
    for i in range(columns):
        for g in range(share):
            group = ((column ^ i) * 2 + core) * share + g
            right.append(lax.dynamic_index_in_dim(stack, group ^ me, 0, keepdims=False))
    right = jnp.concatenate(right, axis=1)
    product = lax.dot_general(
        left, right, (((0,), (0,)), ((), ())), preferred_element_type=jnp.float32
    )
    product = product.reshape(layers, snaps, columns, share * snaps)
    total = product[0, :, 0]
    for j in range(layers):
        for i in range(columns):
            if i or j:
                pairs = [
                    (s * bands + b, (s ^ (2 * j)) * bands + (b ^ (2 * i)))
                    for s in range(groups)
                    for b in range(bands)
                ]
                total += lax.ppermute(product[j, :, i], ("snap", "space"), pairs)
    return total


def solution(mesh):
    return jax.shard_map(
        shards,
        mesh=mesh,
        in_specs=(P("snap", None, "space", None), P(None, "space", None), P(None, "space", None)),
        out_specs=P("snap", "space"),
        check_vma=False,
    )
```

time: 227 us -> 109 us (0.48)
  waiting for transfers between devices: 195 us -> 64 us
  starting transfers between devices: 3.72 us -> 26.1 us
  between operations: 14.2 us -> 1.05 us
  other arithmetic: 5.04 us -> 11.3 us
  matrix products: 6.89 us -> 1.81 us
    all_gather x1 -> x0, waiting for transfers between devices: 173 us -> none  [shards(): lax.all_gather(scaled, 'snap', axis=0, tiled=True)]
    ppermute x2 -> x17, waiting for transfers between devices: 1.77 us -> 64 us  [the longest x8 50.1 us: flip(): return lax.ppermute(cells, axis, [(i, i ^ bits) for i in range(count)])]
    ppermute x2 -> x17, starting transfers between devices: 3.67 us -> 26.1 us  [the longest x7 12.1 us: shards(): total += lax.ppermute(product[j, :, i], ('snap', 'space'), pairs)]
    reduce_scatter x1 -> x0, waiting for transfers between devices: 20 us -> none  [shards(): lax.psum_scatter(partial_value, 'space', scatter_dimension=1, tiled=True)]
    dot_general x1, matrix products: 6.89 us -> 1.81 us  [shards(): lax.dot_general(left, right, (((0,), (0,)), ((), ())), preferred_element_...]
    squeeze x0 -> x2, other arithmetic: none -> 3.92 us  [shards(): right.append(lax.dynamic_index_in_dim(stack, group ^ me, 0, keepdims=False))]
    convert_element_type x2 -> x3, other arithmetic: 4.34 us -> 5.93 us  [the longest x1 3.04 us: scaled_cells(): return (smooth * factor[:, None, None]).astype(jnp.bfloat16)]
  transfers between devices with their start and end apart: 4 -> 17, of which waited for: 3 -> 9; matrix products, arithmetic and copies ran while one was open for 1% -> 3% of each run, Pallas kernels for 0% -> 0%
where the time goes in v1:
time: 109 us
  waiting for transfers between devices  64 us (59%)
  starting transfers between devices  26.1 us (24%)
  other arithmetic  11.3 us (10%)
  local copies, waits for them, and re-layouts  4.53 us (4%)
  matrix products  1.81 us (2%)
    ppermute x8, waiting for transfers between devices, flip(): return lax.ppermute(cells, axis, [(i, i ^ bits) for i in range(count)])  50.1 us
    ppermute x7, waiting for transfers between devices, shards(): total += lax.ppermute(product[j, :, i], ('snap', 'space'), pairs)  12.7 us
    ppermute x7, starting transfers between devices, shards(): total += lax.ppermute(product[j, :, i], ('snap', 'space'), pairs)  12.1 us
    ppermute x8, starting transfers between devices, flip(): return lax.ppermute(cells, axis, [(i, i ^ bits) for i in range(count)])  10.3 us
    squeeze x2, other arithmetic, shards(): right.append(lax.dynamic_index_in_dim(stack, group ^ me, 0, keepdims=False))  3.92 us
    convert_element_type x1, other arithmetic, scaled_cells(): return (smooth * factor[:, None, None]).astype(jnp.bfloat16)  3.04 us
    ppermute x1, starting transfers between devices, scaled_cells(): lax.ppermute(cells[:, rows - 1:], 'space', [(i, i + 1) for i in range(end...  2.37 us
  transfers between devices with their start and end apart: 17, of which 9 were waited for; matrix products, arithmetic and copies ran while one was open for 3% of the time, Pallas kernels for 0%

profile of v1, /device:TPU:0, one launch (start us, length us, event | category | flops | bytes accessed | tf_op | source)
XLA Modules:
  0.0 108.7 jit_solution(15389661156500924987)
XLA Ops:
  0.0 2.0 %fusion.49 = (bf16[2,1,720,128]{3,2,1,0:T(8,128)(2,1)}, bf16[2,1,720,128]{3,2,1,0:T(8,128)(2,1)}) fusion(bf16[2,4,720,128]{3,2,1,0:T(8,128)(2,1)} %bitcast.79), kind=kLoop, calls=%fused_computation.91 | loop fusion | bytes 1474560 | tf_op jit(solution)/shard_map/slice | solution.py:18
  2.0 2.4 %collective-permute-start = (bf16[2,1,720,128]{3,2,1,0:T(8,128)(2,1)}, bf16[2,1,720,128]{3,2,1,0:T(8,128)(2,1)S(1)}, u32[]{:S(2)}, u32[]{:S(2)}) collective-permute-start(bf16[2,1,720,128]{3,2,1,0:T(8,128)(2,1)} %get-tuple-element.21), channel_id=1, source_target_pairs={{0,1},{1,2},{2,3},{4,5},{5,6},{6,7},{8,9},{9,10},{10,11},{12,13},{... | collective-permute-start | bytes 1105928 | tf_op jit(solution)/shard_map/ppermute | solution.py:18
  4.4 1.3 %collective-permute-start.1 = (bf16[2,1,720,128]{3,2,1,0:T(8,128)(2,1)}, bf16[2,1,720,128]{3,2,1,0:T(8,128)(2,1)}, u32[]{:S(2)}, u32[]{:S(2)}) collective-permute-start(bf16[2,1,720,128]{3,2,1,0:T(8,128)(2,1)} %get-tuple-element.22), channel_id=1, source_target_pairs={{1,0},{2,1},{3,2},{5,4},{6,5},{7,6},{9,8},{10,9},{11,10},{13,12},{... | collective-permute-start | bytes 1105928 | tf_op jit(solution)/shard_map/ppermute | solution.py:19
  6.3 1.6 %bitcast_convert_fusion = f32[2,4,720,128]{3,2,1,0:T(8,128)S(1)} fusion(bf16[128,2,4,720]{0,3,2,1:T(8,128)(2,1)} %param.3), kind=kLoop, calls=%fused_computation.88 | loop fusion | flops 737280 | bytes 4423680 | tf_op jit(solution)/shard_map/convert_element_type | solution.py:21
  9.2 1.2 %collective-permute-done.1 = bf16[2,1,720,128]{3,2,1,0:T(8,128)(2,1)} collective-permute-done((bf16[2,1,720,128]{3,2,1,0:T(8,128)(2,1)}, bf16[2,1,720,128]{3,2,1,0:T(8,128)(2,1)}, u32[]{:S(2)}, u32[]{:S(2)}) %collective-permute-start.1) | collective-permute-done | bytes 368672 | tf_op jit(solution)/shard_map/ppermute | solution.py:19
  10.4 1.3 %maximum_convert_fusion = f32[2,6,720,128]{3,2,1,0:T(8,128)S(1)} fusion(bf16[2,1,720,128]{3,2,1,0:T(8,128)(2,1)} %collective-permute-done.1, bf16[2,4,720,128]{3,2,1,0:T(8,128)(2,1)S(1)} %bitcast.80, bf16[2,1,720,128]{3,2,1,0:T(8,128)(2,1)S(1)} %collective-permute-done), kind=kLoop, calls=%fused_computation.41 | loop fusion | flops 3317760 | bytes 6635520 | tf_op jit(solution)/shard_map/convert_element_type | solution.py:20
  11.8 3.0 %fusion.4 = bf16[2,4,720,128]{3,2,1,0:T(8,128)(2,1)S(1)} fusion(f32[2,6,720,128]{3,2,1,0:T(8,128)S(1)} %maximum_convert_fusion, f32[2,4,719,128]{3,2,1,0:T(8,128)S(1)} %get-tuple-element.13, f32[2,4,1,128]{3,2,1,0:T(1,128)S(1)} %get-tuple-element.15, f32[2,4,1,128]{3,2,1,0:T(1,128)S(1)} %get-tuple-element.14, f32[2,4,719,128]{3,2,1,0:T(8,128)S(1)} %get-tuple-element.12, ...), kind=kLoop, calls=%fused_computation.21 | loop fusion | flops 10321920 | bytes 14791696 | tf_op jit(solution)/shard_map/convert_element_type | solution.py:32
  15.0 4.2 %collective-permute-start.7 = (bf16[1440,128]{1,0:T(8,128)(2,1)S(1)}, bf16[1440,128]{1,0:T(8,128)(2,1)S(1)}, u32[]{:S(2)}, u32[]{:S(2)}) collective-permute-start(bf16[1440,128]{1,0:T(8,128)(2,1)S(1)} %get-tuple-element.16), channel_id=1, source_target_pairs={{0,24},{4,28},{8,16},{12,20},{16,8},{20,12},{24,0},{28,4},{1,25},{... | collective-permute-start | bytes 1105928 | tf_op jit(solution)/shard_map/ppermute | solution.py:11
  19.8 1.7 %collective-permute-start.2 = (bf16[1440,128]{1,0:T(8,128)(2,1)S(1)}, bf16[1440,128]{1,0:T(8,128)(2,1)S(1)}, u32[]{:S(2)}, u32[]{:S(2)}) collective-permute-start(bf16[1440,128]{1,0:T(8,128)(2,1)S(1)} %get-tuple-element.20), channel_id=1, source_target_pairs={{0,4},{4,0},{8,12},{12,8},{16,20},{20,16},{24,28},{28,24},{1,5},{5... | collective-permute-start | bytes 1105928 | tf_op jit(solution)/shard_map/ppermute | solution.py:11
  21.5 3.4 %collective-permute-done.7 = bf16[1440,128]{1,0:T(8,128)(2,1)S(1)} collective-permute-done((bf16[1440,128]{1,0:T(8,128)(2,1)S(1)}, bf16[1440,128]{1,0:T(8,128)(2,1)S(1)}, u32[]{:S(2)}, u32[]{:S(2)}) %collective-permute-start.7) | collective-permute-done | bytes 368672 | tf_op jit(solution)/shard_map/ppermute | solution.py:11
  24.9 1.7 %collective-permute-start.8 = (bf16[1440,128]{1,0:T(8,128)(2,1)S(1)}, bf16[1440,128]{1,0:T(8,128)(2,1)S(1)}, u32[]{:S(2)}, u32[]{:S(2)}) collective-permute-start(bf16[1440,128]{1,0:T(8,128)(2,1)S(1)} %collective-permute-done.7), channel_id=1, source_target_pairs={{0,4},{4,0},{8,12},{12,8},{16,20},{20,16},{24,28},{28,24},{1,5},{5... | collective-permute-start | bytes 1105928 | tf_op jit(solution)/shard_map/ppermute | solution.py:11
  26.6 24.4 %collective-permute-done.5 = bf16[1440,128]{1,0:T(8,128)(2,1)S(1)} collective-permute-done((bf16[1440,128]{1,0:T(8,128)(2,1)S(1)}, bf16[1440,128]{1,0:T(8,128)(2,1)S(1)}, u32[]{:S(2)}, u32[]{:S(2)}) %collective-permute-start.5) | collective-permute-done | bytes 368672 | tf_op jit(solution)/shard_map/ppermute | solution.py:11
  51.0 1.3 %collective-permute-start.6 = (bf16[1440,128]{1,0:T(8,128)(2,1)S(1)}, bf16[1440,128]{1,0:T(8,128)(2,1)S(1)}, u32[]{:S(2)}, u32[]{:S(2)}) collective-permute-start(bf16[1440,128]{1,0:T(8,128)(2,1)S(1)} %collective-permute-done.5), channel_id=1, source_target_pairs={{0,4},{4,0},{8,12},{12,8},{16,20},{20,16},{24,28},{28,24},{1,5},{5... | collective-permute-start | bytes 1105928 | tf_op jit(solution)/shard_map/ppermute | solution.py:11
  53.1 16.8 %collective-permute-done.4 = bf16[1440,128]{1,0:T(8,128)(2,1)S(1)} collective-permute-done((bf16[1440,128]{1,0:T(8,128)(2,1)S(1)}, bf16[1440,128]{1,0:T(8,128)(2,1)S(1)}, u32[]{:S(2)}, u32[]{:S(2)}) %collective-permute-start.4) | collective-permute-done | bytes 368672 | tf_op jit(solution)/shard_map/ppermute | solution.py:11
  70.4 5.4 %collective-permute-done.9 = bf16[8,1440,128]{2,1,0:T(8,128)(2,1)} collective-permute-done((bf16[8,1440,128]{2,1,0:T(8,128)(2,1)S(1)}, bf16[8,1440,128]{2,1,0:T(8,128)(2,1)}, u32[]{:S(2)}, u32[]{:S(2)}) %collective-permute-start.9) | collective-permute-done | bytes 2949152 | tf_op jit(solution)/shard_map/ppermute | solution.py:11
  76.9 2.9 %fusion.37 = (bf16[2880,128]{1,0:T(8,128)(2,1)S(1)}, bf16[2880,128]{1,0:T(8,128)(2,1)S(1)}, bf16[2880,128]{1,0:T(8,128)(2,1)S(1)}, bf16[2880,128]{1,0:T(8,128)(2...) fusion(s32[]{:T(128)S(6)} %select_n.47, ...), kind=kLoop, calls=%fused_computation.56 | loop fusion | flops 10321920 | bytes 11059212 | tf_op jit(solution)/shard_map/jit(dynamic_index_in_dim)/squeeze | solution.py:56
  79.8 1.8 %fusion.8 = f32[512,512]{1,0:T(8,128)S(1)} fusion(bf16[2880,128]{1,0:T(8,128)(2,1)S(1)} %get-tuple-element.9, bf16[2880,128]{1,0:T(8,128)(2,1)S(1)} %get-tuple-element.8, bf16[2880,128]{1,0:T(8,128)(2,1)S(1)} %get-tuple-element.7, bf16[2880,128]{1,0:T(8,128)(2,1)S(1)} %get-tuple-element.6, bf16[2880,128]{1,0:T(8,128)(2,1)S(1)} %fusion.38, ...), kind=kOutput, calls=%fused_computation.26 | convolution fusion | flops 1533542400 | bytes 6946816 | tf_op jit(solution)/shard_map/dot_general | solution.py:58
  83.1 2.7 %collective-permute-start.16 = (f32[128,256]{1,0:T(8,128)S(1)}, f32[128,256]{1,0:T(8,128)S(1)}, u32[]{:S(2)}, u32[]{:S(2)}) collective-permute-start(f32[128,256]{1,0:T(8,128)S(1)} %bitcast.87), channel_id=1, source_target_pairs={{0,26},{1,27},{2,24},{3,25},{4,30},{5,31},{6,28},{7,29},{8,18},{9,... | collective-permute-start | bytes 393224 | tf_op jit(solution)/shard_map/ppermute | solution.py:71
  86.8 2.7 %collective-permute-start.12 = (f32[128,256]{1,0:T(8,128)S(1)}, f32[128,256]{1,0:T(8,128)S(1)}, u32[]{:S(2)}, u32[]{:S(2)}) collective-permute-start(f32[128,256]{1,0:T(8,128)S(1)} %bitcast.86), channel_id=1, source_target_pairs={{0,10},{1,11},{2,8},{3,9},{4,14},{5,15},{6,12},{7,13},{8,2},{9,3},... | collective-permute-start | bytes 393224 | tf_op jit(solution)/shard_map/ppermute | solution.py:71
  90.5 1.7 %collective-permute-done.16 = f32[128,256]{1,0:T(8,128)S(1)} collective-permute-done((f32[128,256]{1,0:T(8,128)S(1)}, f32[128,256]{1,0:T(8,128)S(1)}, u32[]{:S(2)}, u32[]{:S(2)}) %collective-permute-start.16) | collective-permute-done | bytes 131104 | tf_op jit(solution)/shard_map/ppermute | solution.py:71
  92.2 3.7 %collective-permute-start.14 = (f32[128,256]{1,0:T(8,128)S(1)}, f32[128,256]{1,0:T(8,128)S(1)}, u32[]{:S(2)}, u32[]{:S(2)}) collective-permute-start(f32[128,256]{1,0:T(8,128)S(1)} %bitcast.83), channel_id=1, source_target_pairs={{0,18},{1,19},{2,16},{3,17},{4,22},{5,23},{6,20},{7,21},{8,26},{9,... | collective-permute-start | bytes 393224 | tf_op jit(solution)/shard_map/ppermute | solution.py:71
  96.9 2.1 %collective-permute-done.11 = f32[128,256]{1,0:T(8,128)S(1)} collective-permute-done((f32[128,256]{1,0:T(8,128)S(1)}, f32[128,256]{1,0:T(8,128)S(1)}, u32[]{:S(2)}, u32[]{:S(2)}) %collective-permute-start.11) | collective-permute-done | bytes 131104 | tf_op jit(solution)/shard_map/ppermute | solution.py:71
  99.0 2.3 %collective-permute-done.12 = f32[128,256]{1,0:T(8,128)S(1)} collective-permute-done((f32[128,256]{1,0:T(8,128)S(1)}, f32[128,256]{1,0:T(8,128)S(1)}, u32[]{:S(2)}, u32[]{:S(2)}) %collective-permute-start.12) | collective-permute-done | bytes 131104 | tf_op jit(solution)/shard_map/ppermute | solution.py:71
  101.4 6.7 %collective-permute-done.14 = f32[128,256]{1,0:T(8,128)S(1)} collective-permute-done((f32[128,256]{1,0:T(8,128)S(1)}, f32[128,256]{1,0:T(8,128)S(1)}, u32[]{:S(2)}, u32[]{:S(2)}) %collective-permute-start.14) | collective-permute-done | bytes 131104 | tf_op jit(solution)/shard_map/ppermute | solution.py:71
  (45 shorter events, 9.4 us)
Async XLA Ops:
  2.0 7.2 %collective-permute-start = (bf16[2,1,720,128]{3,2,1,0:T(8,128)(2,1)}, bf16[2,1,720,128]{3,2,1,0:T(8,128)(2,1)S(1)}, u32[]{:S(2)}, u32[]{:S(2)}) collective-permute-start(bf16[2,1,720,128]{3,2,1,0:T(8,128)(2,1)} %get-tuple-element.21), channel_id=1, source_target_pairs={{0,1},{1,2},{2,3},{4,5},{5,6},{6,7},{8,9},{9,10},{10,11},{12,13},{... | collective-permute-start | bytes 1105928 | tf_op jit(solution)/shard_map/ppermute | solution.py:18
  4.4 6.0 %collective-permute-start.1 = (bf16[2,1,720,128]{3,2,1,0:T(8,128)(2,1)}, bf16[2,1,720,128]{3,2,1,0:T(8,128)(2,1)}, u32[]{:S(2)}, u32[]{:S(2)}) collective-permute-start(bf16[2,1,720,128]{3,2,1,0:T(8,128)(2,1)} %get-tuple-element.22), channel_id=1, source_target_pairs={{1,0},{2,1},{3,2},{5,4},{6,5},{7,6},{9,8},{10,9},{11,10},{13,12},{... | collective-permute-start | bytes 1105928 | tf_op jit(solution)/shard_map/ppermute | solution.py:19
  8.7 1.7 %copy-start = (bf16[128,2,4,720]{0,3,2,1:T(8,128)(2,1)S(1)}, bf16[128,2,4,720]{0,3,2,1:T(8,128)(2,1)}, u32[]{:S(2)}) copy-start(bf16[128,2,4,720]{0,3,2,1:T(8,128)(2,1)} %param.3) | copy-start | bytes 4423684
  9.2 2.6 %copy-start.1 = (f32[2,4,720]{2,1,0:T(4,128)S(1)}, f32[2,4,720]{2,1,0:T(4,128)}, u32[]{:S(2)}) copy-start(f32[2,4,720]{2,1,0:T(4,128)} %param.5) | copy-start | bytes 69124
  9.2 2.6 %copy-start.2 = (f32[2,4,720]{2,1,0:T(4,128)S(1)}, f32[2,4,720]{2,1,0:T(4,128)}, u32[]{:S(2)}) copy-start(f32[2,4,720]{2,1,0:T(4,128)} %param.4) | copy-start | bytes 69124
  15.0 9.9 %collective-permute-start.7 = (bf16[1440,128]{1,0:T(8,128)(2,1)S(1)}, bf16[1440,128]{1,0:T(8,128)(2,1)S(1)}, u32[]{:S(2)}, u32[]{:S(2)}) collective-permute-start(bf16[1440,128]{1,0:T(8,128)(2,1)S(1)} %get-tuple-element.16), channel_id=1, source_target_pairs={{0,24},{4,28},{8,16},{12,20},{16,8},{20,12},{24,0},{28,4},{1,25},{... | collective-permute-start | bytes 1105928 | tf_op jit(solution)/shard_map/ppermute | solution.py:11
  19.2 31.8 %collective-permute-start.5 = (bf16[1440,128]{1,0:T(8,128)(2,1)S(1)}, bf16[1440,128]{1,0:T(8,128)(2,1)S(1)}, u32[]{:S(2)}, u32[]{:S(2)}) collective-permute-start(bf16[1440,128]{1,0:T(8,128)(2,1)S(1)} %get-tuple-element.18), channel_id=1, source_target_pairs={{0,16},{4,20},{8,24},{12,28},{16,0},{20,4},{24,8},{28,12},{1,17},{... | collective-permute-start | bytes 1105928 | tf_op jit(solution)/shard_map/ppermute | solution.py:11
  19.2 33.1 %collective-permute-start.3 = (bf16[1440,128]{1,0:T(8,128)(2,1)S(1)}, bf16[1440,128]{1,0:T(8,128)(2,1)S(1)}, u32[]{:S(2)}, u32[]{:S(2)}) collective-permute-start(bf16[1440,128]{1,0:T(8,128)(2,1)S(1)} %get-tuple-element.19), channel_id=1, source_target_pairs={{0,8},{4,12},{8,0},{12,4},{16,24},{20,28},{24,16},{28,20},{1,9},{5... | collective-permute-start | bytes 1105928 | tf_op jit(solution)/shard_map/ppermute | solution.py:11
  19.8 33.2 %collective-permute-start.2 = (bf16[1440,128]{1,0:T(8,128)(2,1)S(1)}, bf16[1440,128]{1,0:T(8,128)(2,1)S(1)}, u32[]{:S(2)}, u32[]{:S(2)}) collective-permute-start(bf16[1440,128]{1,0:T(8,128)(2,1)S(1)} %get-tuple-element.20), channel_id=1, source_target_pairs={{0,4},{4,0},{8,12},{12,8},{16,20},{20,16},{24,28},{28,24},{1,5},{5... | collective-permute-start | bytes 1105928 | tf_op jit(solution)/shard_map/ppermute | solution.py:11
  24.9 45.3 %collective-permute-start.8 = (bf16[1440,128]{1,0:T(8,128)(2,1)S(1)}, bf16[1440,128]{1,0:T(8,128)(2,1)S(1)}, u32[]{:S(2)}, u32[]{:S(2)}) collective-permute-start(bf16[1440,128]{1,0:T(8,128)(2,1)S(1)} %collective-permute-done.7), channel_id=1, source_target_pairs={{0,4},{4,0},{8,12},{12,8},{16,20},{20,16},{24,28},{28,24},{1,5},{5... | collective-permute-start | bytes 1105928 | tf_op jit(solution)/shard_map/ppermute | solution.py:11
  51.0 19.1 %collective-permute-start.6 = (bf16[1440,128]{1,0:T(8,128)(2,1)S(1)}, bf16[1440,128]{1,0:T(8,128)(2,1)S(1)}, u32[]{:S(2)}, u32[]{:S(2)}) collective-permute-start(bf16[1440,128]{1,0:T(8,128)(2,1)S(1)} %collective-permute-done.5), channel_id=1, source_target_pairs={{0,4},{4,0},{8,12},{12,8},{16,20},{20,16},{24,28},{28,24},{1,5},{5... | collective-permute-start | bytes 1105928 | tf_op jit(solution)/shard_map/ppermute | solution.py:11
  52.3 17.7 %collective-permute-start.4 = (bf16[1440,128]{1,0:T(8,128)(2,1)S(1)}, bf16[1440,128]{1,0:T(8,128)(2,1)S(1)}, u32[]{:S(2)}, u32[]{:S(2)}) collective-permute-start(bf16[1440,128]{1,0:T(8,128)(2,1)S(1)} %collective-permute-done.3), channel_id=1, source_target_pairs={{0,4},{4,0},{8,12},{12,8},{16,20},{20,16},{24,28},{28,24},{1,5},{5... | collective-permute-start | bytes 1105928 | tf_op jit(solution)/shard_map/ppermute | solution.py:11
  70.3 5.6 %collective-permute-start.9 = (bf16[8,1440,128]{2,1,0:T(8,128)(2,1)S(1)}, bf16[8,1440,128]{2,1,0:T(8,128)(2,1)}, u32[]{:S(2)}, u32[]{:S(2)}) collective-permute-start(bf16[8,1440,128]{2,1,0:T(8,128)(2,1)S(1)} %bitcast_dynamic-update-slice_fusion), channel_id=1, source_target_pairs={{0,1},{1,0},{2,3},{3,2},{4,5},{5,4},{6,7},{7,6},{8,9},{9,8},{10,11... | collective-permute-start | bytes 8847368 | tf_op jit(solution)/shard_map/ppermute | solution.py:11
  83.1 9.2 %collective-permute-start.16 = (f32[128,256]{1,0:T(8,128)S(1)}, f32[128,256]{1,0:T(8,128)S(1)}, u32[]{:S(2)}, u32[]{:S(2)}) collective-permute-start(f32[128,256]{1,0:T(8,128)S(1)} %bitcast.87), channel_id=1, source_target_pairs={{0,26},{1,27},{2,24},{3,25},{4,30},{5,31},{6,28},{7,29},{8,18},{9,... | collective-permute-start | bytes 393224 | tf_op jit(solution)/shard_map/ppermute | solution.py:71
  85.8 10.1 %collective-permute-start.10 = (f32[128,256]{1,0:T(8,128)S(1)}, f32[128,256]{1,0:T(8,128)S(1)}, u32[]{:S(2)}, u32[]{:S(2)}) collective-permute-start(f32[128,256]{1,0:T(8,128)S(1)} %bitcast.85), channel_id=1, source_target_pairs={{0,2},{1,3},{2,0},{3,1},{4,6},{5,7},{6,4},{7,5},{8,10},{9,11},{10,... | collective-permute-start | bytes 393224 | tf_op jit(solution)/shard_map/ppermute | solution.py:71
  86.0 13.0 %collective-permute-start.11 = (f32[128,256]{1,0:T(8,128)S(1)}, f32[128,256]{1,0:T(8,128)S(1)}, u32[]{:S(2)}, u32[]{:S(2)}) collective-permute-start(f32[128,256]{1,0:T(8,128)S(1)} %bitcast.88), channel_id=1, source_target_pairs={{0,8},{1,9},{2,10},{3,11},{4,12},{5,13},{6,14},{7,15},{8,0},{9,1},... | collective-permute-start | bytes 393224 | tf_op jit(solution)/shard_map/ppermute | solution.py:71
  86.8 14.6 %collective-permute-start.12 = (f32[128,256]{1,0:T(8,128)S(1)}, f32[128,256]{1,0:T(8,128)S(1)}, u32[]{:S(2)}, u32[]{:S(2)}) collective-permute-start(f32[128,256]{1,0:T(8,128)S(1)} %bitcast.86), channel_id=1, source_target_pairs={{0,10},{1,11},{2,8},{3,9},{4,14},{5,15},{6,12},{7,13},{8,2},{9,3},... | collective-permute-start | bytes 393224 | tf_op jit(solution)/shard_map/ppermute | solution.py:71
  89.5 11.8 %collective-permute-start.13 = (f32[128,256]{1,0:T(8,128)S(1)}, f32[128,256]{1,0:T(8,128)S(1)}, u32[]{:S(2)}, u32[]{:S(2)}) collective-permute-start(f32[128,256]{1,0:T(8,128)S(1)} %bitcast.84), channel_id=1, source_target_pairs={{0,16},{1,17},{2,18},{3,19},{4,20},{5,21},{6,22},{7,23},{8,24},{9,... | collective-permute-start | bytes 393224 | tf_op jit(solution)/shard_map/ppermute | solution.py:71
  92.2 15.8 %collective-permute-start.14 = (f32[128,256]{1,0:T(8,128)S(1)}, f32[128,256]{1,0:T(8,128)S(1)}, u32[]{:S(2)}, u32[]{:S(2)}) collective-permute-start(f32[128,256]{1,0:T(8,128)S(1)} %bitcast.83), channel_id=1, source_target_pairs={{0,18},{1,19},{2,16},{3,17},{4,22},{5,23},{6,20},{7,21},{8,26},{9,... | collective-permute-start | bytes 393224 | tf_op jit(solution)/shard_map/ppermute | solution.py:71
  95.9 12.1 %collective-permute-start.15 = (f32[128,256]{1,0:T(8,128)S(1)}, f32[128,256]{1,0:T(8,128)S(1)}, u32[]{:S(2)}, u32[]{:S(2)}) collective-permute-start(f32[128,256]{1,0:T(8,128)S(1)} %bitcast.82), channel_id=1, source_target_pairs={{0,24},{1,25},{2,26},{3,27},{4,28},{5,29},{6,30},{7,31},{8,16},{9,... | collective-permute-start | bytes 393224 | tf_op jit(solution)/shard_map/ppermute | solution.py:71

commit v2 on v1

v2 whole, which is shorter than its diff:
```python
import functools
import math

import jax
import jax.numpy as jnp
import numpy as np
from jax import lax
from jax.experimental import pallas as pl
from jax.experimental.pallas import tpu as pltpu
from jax.sharding import PartitionSpec as P

EXTRA = 8
VMEM_BYTES = 48 * 2**20


def flip(cells, axis, bits):
    count = lax.axis_size(axis)
    return lax.ppermute(cells, axis, [(i, i ^ bits) for i in range(count)])


def after(value, *earlier):
    return lax.optimization_barrier((value, *earlier))[0]


def row_factors(nlat, fields, nlon):
    cosine = np.cos(np.deg2rad(45.0 + 0.5 * (np.arange(nlat) + 0.5 - nlat / 2.0)))
    total = fields * nlon * cosine.sum()
    return np.sqrt(cosine) * total ** (-0.25)


def smooth_kernel(part, layers, edges, at_ref, factor_ref, x_ref, lon_ref, lat_ref, *rest):
    rows, nlon, snaps = x_ref.shape[1:]
    if edges:
        above_ref, below_ref, *out_refs = rest
    else:
        out_refs = rest
    inner = x_ref.shape[0] * (rows - 2)
    for j in range(layers):
        n = part * layers + (at_ref[0] ^ j)
        field, row = n // (rows - 2), 1 + n % (rows - 2)
        if edges:
            m = n - inner
            field = jnp.where(m < 0, field, m // 2)
            row = jnp.where(m < 0, row, (rows - 1) * (m % 2))
        up = x_ref[field, jnp.maximum(row - 1, 0)].astype(jnp.float32)
        down = x_ref[field, jnp.minimum(row + 1, rows - 1)].astype(jnp.float32)
        if edges:
            up = jnp.where(row == 0, above_ref[field, 0].astype(jnp.float32), up)
            down = jnp.where(row == rows - 1, below_ref[field, 0].astype(jnp.float32), down)
        x = x_ref[field, row].astype(jnp.float32)
        lon = jnp.broadcast_to(lon_ref[field, pl.ds(row, 1), :], (snaps, nlon)).T
        lat = jnp.broadcast_to(lat_ref[field, pl.ds(row, 1), :], (snaps, nlon)).T
        lon_part = pltpu.roll(x, 1, 0) + pltpu.roll(x, nlon - 1, 0) - 2.0 * x
        lat_part = up + down - 2.0 * x
        smooth = x + lon * lon_part + lat * lat_part
        out_refs[j][...] = (smooth * factor_ref[row]).astype(jnp.bfloat16)


def scaled_part(part, layers, at, factors, cells, lon_coeff, lat_coeff, halo):
    nlon, snaps = cells.shape[2:]
    vmem, smem = pl.BlockSpec(memory_space=pltpu.VMEM), pl.BlockSpec(memory_space=pltpu.SMEM)
    return pl.pallas_call(
        functools.partial(smooth_kernel, part, layers, bool(halo)),
        out_shape=[jax.ShapeDtypeStruct((nlon, snaps), jnp.bfloat16)] * layers,
        in_specs=[smem, smem] + [vmem] * (3 + len(halo)),
        out_specs=[vmem] * layers,
        compiler_params=pltpu.CompilerParams(vmem_limit_bytes=VMEM_BYTES),
        name="smooth_rows",
    )(at, factors, cells, lon_coeff, lat_coeff, *halo)


def product_kernel(layers, picks, last, at_ref, *refs):
    count = 4 * layers
    pieces, refs = refs[:count], refs[count:]
    if last:
        sum_ref, own_ref, out_ref, stack, right, sems = refs
    else:
        out_ref, stack, right, sems = refs
    depth, snaps = pieces[0].shape
    copies = [
        pltpu.make_async_copy(piece, stack.at[n // 2, pl.ds((n % 2) * depth, depth)], sems.at[n])
        for n, piece in enumerate(pieces)
    ]
    for copy in copies:
        copy.start()
    for copy in copies:
        copy.wait()
    for c in range(picks):
        right[:, c * snaps : (c + 1) * snaps] = stack[at_ref[c]]
    blocks = []
    for j in range(layers):
        product = lax.dot_general(
            stack[2 * j], right[...], (((0,), (0,)), ((), ())), preferred_element_type=jnp.float32
        )
        wide = out_ref.shape[2]
        for i in range(picks * snaps // wide):
            blocks.append(product[:, i * wide : (i + 1) * wide])
    if not last:
        for n, block in enumerate(blocks):
            out_ref[n] = block
        return
    blocks = [block + sum_ref[n] for n, block in enumerate(blocks)]
    own_ref[...] = blocks[0]
    largest = functools.reduce(jnp.maximum, [jnp.abs(block) for block in blocks[1:]])
    largest = jnp.maximum(jnp.max(largest, axis=(0, 1), keepdims=True), 1e-30)
    power = jnp.ceil(jnp.log2(largest)) - 15.0
    scale = jnp.exp2(-power)
    for n, block in enumerate(blocks[1:]):
        out_ref[n, :snaps] = block * scale
        out_ref[n, snaps:] = jnp.broadcast_to(power, (EXTRA, block.shape[1]))


def product_part(layers, columns, share, at, pieces, so_far):
    depth, snaps = pieces[0].shape
    picks, wide, count = columns * share, share * snaps, layers * columns
    vmem, smem = pl.BlockSpec(memory_space=pltpu.VMEM), pl.BlockSpec(memory_space=pltpu.SMEM)
    last = so_far is not None
    if last:
        out_shape = [
            jax.ShapeDtypeStruct((snaps, wide), jnp.float32),
            jax.ShapeDtypeStruct((count - 1, snaps + EXTRA, wide), jnp.float32),
        ]
    else:
        out_shape = [jax.ShapeDtypeStruct((count, snaps, wide), jnp.float32)]
    return pl.pallas_call(
        functools.partial(product_kernel, layers, picks, last),
        out_shape=out_shape,
        in_specs=[smem] + [pl.BlockSpec(memory_space=pl.ANY)] * len(pieces) + [vmem] * last,
        out_specs=[vmem] * len(out_shape),
        scratch_shapes=[
            pltpu.VMEM((2 * layers, 2 * depth, snaps), jnp.bfloat16),
            pltpu.VMEM((2 * depth, picks * snaps), jnp.bfloat16),
            pltpu.SemaphoreType.DMA((len(pieces),)),
        ],
        compiler_params=pltpu.CompilerParams(vmem_limit_bytes=VMEM_BYTES),
        name="block_products",
    )(at, *pieces, *([so_far] if last else []))


def shards(snapshots, lon_coeff, lat_coeff):
    snaps, fields, rows, nlon = snapshots.shape
    groups, bands = lax.axis_size("snap"), lax.axis_size("space")
    layers, columns, share = groups // 2, bands // 2, groups // bands
    me, band = lax.axis_index("snap"), lax.axis_index("space")
    layer, column, core = me // 2, band // 2, band % 2
    parts = fields * rows // layers
    inner_parts = fields * (rows - 2) // layers

    table = jnp.asarray(row_factors(bands * rows, fields, nlon), jnp.float32)
    factors = lax.dynamic_slice_in_dim(table, band * rows, rows)
    cells = jnp.transpose(snapshots, (1, 2, 3, 0))
    at = layer[None]
    scaled = [
        scaled_part(t, layers, at, factors, cells, lon_coeff, lat_coeff, ())
        for t in range(inner_parts)
    ]
    first = scaled[-1][0] if scaled else cells
    tail, head = after((cells[:, rows - 1 :], cells[:, :1]), first)
    ends = bands - 1
    halo = (
        lax.ppermute(tail, "space", [(i, i + 1) for i in range(ends)]),
        lax.ppermute(head, "space", [(i + 1, i) for i in range(ends)]),
    )
    scaled += [
        scaled_part(t, layers, at, factors, cells, lon_coeff, lat_coeff, halo)
        for t in range(inner_parts, parts)
    ]

    picked = [
        (((column ^ i) * 2 + core) * share + g) ^ me for i in range(columns) for g in range(share)
    ]
    picked = jnp.stack(picked).astype(jnp.int32)
    before, product = {}, None
    for t in range(parts):
        pieces = []
        for j in range(layers):
            held = scaled[t][j]
            if j:
                held = flip(after(held, before[j]) if j in before else held, "snap", 2 * j)
                before[j] = held
            other = flip(held, "snap", 1)
            pieces += [held, flip(held, "space", 1), other, flip(other, "space", 1)]
        if t < parts - 1 and product is None:
            (product,) = product_part(layers, columns, share, picked, pieces, None)
    if product is None:
        product = jnp.zeros((layers * columns, snaps, share * snaps), jnp.float32)
    own, blocks = product_part(layers, columns, share, picked, pieces, product)

    blocks = blocks.astype(jnp.float16)
    total = own
    for j in range(layers):
        for i in range(columns):
            if i or j:
                pairs = [
                    (s * bands + b, (s ^ (2 * j)) * bands + (b ^ (2 * i)))
                    for s in range(groups)
                    for b in range(bands)
                ]
                block = lax.ppermute(blocks[j * columns + i - 1], ("snap", "space"), pairs)
                block = block.astype(jnp.float32)
                total += block[:snaps] * jnp.exp2(block[snaps : snaps + 1])
    return total


def solution(mesh):
    return jax.shard_map(
        shards,
        mesh=mesh,
        in_specs=(P("snap", None, "space", None), P(None, "space", None), P(None, "space", None)),
        out_specs=P("snap", "space"),
        check_vma=False,
    )
```

time: 109 us -> 105 us (0.963)
  waiting for transfers between devices: 64 us -> 45.6 us
  Pallas kernels: 0 us -> 13.9 us
  starting transfers between devices: 26.1 us -> 38 us
  other arithmetic: 11.3 us -> 1.05 us
  matrix products: 1.81 us -> 0 us
  local copies, waits for them, and re-layouts: 4.53 us -> 5.78 us
    pallas_call x0 -> x4, Pallas kernels: none -> 13.9 us  [the longest x2 10.6 us: product_part(): pl.pallas_call(functools.partial(product_kernel, layers, picks, last), ou...]
    ppermute x8 -> x30, starting transfers between devices: 10.3 us -> 22.7 us  [flip(): return lax.ppermute(cells, axis, [(i, i ^ bits) for i in range(count)])]
    ppermute x8 -> x30, waiting for transfers between devices: 50.1 us -> 39.4 us  [flip(): return lax.ppermute(cells, axis, [(i, i ^ bits) for i in range(count)])]
    ppermute x9, waiting for transfers between devices: 13.9 us -> 6.17 us  [the longest x7 6.17 us: shards(): block = lax.ppermute(blocks[j * columns + i - 1], ('snap', 'space'), pairs)]
    convert_element_type x3 -> x8, other arithmetic: 5.93 us -> 0.17 us  [the longest x1 0.09 us: shards(): blocks = blocks.astype(jnp.float16)]
    unnamed x19 -> x18, local copies, waits for them, and re-layouts: 0.39 us -> 4.91 us
    squeeze x2 -> x0, other arithmetic: 3.92 us -> none  [shards(): right.append(lax.dynamic_index_in_dim(stack, group ^ me, 0, keepdims=False))]
    slice x4 -> x1, local copies, waits for them, and re-layouts: 3.23 us -> 0.05 us  [shards(): tail, head = after((cells[:, rows - 1:], cells[:, :1]), first)]
  transfers between devices with their start and end apart: 17 -> 39, of which waited for: 9 -> 11; matrix products, arithmetic and copies ran while one was open for 3% -> 0% of each run, Pallas kernels for 0% -> 7%
where the time goes in v2:
time: 105 us
  waiting for transfers between devices  45.6 us (43%)
  starting transfers between devices  38 us (36%)
  Pallas kernels  13.9 us (13%)
  local copies, waits for them, and re-layouts  5.78 us (6%)
  other arithmetic  1.05 us (1%)
    ppermute x30, waiting for transfers between devices, flip(): return lax.ppermute(cells, axis, [(i, i ^ bits) for i in range(count)])  39.4 us
    ppermute x30, starting transfers between devices, flip(): return lax.ppermute(cells, axis, [(i, i ^ bits) for i in range(count)])  22.7 us
    ppermute x7, starting transfers between devices, shards(): block = lax.ppermute(blocks[j * columns + i - 1], ('snap', 'space'), pairs)  11.6 us
    pallas_call x2, Pallas kernels, product_part(): pl.pallas_call(functools.partial(product_kernel, layers, picks, last), ou...  10.6 us
    ppermute x7, waiting for transfers between devices, shards(): block = lax.ppermute(blocks[j * columns + i - 1], ('snap', 'space'), pairs)  6.17 us
    unnamed x18, local copies, waits for them, and re-layouts  4.91 us
    pallas_call x2, Pallas kernels, scaled_part(): pl.pallas_call(functools.partial(smooth_kernel, part, layers, bool(halo))...  3.26 us
    ppermute x1, starting transfers between devices, shards(): lax.ppermute(tail, 'space', [(i, i + 1) for i in range(ends)])  2.42 us
  transfers between devices with their start and end apart: 39, of which 11 were waited for; matrix products, arithmetic and copies ran while one was open for 0% of the time, Pallas kernels for 7%

profile of v2, /device:TPU:0, one launch (start us, length us, event | category | flops | bytes accessed | tf_op | source)
XLA Modules:
  0.0 104.6 jit_solution(9116287940561733036)
XLA Ops:
  3.6 1.5 %smooth_rows.2 = (bf16[720,128]{1,0:T(8,128)(2,1)S(1)}, bf16[720,128]{1,0:T(8,128)(2,1)S(1)}, bf16[720,128]{1,0:T(8,128)(2,1)S(1)}, bf16[720,128]{1,0:T(8,128)(2,1)S(1)}) custom-call(s32[1]{0:T(128)} %bitcast.4.at_ref, f32[4]{0:T(128)S(1)} %dynamic_slice.3.factor_ref, bf16[2,4,720,128]{3,2,1,0:T(8,128)(2,1)S(1)} %bitcast.27, f32[2,4,720]{2,1,0:T(4,128)S(1)} %copy-done.7, ...), custom_call_target="tpu_custom_call" | custom-call | tf_op jit(solution)/shard_map/smooth_rows/pallas_call | solution.py:62
  5.1 3.0 %collective-permute-start.21 = (bf16[720,128]{1,0:T(8,128)(2,1)S(1)}, bf16[720,128]{1,0:T(8,128)(2,1)S(1)}, u32[]{:S(2)}, u32[]{:S(2)}) collective-permute-start(bf16[720,128]{1,0:T(8,128)(2,1)S(1)} %get-tuple-element.20.refs_0_), channel_id=1, source_target_pairs={{0,4},{4,0},{8,12},{12,8},{16,20},{20,16},{24,28},{28,24},{1,5},{5... | collective-permute-start | bytes 552968 | tf_op jit(solution)/shard_map/ppermute | solution.py:18
  8.2 1.6 %collective-permute-start.5 = (bf16[720,128]{1,0:T(8,128)(2,1)S(1)}, bf16[720,128]{1,0:T(8,128)(2,1)S(1)}, u32[]{:S(2)}, u32[]{:S(2)}) collective-permute-start(bf16[720,128]{1,0:T(8,128)(2,1)S(1)} %get-tuple-element.25), channel_id=1, source_target_pairs={{0,8},{4,12},{8,0},{12,4},{16,24},{20,28},{24,16},{28,20},{1,9},{5... | collective-permute-start | bytes 552968 | tf_op jit(solution)/shard_map/ppermute | solution.py:18
  9.7 2.6 %collective-permute-start.10 = (bf16[720,128]{1,0:T(8,128)(2,1)S(1)}, bf16[720,128]{1,0:T(8,128)(2,1)S(1)}, u32[]{:S(2)}, u32[]{:S(2)}) collective-permute-start(bf16[720,128]{1,0:T(8,128)(2,1)S(1)} %get-tuple-element.28), channel_id=1, source_target_pairs={{0,16},{4,20},{8,24},{12,28},{16,0},{20,4},{24,8},{28,12},{1,17},{... | collective-permute-start | bytes 552968 | tf_op jit(solution)/shard_map/ppermute | solution.py:18
  12.6 6.1 %collective-permute-done.5.refs_4_ = bf16[720,128]{1,0:T(8,128)(2,1)S(1)} collective-permute-done((bf16[720,128]{1,0:T(8,128)(2,1)S(1)}, bf16[720,128]{1,0:T(8,128)(2,1)S(1)}, u32[]{:S(2)}, u32[]{:S(2)}) %collective-permute-start.5) | collective-permute-done | bytes 184352 | tf_op jit(solution)/shard_map/ppermute | solution.py:18
  19.1 7.0 %collective-permute-done.10.refs_8_ = bf16[720,128]{1,0:T(8,128)(2,1)S(1)} collective-permute-done((bf16[720,128]{1,0:T(8,128)(2,1)S(1)}, bf16[720,128]{1,0:T(8,128)(2,1)S(1)}, u32[]{:S(2)}, u32[]{:S(2)}) %collective-permute-start.10) | collective-permute-done | bytes 184352 | tf_op jit(solution)/shard_map/ppermute | solution.py:18
  26.1 2.4 %collective-permute-start = (bf16[2,1,720,128]{3,2,1,0:T(8,128)(2,1)S(1)}, bf16[2,1,720,128]{3,2,1,0:T(8,128)(2,1)S(1)}, u32[]{:S(2)}, u32[]{:S(2)}) collective-permute-start(bf16[2,1,720,128]{3,2,1,0:T(8,128)(2,1)S(1)} %get-tuple-element.21), channel_id=1, source_target_pairs={{0,1},{1,2},{2,3},{4,5},{5,6},{6,7},{8,9},{9,10},{10,11},{12,13},{... | collective-permute-start | bytes 1105928 | tf_op jit(solution)/shard_map/ppermute | solution.py:161
  31.8 1.5 %collective-permute-start.30 = (bf16[720,128]{1,0:T(8,128)(2,1)S(1)}, bf16[720,128]{1,0:T(8,128)(2,1)S(1)}, u32[]{:S(2)}, u32[]{:S(2)}) collective-permute-start(bf16[720,128]{1,0:T(8,128)(2,1)S(1)} %collective-permute-done.15.refs_12_), channel_id=1, source_target_pairs={{0,4},{4,0},{8,12},{12,8},{16,20},{20,16},{24,28},{28,24},{1,5},{5... | collective-permute-start | bytes 552968 | tf_op jit(solution)/shard_map/ppermute | solution.py:18
  33.3 3.3 %collective-permute-done.27.refs_10_ = bf16[720,128]{1,0:T(8,128)(2,1)S(1)} collective-permute-done((bf16[720,128]{1,0:T(8,128)(2,1)S(1)}, bf16[720,128]{1,0:T(8,128)(2,1)S(1)}, u32[]{:S(2)}, u32[]{:S(2)}) %collective-permute-start.27) | collective-permute-done | bytes 184352 | tf_op jit(solution)/shard_map/ppermute | solution.py:18
  38.2 2.4 %collective-permute-done.30.refs_14_ = bf16[720,128]{1,0:T(8,128)(2,1)S(1)} collective-permute-done((bf16[720,128]{1,0:T(8,128)(2,1)S(1)}, bf16[720,128]{1,0:T(8,128)(2,1)S(1)}, u32[]{:S(2)}, u32[]{:S(2)}) %collective-permute-start.30) | collective-permute-done | bytes 184352 | tf_op jit(solution)/shard_map/ppermute | solution.py:18
  41.7 1.7 %smooth_rows.3 = (bf16[720,128]{1,0:T(8,128)(2,1)S(1)}, bf16[720,128]{1,0:T(8,128)(2,1)S(1)}, bf16[720,128]{1,0:T(8,128)(2,1)S(1)}, bf16[720,128]{1,0:T(8,128)(2,1)S(1)}) custom-call(s32[1]{0:T(128)} %bitcast.4.at_ref, f32[4]{0:T(128)S(1)} %dynamic_slice.3.factor_ref, bf16[2,4,720,128]{3,2,1,0:T(8,128)(2,1)S(1)} %bitcast.29, f32[2,4,720]{2,1,0:T(4,128)S(1)} %copy-done.7, ...), custom_call_target="tpu_custom_call" | custom-call | tf_op jit(solution)/shard_map/smooth_rows/pallas_call | solution.py:62
  43.4 2.5 %collective-permute-start.16 = (bf16[720,128]{1,0:T(8,128)(2,1)S(1)}, bf16[720,128]{1,0:T(8,128)(2,1)S(1)}, u32[]{:S(2)}, u32[]{:S(2)}) collective-permute-start(bf16[720,128]{1,0:T(8,128)(2,1)S(1)} %get-tuple-element.32), channel_id=1, source_target_pairs={{0,24},{4,28},{8,16},{12,20},{16,8},{20,12},{24,0},{28,4},{1,25},{... | collective-permute-start | bytes 552968 | tf_op jit(solution)/shard_map/ppermute | solution.py:18
  46.0 1.7 %collective-permute-start.11 = (bf16[720,128]{1,0:T(8,128)(2,1)S(1)}, bf16[720,128]{1,0:T(8,128)(2,1)S(1)}, u32[]{:S(2)}, u32[]{:S(2)}) collective-permute-start(bf16[720,128]{1,0:T(8,128)(2,1)S(1)} %get-tuple-element.29), channel_id=1, source_target_pairs={{0,16},{4,20},{8,24},{12,28},{16,0},{20,4},{24,8},{28,12},{1,17},{... | collective-permute-start | bytes 552968 | tf_op jit(solution)/shard_map/ppermute | solution.py:18
  48.6 4.3 %collective-permute-done.16.refs_12_ = bf16[720,128]{1,0:T(8,128)(2,1)S(1)} collective-permute-done((bf16[720,128]{1,0:T(8,128)(2,1)S(1)}, bf16[720,128]{1,0:T(8,128)(2,1)S(1)}, u32[]{:S(2)}, u32[]{:S(2)}) %collective-permute-start.16) | collective-permute-done | bytes 184352 | tf_op jit(solution)/shard_map/ppermute | solution.py:18
  53.3 10.5 %collective-permute-done.11.refs_8_ = bf16[720,128]{1,0:T(8,128)(2,1)S(1)} collective-permute-done((bf16[720,128]{1,0:T(8,128)(2,1)S(1)}, bf16[720,128]{1,0:T(8,128)(2,1)S(1)}, u32[]{:S(2)}, u32[]{:S(2)}) %collective-permute-start.11) | collective-permute-done | bytes 184352 | tf_op jit(solution)/shard_map/ppermute | solution.py:18
  65.2 1.5 %collective-permute-start.8 = (bf16[720,128]{1,0:T(8,128)(2,1)}, bf16[720,128]{1,0:T(8,128)(2,1)}, u32[]{:S(2)}, u32[]{:S(2)}) collective-permute-start(bf16[720,128]{1,0:T(8,128)(2,1)} %collective-permute-done.6.refs_4_), channel_id=1, source_target_pairs={{0,4},{4,0},{8,12},{12,8},{16,20},{20,16},{24,28},{28,24},{1,5},{5... | collective-permute-start | bytes 552968 | tf_op jit(solution)/shard_map/ppermute | solution.py:18
  67.9 3.4 %collective-permute-done.13.refs_10_ = bf16[720,128]{1,0:T(8,128)(2,1)} collective-permute-done((bf16[720,128]{1,0:T(8,128)(2,1)S(1)}, bf16[720,128]{1,0:T(8,128)(2,1)}, u32[]{:S(2)}, u32[]{:S(2)}) %collective-permute-start.13) | collective-permute-done | bytes 184352 | tf_op jit(solution)/shard_map/ppermute | solution.py:18
  72.5 2.4 %collective-permute-done.8.refs_6_ = bf16[720,128]{1,0:T(8,128)(2,1)} collective-permute-done((bf16[720,128]{1,0:T(8,128)(2,1)}, bf16[720,128]{1,0:T(8,128)(2,1)}, u32[]{:S(2)}, u32[]{:S(2)}) %collective-permute-start.8) | collective-permute-done | bytes 184352 | tf_op jit(solution)/shard_map/ppermute | solution.py:18
  75.0 5.8 %block_products.2.refs_16_ = f32[8,128,256]{2,1,0:T(8,128)S(1)} custom-call(s32[4]{0:T(128)S(1)} %pad_add_fusion.at_ref, bf16[720,128]{1,0:T(8,128)(2,1)S(1)} %get-tuple-element.20.refs_0_, bf16[720,128]{1,0:T(8,128)(2,1)S(1)} %collective-permute-done.20.refs_1_, bf16[720,128]{1,0:T(8,128)(2,1)S(1)} %collective-permute-done.21.refs_2_, ...), custom_call_target="tpu_custom_call" | custom-call | tf_op jit(solution)/shard_map/block_products/pallas_call | solution.py:125
  80.9 4.8 %block_products.3 = (f32[128,256]{1,0:T(8,128)S(1)}, f32[7,136,256]{2,1,0:T(8,128)S(1)}) custom-call(s32[4]{0:T(128)S(1)} %pad_add_fusion.at_ref, bf16[720,128]{1,0:T(8,128)(2,1)S(1)} %get-tuple-element.23.refs_0_, bf16[720,128]{1,0:T(8,128)(2,1)S(1)} %copy-done.2, bf16[720,128]{1,0:T(8,128)(2,1)} %collective-permute-done.3.refs_2_, ...), custom_call_target="tpu_custom_call" | custom-call | tf_op jit(solution)/shard_map/block_products/pallas_call | solution.py:125
  85.9 2.3 %collective-permute-start.32 = (f16[136,256]{1,0:T(8,128)(2,1)S(1)}, f16[136,256]{1,0:T(8,128)(2,1)S(1)}, u32[]{:S(2)}, u32[]{:S(2)}) collective-permute-start(f16[136,256]{1,0:T(8,128)(2,1)S(1)} %get-tuple-element.37), channel_id=1, source_target_pairs={{0,2},{1,3},{2,0},{3,1},{4,6},{5,7},{6,4},{7,5},{8,10},{9,11},{10,... | collective-permute-start | bytes 208904 | tf_op jit(solution)/shard_map/ppermute | solution.py:199
  88.2 2.0 %collective-permute-start.38 = (f16[136,256]{1,0:T(8,128)(2,1)S(1)}, f16[136,256]{1,0:T(8,128)(2,1)S(1)}, u32[]{:S(2)}, u32[]{:S(2)}) collective-permute-start(f16[136,256]{1,0:T(8,128)(2,1)S(1)} %get-tuple-element.38), channel_id=1, source_target_pairs={{0,26},{1,27},{2,24},{3,25},{4,30},{5,31},{6,28},{7,29},{8,18},{9,... | collective-permute-start | bytes 208904 | tf_op jit(solution)/shard_map/ppermute | solution.py:199
  92.2 3.6 %collective-permute-start.35 = (f16[136,256]{1,0:T(8,128)(2,1)S(1)}, f16[136,256]{1,0:T(8,128)(2,1)S(1)}, u32[]{:S(2)}, u32[]{:S(2)}) collective-permute-start(f16[136,256]{1,0:T(8,128)(2,1)S(1)} %get-tuple-element.41), channel_id=1, source_target_pairs={{0,16},{1,17},{2,18},{3,19},{4,20},{5,21},{6,22},{7,23},{8,24},{9,... | collective-permute-start | bytes 208904 | tf_op jit(solution)/shard_map/ppermute | solution.py:199
  97.6 4.7 %collective-permute-done.36 = f16[136,256]{1,0:T(8,128)(2,1)S(1)} collective-permute-done((f16[136,256]{1,0:T(8,128)(2,1)S(1)}, f16[136,256]{1,0:T(8,128)(2,1)S(1)}, u32[]{:S(2)}, u32[]{:S(2)}) %collective-permute-start.36) | collective-permute-done | bytes 69664 | tf_op jit(solution)/shard_map/ppermute | solution.py:199
  (96 shorter events, 21.6 us)
Async XLA Ops:
  5.1 23.4 %collective-permute-start.21 = (bf16[720,128]{1,0:T(8,128)(2,1)S(1)}, bf16[720,128]{1,0:T(8,128)(2,1)S(1)}, u32[]{:S(2)}, u32[]{:S(2)}) collective-permute-start(bf16[720,128]{1,0:T(8,128)(2,1)S(1)} %get-tuple-element.20.refs_0_), channel_id=1, source_target_pairs={{0,4},{4,0},{8,12},{12,8},{16,20},{20,16},{24,28},{28,24},{1,5},{5... | collective-permute-start | bytes 552968 | tf_op jit(solution)/shard_map/ppermute | solution.py:18
  8.1 21.7 %collective-permute-start.20 = (bf16[720,128]{1,0:T(8,128)(2,1)S(1)}, bf16[720,128]{1,0:T(8,128)(2,1)S(1)}, u32[]{:S(2)}, u32[]{:S(2)}) collective-permute-start(bf16[720,128]{1,0:T(8,128)(2,1)S(1)} %get-tuple-element.20.refs_0_), channel_id=1, source_target_pairs={{0,1},{1,0},{2,3},{3,2},{4,5},{5,4},{6,7},{7,6},{8,9},{9,8},{10,11... | collective-permute-start | bytes 552968 | tf_op jit(solution)/shard_map/ppermute | solution.py:18
  8.2 10.6 %collective-permute-start.5 = (bf16[720,128]{1,0:T(8,128)(2,1)S(1)}, bf16[720,128]{1,0:T(8,128)(2,1)S(1)}, u32[]{:S(2)}, u32[]{:S(2)}) collective-permute-start(bf16[720,128]{1,0:T(8,128)(2,1)S(1)} %get-tuple-element.25), channel_id=1, source_target_pairs={{0,8},{4,12},{8,0},{12,4},{16,24},{20,28},{24,16},{28,20},{1,9},{5... | collective-permute-start | bytes 552968 | tf_op jit(solution)/shard_map/ppermute | solution.py:18
  9.7 16.3 %collective-permute-start.10 = (bf16[720,128]{1,0:T(8,128)(2,1)S(1)}, bf16[720,128]{1,0:T(8,128)(2,1)S(1)}, u32[]{:S(2)}, u32[]{:S(2)}) collective-permute-start(bf16[720,128]{1,0:T(8,128)(2,1)S(1)} %get-tuple-element.28), channel_id=1, source_target_pairs={{0,16},{4,20},{8,24},{12,28},{16,0},{20,4},{24,8},{28,12},{1,17},{... | collective-permute-start | bytes 552968 | tf_op jit(solution)/shard_map/ppermute | solution.py:18
  12.3 13.7 %collective-permute-start.15 = (bf16[720,128]{1,0:T(8,128)(2,1)S(1)}, bf16[720,128]{1,0:T(8,128)(2,1)S(1)}, u32[]{:S(2)}, u32[]{:S(2)}) collective-permute-start(bf16[720,128]{1,0:T(8,128)(2,1)S(1)} %get-tuple-element.31), channel_id=1, source_target_pairs={{0,24},{4,28},{8,16},{12,20},{16,8},{20,12},{24,0},{28,4},{1,25},{... | collective-permute-start | bytes 552968 | tf_op jit(solution)/shard_map/ppermute | solution.py:18
  18.7 11.7 %collective-permute-start.24 = (bf16[720,128]{1,0:T(8,128)(2,1)S(1)}, bf16[720,128]{1,0:T(8,128)(2,1)S(1)}, u32[]{:S(2)}, u32[]{:S(2)}) collective-permute-start(bf16[720,128]{1,0:T(8,128)(2,1)S(1)} %collective-permute-done.5.refs_4_), channel_id=1, source_target_pairs={{0,4},{4,0},{8,12},{12,8},{16,20},{20,16},{24,28},{28,24},{1,5},{5... | collective-permute-start | bytes 552968 | tf_op jit(solution)/shard_map/ppermute | solution.py:18
  26.1 15.1 %collective-permute-start = (bf16[2,1,720,128]{3,2,1,0:T(8,128)(2,1)S(1)}, bf16[2,1,720,128]{3,2,1,0:T(8,128)(2,1)S(1)}, u32[]{:S(2)}, u32[]{:S(2)}) collective-permute-start(bf16[2,1,720,128]{3,2,1,0:T(8,128)(2,1)S(1)} %get-tuple-element.21), channel_id=1, source_target_pairs={{0,1},{1,2},{2,3},{4,5},{5,6},{6,7},{8,9},{9,10},{10,11},{12,13},{... | collective-permute-start | bytes 1105928 | tf_op jit(solution)/shard_map/ppermute | solution.py:161
  28.5 12.7 %collective-permute-start.1 = (bf16[2,1,720,128]{3,2,1,0:T(8,128)(2,1)S(1)}, bf16[2,1,720,128]{3,2,1,0:T(8,128)(2,1)S(1)}, u32[]{:S(2)}, u32[]{:S(2)}) collective-permute-start(bf16[2,1,720,128]{3,2,1,0:T(8,128)(2,1)S(1)} %get-tuple-element.22), channel_id=1, source_target_pairs={{1,0},{2,1},{3,2},{5,4},{6,5},{7,6},{9,8},{10,9},{11,10},{13,12},{... | collective-permute-start | bytes 1105928 | tf_op jit(solution)/shard_map/ppermute | solution.py:162
  31.8 8.8 %collective-permute-start.30 = (bf16[720,128]{1,0:T(8,128)(2,1)S(1)}, bf16[720,128]{1,0:T(8,128)(2,1)S(1)}, u32[]{:S(2)}, u32[]{:S(2)}) collective-permute-start(bf16[720,128]{1,0:T(8,128)(2,1)S(1)} %collective-permute-done.15.refs_12_), channel_id=1, source_target_pairs={{0,4},{4,0},{8,12},{12,8},{16,20},{20,16},{24,28},{28,24},{1,5},{5... | collective-permute-start | bytes 552968 | tf_op jit(solution)/shard_map/ppermute | solution.py:18
  43.4 9.5 %collective-permute-start.16 = (bf16[720,128]{1,0:T(8,128)(2,1)S(1)}, bf16[720,128]{1,0:T(8,128)(2,1)S(1)}, u32[]{:S(2)}, u32[]{:S(2)}) collective-permute-start(bf16[720,128]{1,0:T(8,128)(2,1)S(1)} %get-tuple-element.32), channel_id=1, source_target_pairs={{0,24},{4,28},{8,16},{12,20},{16,8},{20,12},{24,0},{28,4},{1,25},{... | collective-permute-start | bytes 552968 | tf_op jit(solution)/shard_map/ppermute | solution.py:18
  46.0 17.8 %collective-permute-start.11 = (bf16[720,128]{1,0:T(8,128)(2,1)S(1)}, bf16[720,128]{1,0:T(8,128)(2,1)S(1)}, u32[]{:S(2)}, u32[]{:S(2)}) collective-permute-start(bf16[720,128]{1,0:T(8,128)(2,1)S(1)} %get-tuple-element.29), channel_id=1, source_target_pairs={{0,16},{4,20},{8,24},{12,28},{16,0},{20,4},{24,8},{28,12},{1,17},{... | collective-permute-start | bytes 552968 | tf_op jit(solution)/shard_map/ppermute | solution.py:18
  47.7 16.1 %collective-permute-start.6 = (bf16[720,128]{1,0:T(8,128)(2,1)S(1)}, bf16[720,128]{1,0:T(8,128)(2,1)}, u32[]{:S(2)}, u32[]{:S(2)}) collective-permute-start(bf16[720,128]{1,0:T(8,128)(2,1)S(1)} %get-tuple-element.26), channel_id=1, source_target_pairs={{0,8},{4,12},{8,0},{12,4},{16,24},{20,28},{24,16},{28,20},{1,9},{5... | collective-permute-start | bytes 552968 | tf_op jit(solution)/shard_map/ppermute | solution.py:18
  47.9 16.4 %collective-permute-start.3 = (bf16[720,128]{1,0:T(8,128)(2,1)S(1)}, bf16[720,128]{1,0:T(8,128)(2,1)}, u32[]{:S(2)}, u32[]{:S(2)}) collective-permute-start(bf16[720,128]{1,0:T(8,128)(2,1)S(1)} %get-tuple-element.23.refs_0_), channel_id=1, source_target_pairs={{0,4},{4,0},{8,12},{12,8},{16,20},{20,16},{24,28},{28,24},{1,5},{5... | collective-permute-start | bytes 552968 | tf_op jit(solution)/shard_map/ppermute | solution.py:18
  48.6 15.9 %collective-permute-start.2 = (bf16[720,128]{1,0:T(8,128)(2,1)S(1)}, bf16[720,128]{1,0:T(8,128)(2,1)S(1)}, u32[]{:S(2)}, u32[]{:S(2)}) collective-permute-start(bf16[720,128]{1,0:T(8,128)(2,1)S(1)} %get-tuple-element.23.refs_0_), channel_id=1, source_target_pairs={{0,1},{1,0},{2,3},{3,2},{4,5},{5,4},{6,7},{7,6},{8,9},{9,8},{10,11... | collective-permute-start | bytes 552968 | tf_op jit(solution)/shard_map/ppermute | solution.py:18
  52.9 13.8 %collective-permute-start.18 = (bf16[720,128]{1,0:T(8,128)(2,1)S(1)}, bf16[720,128]{1,0:T(8,128)(2,1)}, u32[]{:S(2)}, u32[]{:S(2)}) collective-permute-start(bf16[720,128]{1,0:T(8,128)(2,1)S(1)} %collective-permute-done.16.refs_12_), channel_id=1, source_target_pairs={{0,4},{4,0},{8,12},{12,8},{16,20},{20,16},{24,28},{28,24},{1,5},{5... | collective-permute-start | bytes 552968 | tf_op jit(solution)/shard_map/ppermute | solution.py:18
  65.2 9.7 %collective-permute-start.8 = (bf16[720,128]{1,0:T(8,128)(2,1)}, bf16[720,128]{1,0:T(8,128)(2,1)}, u32[]{:S(2)}, u32[]{:S(2)}) collective-permute-start(bf16[720,128]{1,0:T(8,128)(2,1)} %collective-permute-done.6.refs_4_), channel_id=1, source_target_pairs={{0,4},{4,0},{8,12},{12,8},{16,20},{20,16},{24,28},{28,24},{1,5},{5... | collective-permute-start | bytes 552968 | tf_op jit(solution)/shard_map/ppermute | solution.py:18
  66.7 14.1 %collective-permute-start.7 = (bf16[720,128]{1,0:T(8,128)(2,1)}, bf16[720,128]{1,0:T(8,128)(2,1)}, u32[]{:S(2)}, u32[]{:S(2)}) collective-permute-start(bf16[720,128]{1,0:T(8,128)(2,1)} %collective-permute-done.6.refs_4_), channel_id=1, source_target_pairs={{0,1},{1,0},{2,3},{3,2},{4,5},{5,4},{6,7},{7,6},{8,9},{9,8},{10,11... | collective-permute-start | bytes 552968 | tf_op jit(solution)/shard_map/ppermute | solution.py:18
  67.4 13.4 %collective-permute-start.4 = (bf16[720,128]{1,0:T(8,128)(2,1)}, bf16[720,128]{1,0:T(8,128)(2,1)}, u32[]{:S(2)}, u32[]{:S(2)}) collective-permute-start(bf16[720,128]{1,0:T(8,128)(2,1)} %collective-permute-done.3.refs_2_), channel_id=1, source_target_pairs={{0,1},{1,0},{2,3},{3,2},{4,5},{5,4},{6,7},{7,6},{8,9},{9,8},{10,11... | collective-permute-start | bytes 552968 | tf_op jit(solution)/shard_map/ppermute | solution.py:18
  71.3 9.5 %collective-permute-start.19 = (bf16[720,128]{1,0:T(8,128)(2,1)}, bf16[720,128]{1,0:T(8,128)(2,1)}, u32[]{:S(2)}, u32[]{:S(2)}) collective-permute-start(bf16[720,128]{1,0:T(8,128)(2,1)} %collective-permute-done.18.refs_14_), channel_id=1, source_target_pairs={{0,1},{1,0},{2,3},{3,2},{4,5},{5,4},{6,7},{7,6},{8,9},{9,8},{10,11... | collective-permute-start | bytes 552968 | tf_op jit(solution)/shard_map/ppermute | solution.py:18
  72.0 8.8 %collective-permute-start.14 = (bf16[720,128]{1,0:T(8,128)(2,1)}, bf16[720,128]{1,0:T(8,128)(2,1)}, u32[]{:S(2)}, u32[]{:S(2)}) collective-permute-start(bf16[720,128]{1,0:T(8,128)(2,1)} %collective-permute-done.13.refs_10_), channel_id=1, source_target_pairs={{0,1},{1,0},{2,3},{3,2},{4,5},{5,4},{6,7},{7,6},{8,9},{9,8},{10,11... | collective-permute-start | bytes 552968 | tf_op jit(solution)/shard_map/ppermute | solution.py:18
  85.9 10.0 %collective-permute-start.32 = (f16[136,256]{1,0:T(8,128)(2,1)S(1)}, f16[136,256]{1,0:T(8,128)(2,1)S(1)}, u32[]{:S(2)}, u32[]{:S(2)}) collective-permute-start(f16[136,256]{1,0:T(8,128)(2,1)S(1)} %get-tuple-element.37), channel_id=1, source_target_pairs={{0,2},{1,3},{2,0},{3,1},{4,6},{5,7},{6,4},{7,5},{8,10},{9,11},{10,... | collective-permute-start | bytes 208904 | tf_op jit(solution)/shard_map/ppermute | solution.py:199
  91.6 10.7 %collective-permute-start.36 = (f16[136,256]{1,0:T(8,128)(2,1)S(1)}, f16[136,256]{1,0:T(8,128)(2,1)S(1)}, u32[]{:S(2)}, u32[]{:S(2)}) collective-permute-start(f16[136,256]{1,0:T(8,128)(2,1)S(1)} %get-tuple-element.40), channel_id=1, source_target_pairs={{0,18},{1,19},{2,16},{3,17},{4,22},{5,23},{6,20},{7,21},{8,26},{9,... | collective-permute-start | bytes 208904 | tf_op jit(solution)/shard_map/ppermute | solution.py:199
  92.2 10.2 %collective-permute-start.35 = (f16[136,256]{1,0:T(8,128)(2,1)S(1)}, f16[136,256]{1,0:T(8,128)(2,1)S(1)}, u32[]{:S(2)}, u32[]{:S(2)}) collective-permute-start(f16[136,256]{1,0:T(8,128)(2,1)S(1)} %get-tuple-element.41), channel_id=1, source_target_pairs={{0,16},{1,17},{2,18},{3,19},{4,20},{5,21},{6,22},{7,23},{8,24},{9,... | collective-permute-start | bytes 208904 | tf_op jit(solution)/shard_map/ppermute | solution.py:199
  95.9 7.9 %collective-permute-start.34 = (f16[136,256]{1,0:T(8,128)(2,1)S(1)}, f16[136,256]{1,0:T(8,128)(2,1)S(1)}, u32[]{:S(2)}, u32[]{:S(2)}) collective-permute-start(f16[136,256]{1,0:T(8,128)(2,1)S(1)} %get-tuple-element.42), channel_id=1, source_target_pairs={{0,10},{1,11},{2,8},{3,9},{4,14},{5,15},{6,12},{7,13},{8,2},{9,3},... | collective-permute-start | bytes 208904 | tf_op jit(solution)/shard_map/ppermute | solution.py:199
  (24 other events, 125.2 us)

commit v3 on v2

v3 whole, which is shorter than its diff:
```python
import functools
import math

import jax
import jax.numpy as jnp
import numpy as np
from jax import lax
from jax.experimental import pallas as pl
from jax.experimental.pallas import tpu as pltpu
from jax.sharding import PartitionSpec as P

EXTRA = 8
VMEM_BYTES = 16 * 2**20
ANY = pl.BlockSpec(memory_space=pl.ANY)
HBM = pl.BlockSpec(memory_space=pltpu.HBM)
VMEM = pl.BlockSpec(memory_space=pltpu.VMEM)
PARAMS = pltpu.CompilerParams(vmem_limit_bytes=VMEM_BYTES)


def flip(cells, axis, bits):
    count = lax.axis_size(axis)
    return lax.ppermute(cells, axis, [(i, i ^ bits) for i in range(count)])


def after(value, *earlier):
    return lax.optimization_barrier((value, *earlier))[0]


def row_factors(nlat, fields, nlon):
    cosine = np.cos(np.deg2rad(45.0 + 0.5 * (np.arange(nlat) + 0.5 - nlat / 2.0)))
    total = fields * nlon * cosine.sum()
    return [float(value) for value in np.sqrt(cosine) * total ** (-0.25)]


def chosen(values, at):
    value = jnp.float32(values[0])
    for n in range(1, len(values)):
        value = jnp.where(at == n, jnp.float32(values[n]), value)
    return value


def smooth_kernel(part, edges, factors, x_hbm, lon_hbm, lat_hbm, *rest):
    if edges:
        above_hbm, below_hbm, *rest = rest
    *out_refs, x_ref, lon_ref, lat_ref, above_ref, below_ref, sems = rest
    sources = [(lon_hbm, lon_ref), (lat_hbm, lat_ref), (x_hbm, x_ref)]
    if edges:
        sources += [(above_hbm, above_ref), (below_hbm, below_ref)]
    copies = [pltpu.make_async_copy(a, b, sems.at[n]) for n, (a, b) in enumerate(sources)]
    for copy in copies:
        copy.start()
    for copy in copies:
        copy.wait()
    rows, nlon, snaps = x_ref.shape[1:]
    if not edges:
        tail_ref, head_ref, *out_refs = out_refs
        tail_ref[...] = x_ref[:, rows - 1]
        head_ref[...] = x_ref[:, 0]
    layers = len(out_refs)
    layer, band = lax.axis_index("snap") // 2, lax.axis_index("space")
    inner = x_ref.shape[0] * (rows - 2)
    for j in reversed(range(layers)):
        n = part * layers + (layer ^ j)
        field, row = n // (rows - 2), 1 + n % (rows - 2)
        if edges:
            m = n - inner
            field = jnp.where(m < 0, field, m // 2)
            row = jnp.where(m < 0, row, (rows - 1) * (m % 2))
        up = x_ref[field, jnp.maximum(row - 1, 0)].astype(jnp.float32)
        down = x_ref[field, jnp.minimum(row + 1, rows - 1)].astype(jnp.float32)
        if edges:
            up = jnp.where(row == 0, above_ref[field].astype(jnp.float32), up)
            down = jnp.where(row == rows - 1, below_ref[field].astype(jnp.float32), down)
        x = x_ref[field, row].astype(jnp.float32)
        lon = jnp.broadcast_to(lon_ref[field, pl.ds(row, 1), :], (snaps, nlon)).T
        lat = jnp.broadcast_to(lat_ref[field, pl.ds(row, 1), :], (snaps, nlon)).T
        lon_part = pltpu.roll(x, 1, 0) + pltpu.roll(x, nlon - 1, 0) - 2.0 * x
        lat_part = up + down - 2.0 * x
        smooth = x + lon * lon_part + lat * lat_part
        factor = chosen(factors, band * rows + row)
        out_refs[j][...] = (smooth * factor).astype(jnp.bfloat16)


def scaled_part(part, layers, factors, cells, lon_coeff, lat_coeff, halo):
    fields, rows, nlon, snaps = cells.shape
    edge = (fields, nlon, snaps)
    row = jax.ShapeDtypeStruct((nlon, snaps), jnp.bfloat16)
    out_shape = [row] * layers
    in_place = [pltpu.with_memory_space_constraint(v, pltpu.HBM) for v in (cells, lon_coeff, lat_coeff)]
    if not halo:
        out_shape = [jax.ShapeDtypeStruct(edge, cells.dtype)] * 2 + out_shape
    return pl.pallas_call(
        functools.partial(smooth_kernel, part, bool(halo), factors),
        out_shape=out_shape,
        in_specs=[HBM] * 3 + [ANY] * len(halo),
        out_specs=[VMEM] * len(out_shape),
        scratch_shapes=[
            pltpu.VMEM(cells.shape, cells.dtype),
            pltpu.VMEM(lon_coeff.shape, lon_coeff.dtype),
            pltpu.VMEM(lat_coeff.shape, lat_coeff.dtype),
            pltpu.VMEM(edge, cells.dtype),
            pltpu.VMEM(edge, cells.dtype),
            pltpu.SemaphoreType.DMA((5,)),
        ],
        compiler_params=PARAMS,
        name="smooth_rows",
    )(*in_place, *halo)


def turn_kernel(*refs):
    *pieces, out_ref = refs
    snaps = pieces[0].shape[1]
    at = [lax.broadcasted_iota(jnp.int32, (snaps, snaps), axis) for axis in (0, 1)]
    one = jnp.where(at[0] == at[1], 1.0, 0.0).astype(jnp.bfloat16)
    for n, piece in enumerate(pieces):
        turned = lax.dot_general(
            one, piece[...], (((1,), (1,)), ((), ())), preferred_element_type=jnp.float32
        )
        out_ref[n // 2, n % 2] = turned.astype(jnp.bfloat16)


def turned(pieces):
    depth, snaps = pieces[0].shape
    return pl.pallas_call(
        turn_kernel,
        out_shape=jax.ShapeDtypeStruct((len(pieces) // 2, 2, snaps, depth), jnp.bfloat16),
        in_specs=[VMEM] * len(pieces),
        out_specs=VMEM,
        compiler_params=PARAMS,
        name="turn_pieces",
    )(*pieces)


def product_kernel(layers, columns, share, last, left_ref, *refs):
    count, picks = 4 * layers, columns * share
    pieces, refs = refs[:count], refs[count:]
    if last:
        sum_ref, own_ref, out_ref, right, sems = refs
    else:
        out_ref, right, sems = refs
    depth, snaps = pieces[0].shape
    me, band = lax.axis_index("snap"), lax.axis_index("space")
    for i in range(columns):
        for g in range(share):
            c = i * share + g
            wanted = ((((band // 2) ^ i) * 2 + band % 2) * share + g) ^ me
            for n, piece in enumerate(pieces):

                @pl.when(wanted == n // 2)
                def _():
                    pltpu.make_async_copy(
                        piece, right.at[n % 2, :, pl.ds(c * snaps, snaps)], sems.at[c, n % 2]
                    ).start()

    for c in range(picks):
        for side in range(2):
            pltpu.make_async_copy(
                pieces[side], right.at[side, :, pl.ds(c * snaps, snaps)], sems.at[c, side]
            ).wait()
    blocks, wide = [], out_ref.shape[2]
    for j in range(layers):
        product = sum(
            jnp.dot(left_ref[j, side], right[side], preferred_element_type=jnp.float32)
            for side in range(2)
        )
        for i in range(columns):
            blocks.append(product[:, i * wide : (i + 1) * wide])
    if not last:
        for n, block in enumerate(blocks):
            out_ref[n] = block
        return
    blocks = [block + sum_ref[n] for n, block in enumerate(blocks)]
    own_ref[...] = blocks[0]
    largest = functools.reduce(jnp.maximum, [jnp.abs(block) for block in blocks[1:]])
    largest = jnp.maximum(jnp.max(largest, axis=(0, 1), keepdims=True), 1e-30)
    power = jnp.ceil(jnp.log2(largest)) - 15.0
    scale = jnp.exp2(-power)
    for n, block in enumerate(blocks[1:]):
        out_ref[n, :snaps] = block * scale
        out_ref[n, snaps:] = jnp.broadcast_to(power, (EXTRA, block.shape[1]))


def product_part(layers, columns, share, left, pieces, so_far):
    depth, snaps = pieces[0].shape
    picks, wide, count = columns * share, share * snaps, layers * columns
    last = so_far is not None
    if last:
        out_shape = [
            jax.ShapeDtypeStruct((snaps, wide), jnp.float32),
            jax.ShapeDtypeStruct((count - 1, snaps + EXTRA, wide), jnp.float32),
        ]
    else:
        out_shape = [jax.ShapeDtypeStruct((count, snaps, wide), jnp.float32)]
    return pl.pallas_call(
        functools.partial(product_kernel, layers, columns, share, last),
        out_shape=out_shape,
        in_specs=[VMEM] + [ANY] * len(pieces) + [VMEM] * last,
        out_specs=[VMEM] * len(out_shape),
        scratch_shapes=[
            pltpu.VMEM((2, depth, picks * snaps), jnp.bfloat16),
            pltpu.SemaphoreType.DMA((picks, 2)),
        ],
        compiler_params=PARAMS,
        name="block_products",
    )(left, *pieces, *([so_far] if last else []))


def shards(snapshots, lon_coeff, lat_coeff):
    snaps, fields, rows, nlon = snapshots.shape
    groups, bands = lax.axis_size("snap"), lax.axis_size("space")
    layers, columns, share = groups // 2, bands // 2, groups // bands
    parts = fields * rows // layers
    inner_parts = fields * (rows - 2) // layers

    factors = row_factors(bands * rows, fields, nlon)
    cells = jnp.transpose(snapshots, (1, 2, 3, 0))
    tail, head = cells[:, rows - 1], cells[:, 0]
    scaled = []
    for t in range(inner_parts):
        tail, head, *part = scaled_part(t, layers, factors, cells, lon_coeff, lat_coeff, ())
        scaled.append(part)
    if scaled:
        tail, head = after((tail, head), flip(scaled[0][0], "space", 1))
    ends = bands - 1
    halo = (
        lax.ppermute(tail, "space", [(i, i + 1) for i in range(ends)]),
        lax.ppermute(head, "space", [(i + 1, i) for i in range(ends)]),
    )
    scaled += [
        scaled_part(t, layers, factors, cells, lon_coeff, lat_coeff, halo)
        for t in range(inner_parts, parts)
    ]
    ready = scaled[-1][0]

    far = range(layers // 2, layers)
    near = range(1, layers // 2)
    own = [after(scaled[t][0], ready) for t in range(parts)]
    held = [{0: own[t]} for t in range(parts)]
    other = [{0: flip(own[t], "snap", 1)} for t in range(parts)]
    begun = [other[t][0] for t in range(parts)]
    for t in range(parts):
        for j in near:
            held[t][j] = after(flip(scaled[t][j], "snap", 2 * j), ready, *begun)
            other[t][j] = flip(held[t][j], "snap", 1)
    for t in range(parts):
        for j in far:
            held[t][j] = after(flip(scaled[t][j], "snap", 2 * j), ready, *begun)
            other[t][j] = flip(held[t][j], "snap", 1)
        begun = [other[t][j] for j in far]
    final = [held[parts - 1][j] for j in far]
    product = None
    for t in range(parts):
        rows_of, pieces = [], []
        for j in range(layers):
            mine, theirs = held[t][j], other[t][j]
            mine_too = flip(after(mine, *final), "space", 1)
            theirs_too = flip(after(theirs, *final), "space", 1)
            rows_of += [mine, mine_too]
            pieces += [mine, mine_too, theirs, theirs_too]
        left = turned(rows_of)
        if t < parts - 1 and product is None:
            (product,) = product_part(layers, columns, share, left, pieces, None)
    if product is None:
        product = jnp.zeros((layers * columns, snaps, share * snaps), jnp.float32)
    own, blocks = product_part(layers, columns, share, left, pieces, product)

    blocks = blocks.astype(jnp.float16)
    total = own
    for j in range(layers):
        for i in range(columns):
            if i or j:
                pairs = [
                    (s * bands + b, (s ^ (2 * j)) * bands + (b ^ (2 * i)))
                    for s in range(groups)
                    for b in range(bands)
                ]
                block = lax.ppermute(blocks[j * columns + i - 1], ("snap", "space"), pairs)
                block = block.astype(jnp.float32)
                total += block[:snaps] * jnp.exp2(block[snaps : snaps + 1])
    return total


def solution(mesh):
    return jax.shard_map(
        shards,
        mesh=mesh,
        in_specs=(P("snap", None, "space", None), P(None, "space", None), P(None, "space", None)),
        out_specs=P("snap", "space"),
        check_vma=False,
    )
```

time: 105 us -> 80.5 us (0.77)
  waiting for transfers between devices: 45.6 us -> 25.3 us
  starting transfers between devices: 38 us -> 43.9 us
  local copies, waits for them, and re-layouts: 5.78 us -> 0.1 us
  Pallas kernels: 13.9 us -> 9.72 us
    ppermute x30, waiting for transfers between devices: 39.4 us -> 22.5 us  [flip(): return lax.ppermute(cells, axis, [(i, i ^ bits) for i in range(count)])]
    unnamed x18 -> x0, local copies, waits for them, and re-layouts: 4.91 us -> none
    pallas_call x4 -> x6, Pallas kernels: 13.9 us -> 9.72 us  [the longest x2 5.13 us: scaled_part(): pl.pallas_call(functools.partial(smooth_kernel, part, bool(halo), factors...]
    ppermute x30, starting transfers between devices: 22.7 us -> 26.1 us  [flip(): return lax.ppermute(cells, axis, [(i, i ^ bits) for i in range(count)])]
    ppermute x7, waiting for transfers between devices: 6.17 us -> 2.8 us  [shards(): block = lax.ppermute(blocks[j * columns + i - 1], ('snap', 'space'), pairs)]
    ppermute x7, starting transfers between devices: 11.6 us -> 14.1 us  [shards(): block = lax.ppermute(blocks[j * columns + i - 1], ('snap', 'space'), pairs)]
  transfers between devices with their start and end apart: 39 -> 39, of which waited for: 11 -> 9; matrix products, arithmetic and copies ran while one was open for 0% -> 0% of each run, Pallas kernels for 7% -> 7%
where the time goes in v3:
time: 80.5 us; the launch traced here: 80.3 us
  starting transfers between devices  43.9 us (55%)
  waiting for transfers between devices  25.3 us (31%)
  Pallas kernels  9.72 us (12%)
  other arithmetic  0.96 us (1%)
    ppermute x30, starting transfers between devices, flip(): return lax.ppermute(cells, axis, [(i, i ^ bits) for i in range(count)])  26.1 us
    ppermute x30, waiting for transfers between devices, flip(): return lax.ppermute(cells, axis, [(i, i ^ bits) for i in range(count)])  22.5 us
    ppermute x7, starting transfers between devices, shards(): block = lax.ppermute(blocks[j * columns + i - 1], ('snap', 'space'), pairs)  14.1 us
    pallas_call x2, Pallas kernels, scaled_part(): pl.pallas_call(functools.partial(smooth_kernel, part, bool(halo), factors...  5.13 us
    pallas_call x2, Pallas kernels, product_part(): pl.pallas_call(functools.partial(product_kernel, layers, columns, share,...  3.22 us
    ppermute x7, waiting for transfers between devices, shards(): block = lax.ppermute(blocks[j * columns + i - 1], ('snap', 'space'), pairs)  2.8 us
    ppermute x1, starting transfers between devices, shards(): lax.ppermute(tail, 'space', [(i, i + 1) for i in range(ends)])  2.38 us
  transfers between devices with their start and end apart: 39, of which 9 were waited for; matrix products, arithmetic and copies ran while one was open for 0% of the time, Pallas kernels for 7%

profile of v3, /device:TPU:0, one launch (start us, length us, event | category | flops | bytes accessed | tf_op | source)
XLA Modules:
  0.0 80.3 jit_solution(12735954209398390388)
XLA Ops:
  0.0 2.5 %smooth_rows.2 = (bf16[2,720,128]{2,1,0:T(8,128)(2,1)S(1)}, bf16[2,720,128]{2,1,0:T(8,128)(2,1)S(1)}, bf16[720,128]{1,0:T(8,128)(2,1)S(1)}, bf16[720,128]{1,0:T(...) custom-call(bf16[2,4,720,128]{3,2,1,0:T(8,128)(2,1)} %bitcast.22, f32[2,4,720]{2,1,0:T(4,128)} %lon_hbm.3, ...), custom_call_target="tpu_custom_call" | custom-call | tf_op jit(solution)/shard_map/smooth_rows/pallas_call | solution.py:92
  2.5 2.4 %collective-permute-start = (bf16[2,720,128]{2,1,0:T(8,128)(2,1)S(1)}, bf16[2,720,128]{2,1,0:T(8,128)(2,1)S(1)}, u32[]{:S(2)}, u32[]{:S(2)}) collective-permute-start(bf16[2,720,128]{2,1,0:T(8,128)(2,1)S(1)} %get-tuple-element.45), channel_id=1, source_target_pairs={{0,1},{1,2},{2,3},{4,5},{5,6},{6,7},{8,9},{9,10},{10,11},{12,13},{... | collective-permute-start | bytes 1105928 | tf_op jit(solution)/shard_map/ppermute | solution.py:226
  4.9 1.3 %collective-permute-start.1 = (bf16[2,720,128]{2,1,0:T(8,128)(2,1)S(1)}, bf16[2,720,128]{2,1,0:T(8,128)(2,1)S(1)}, u32[]{:S(2)}, u32[]{:S(2)}) collective-permute-start(bf16[2,720,128]{2,1,0:T(8,128)(2,1)S(1)} %get-tuple-element.46), channel_id=1, source_target_pairs={{1,0},{2,1},{3,2},{5,4},{6,5},{7,6},{9,8},{10,9},{11,10},{13,12},{... | collective-permute-start | bytes 1105928 | tf_op jit(solution)/shard_map/ppermute | solution.py:227
  6.2 4.5 %collective-permute-start.7 = (bf16[720,128]{1,0:T(8,128)(2,1)S(1)}, bf16[720,128]{1,0:T(8,128)(2,1)S(1)}, u32[]{:S(2)}, u32[]{:S(2)}) collective-permute-start(bf16[720,128]{1,0:T(8,128)(2,1)S(1)} %get-tuple-element.54), channel_id=1, source_target_pairs={{0,24},{4,28},{8,16},{12,20},{16,8},{20,12},{24,0},{28,4},{1,25},{... | collective-permute-start | bytes 552968 | tf_op jit(solution)/shard_map/ppermute | solution.py:22
  10.7 2.6 %smooth_rows.3 = (bf16[720,128]{1,0:T(8,128)(2,1)S(1)}, bf16[720,128]{1,0:T(8,128)(2,1)S(1)}, bf16[720,128]{1,0:T(8,128)(2,1)S(1)}, bf16[720,128]{1,0:T(8,128)(2,1)S(1)}) custom-call(bf16[2,4,720,128]{3,2,1,0:T(8,128)(2,1)} %bitcast.23, f32[2,4,720]{2,1,0:T(4,128)} %lon_hbm.3, f32[2,4,720]{2,1,0:T(4,128)} %lat_hbm.3, ...), custom_call_target="tpu_custom_call" | custom-call | tf_op jit(solution)/shard_map/smooth_rows/pallas_call | solution.py:92
  13.3 1.6 %collective-permute-start.4 = (bf16[720,128]{1,0:T(8,128)(2,1)S(1)}, bf16[720,128]{1,0:T(8,128)(2,1)S(1)}, u32[]{:S(2)}, u32[]{:S(2)}) collective-permute-start(bf16[720,128]{1,0:T(8,128)(2,1)S(1)} %get-tuple-element.69.refs_0_), channel_id=1, source_target_pairs={{0,4},{4,0},{8,12},{12,8},{16,20},{20,16},{24,28},{28,24},{1,5},{5... | collective-permute-start | bytes 552968 | tf_op jit(solution)/shard_map/ppermute | solution.py:22
  15.4 2.5 %collective-permute-start.3 = (bf16[720,128]{1,0:T(8,128)(2,1)S(1)}, bf16[720,128]{1,0:T(8,128)(2,1)S(1)}, u32[]{:S(2)}, u32[]{:S(2)}) collective-permute-start(bf16[720,128]{1,0:T(8,128)(2,1)S(1)} %get-tuple-element.50), channel_id=1, source_target_pairs={{0,16},{4,20},{8,24},{12,28},{16,0},{20,4},{24,8},{28,12},{1,17},{... | collective-permute-start | bytes 552968 | tf_op jit(solution)/shard_map/ppermute | solution.py:22
  17.9 1.6 %collective-permute-start.23 = (bf16[720,128]{1,0:T(8,128)(2,1)S(1)}, bf16[720,128]{1,0:T(8,128)(2,1)S(1)}, u32[]{:S(2)}, u32[]{:S(2)}) collective-permute-start(bf16[720,128]{1,0:T(8,128)(2,1)S(1)} %get-tuple-element.70), channel_id=1, source_target_pairs={{0,8},{4,12},{8,0},{12,4},{16,24},{20,28},{24,16},{28,20},{1,9},{5... | collective-permute-start | bytes 552968 | tf_op jit(solution)/shard_map/ppermute | solution.py:22
  19.9 2.5 %collective-permute-start.9 = (bf16[720,128]{1,0:T(8,128)(2,1)S(1)}, bf16[720,128]{1,0:T(8,128)(2,1)S(1)}, u32[]{:S(2)}, u32[]{:S(2)}) collective-permute-start(bf16[720,128]{1,0:T(8,128)(2,1)S(1)} %get-tuple-element.57), channel_id=1, source_target_pairs={{0,24},{4,28},{8,16},{12,20},{16,8},{20,12},{24,0},{28,4},{1,25},{... | collective-permute-start | bytes 552968 | tf_op jit(solution)/shard_map/ppermute | solution.py:22
  22.4 1.5 %collective-permute-start.8 = (bf16[720,128]{1,0:T(8,128)(2,1)S(1)}, bf16[720,128]{1,0:T(8,128)(2,1)S(1)}, u32[]{:S(2)}, u32[]{:S(2)}) collective-permute-start(bf16[720,128]{1,0:T(8,128)(2,1)S(1)} %collective-permute-done.7.refs_6_.refs_12_), channel_id=1, source_target_pairs={{0,4},{4,0},{8,12},{12,8},{16,20},{20,16},{24,28},{28,24},{1,5},{5... | collective-permute-start | bytes 552968 | tf_op jit(solution)/shard_map/ppermute | solution.py:22
  23.9 1.5 %collective-permute-start.6 = (bf16[720,128]{1,0:T(8,128)(2,1)S(1)}, bf16[720,128]{1,0:T(8,128)(2,1)S(1)}, u32[]{:S(2)}, u32[]{:S(2)}) collective-permute-start(bf16[720,128]{1,0:T(8,128)(2,1)S(1)} %collective-permute-done.3.refs_4_.refs_8_), channel_id=1, source_target_pairs={{0,4},{4,0},{8,12},{12,8},{16,20},{20,16},{24,28},{28,24},{1,5},{5... | collective-permute-start | bytes 552968 | tf_op jit(solution)/shard_map/ppermute | solution.py:22
  25.9 5.4 %collective-permute-done.11.refs_2_.refs_4_ = bf16[720,128]{1,0:T(8,128)(2,1)S(1)} collective-permute-done((bf16[720,128]{1,0:T(8,128)(2,1)S(1)}, bf16[720,128]{1,0:T(8,128)(2,1)S(1)}, u32[]{:S(2)}, u32[]{:S(2)}) %collective-permute-start.11) | collective-permute-done | bytes 184352 | tf_op jit(solution)/shard_map/ppermute | solution.py:22
  31.3 1.5 %collective-permute-start.28 = (bf16[720,128]{1,0:T(8,128)(2,1)S(1)}, bf16[720,128]{1,0:T(8,128)(2,1)S(1)}, u32[]{:S(2)}, u32[]{:S(2)}) collective-permute-start(bf16[720,128]{1,0:T(8,128)(2,1)S(1)} %collective-permute-done.23.refs_2_.refs_4_), channel_id=1, source_target_pairs={{0,4},{4,0},{8,12},{12,8},{16,20},{20,16},{24,28},{28,24},{1,5},{5... | collective-permute-start | bytes 552968 | tf_op jit(solution)/shard_map/ppermute | solution.py:22
  33.6 8.6 %collective-permute-done.2.refs_4_.refs_8_ = bf16[720,128]{1,0:T(8,128)(2,1)S(1)} collective-permute-done((bf16[720,128]{1,0:T(8,128)(2,1)S(1)}, bf16[720,128]{1,0:T(8,128)(2,1)S(1)}, u32[]{:S(2)}, u32[]{:S(2)}) %collective-permute-start.2) | collective-permute-done | bytes 184352 | tf_op jit(solution)/shard_map/ppermute | solution.py:22
  42.2 1.5 %collective-permute-start.31 = (bf16[720,128]{1,0:T(8,128)(2,1)S(1)}, bf16[720,128]{1,0:T(8,128)(2,1)S(1)}, u32[]{:S(2)}, u32[]{:S(2)}) collective-permute-start(bf16[720,128]{1,0:T(8,128)(2,1)S(1)} %collective-permute-done.8.refs_14_), channel_id=1, source_target_pairs={{0,1},{1,0},{2,3},{3,2},{4,5},{5,4},{6,7},{7,6},{8,9},{9,8},{10,11... | collective-permute-start | bytes 552968 | tf_op jit(solution)/shard_map/ppermute | solution.py:22
  45.2 1.5 %collective-permute-start.20 = (bf16[720,128]{1,0:T(8,128)(2,1)S(1)}, bf16[720,128]{1,0:T(8,128)(2,1)S(1)}, u32[]{:S(2)}, u32[]{:S(2)}) collective-permute-start(bf16[720,128]{1,0:T(8,128)(2,1)S(1)} %collective-permute-done.9.refs_6_.refs_12_), channel_id=1, source_target_pairs={{0,4},{4,0},{8,12},{12,8},{16,20},{20,16},{24,28},{28,24},{1,5},{5... | collective-permute-start | bytes 552968 | tf_op jit(solution)/shard_map/ppermute | solution.py:22
  47.8 4.8 %collective-permute-done.20.refs_14_ = bf16[720,128]{1,0:T(8,128)(2,1)S(1)} collective-permute-done((bf16[720,128]{1,0:T(8,128)(2,1)S(1)}, bf16[720,128]{1,0:T(8,128)(2,1)S(1)}, u32[]{:S(2)}, u32[]{:S(2)}) %collective-permute-start.20) | collective-permute-done | bytes 184352 | tf_op jit(solution)/shard_map/ppermute | solution.py:22
  52.7 3.3 %collective-permute-done.18.refs_10_ = bf16[720,128]{1,0:T(8,128)(2,1)S(1)} collective-permute-done((bf16[720,128]{1,0:T(8,128)(2,1)S(1)}, bf16[720,128]{1,0:T(8,128)(2,1)S(1)}, u32[]{:S(2)}, u32[]{:S(2)}) %collective-permute-start.18) | collective-permute-done | bytes 184352 | tf_op jit(solution)/shard_map/ppermute | solution.py:22
  58.9 1.5 %block_products.2.refs_16_ = f32[8,128,256]{2,1,0:T(8,128)S(1)} custom-call(bf16[4,2,128,720]{3,2,1,0:T(8,128)(2,1)S(1)} %turn_pieces.3.left_ref, bf16[720,128]{1,0:T(8,128)(2,1)S(1)} %get-tuple-element.69.refs_0_, bf16[720,128]{1,0:T(8,128)(2,1)S(1)} %collective-permute-done.22.refs_1_, bf16[720,128]{1,0:T(8,128)(2,1)S(1)} %collective-permute-done.4.refs_2_, ...), custom_call_target="tpu_custom_call" | custom-call | tf_op jit(solution)/shard_map/block_products/pallas_call | solution.py:194
  60.5 1.7 %block_products.3 = (f32[128,256]{1,0:T(8,128)S(1)}, f32[7,136,256]{2,1,0:T(8,128)S(1)}) custom-call(bf16[4,2,128,720]{3,2,1,0:T(8,128)(2,1)S(1)} %turn_pieces.2.left_ref, bf16[720,128]{1,0:T(8,128)(2,1)S(1)} %get-tuple-element.59.refs_0_, bf16[720,128]{1,0:T(8,128)(2,1)S(1)} %collective-permute-done.10.refs_1_, ...), custom_call_target="tpu_custom_call" | custom-call | tf_op jit(solution)/shard_map/block_products/pallas_call | solution.py:194
  62.4 4.9 %collective-permute-start.36 = (f16[136,256]{1,0:T(8,128)(2,1)S(1)}, f16[136,256]{1,0:T(8,128)(2,1)S(1)}, u32[]{:S(2)}, u32[]{:S(2)}) collective-permute-start(f16[136,256]{1,0:T(8,128)(2,1)S(1)} %get-tuple-element.84), channel_id=1, source_target_pairs={{0,18},{1,19},{2,16},{3,17},{4,22},{5,23},{6,20},{7,21},{8,26},{9,... | collective-permute-start | bytes 208904 | tf_op jit(solution)/shard_map/ppermute | solution.py:277
  68.4 2.2 %collective-permute-start.38 = (f16[136,256]{1,0:T(8,128)(2,1)S(1)}, f16[136,256]{1,0:T(8,128)(2,1)S(1)}, u32[]{:S(2)}, u32[]{:S(2)}) collective-permute-start(f16[136,256]{1,0:T(8,128)(2,1)S(1)} %get-tuple-element.82), channel_id=1, source_target_pairs={{0,26},{1,27},{2,24},{3,25},{4,30},{5,31},{6,28},{7,29},{8,18},{9,... | collective-permute-start | bytes 208904 | tf_op jit(solution)/shard_map/ppermute | solution.py:277
  70.6 2.0 %collective-permute-start.32 = (f16[136,256]{1,0:T(8,128)(2,1)S(1)}, f16[136,256]{1,0:T(8,128)(2,1)S(1)}, u32[]{:S(2)}, u32[]{:S(2)}) collective-permute-start(f16[136,256]{1,0:T(8,128)(2,1)S(1)} %get-tuple-element.81), channel_id=1, source_target_pairs={{0,2},{1,3},{2,0},{3,1},{4,6},{5,7},{6,4},{7,5},{8,10},{9,11},{10,... | collective-permute-start | bytes 208904 | tf_op jit(solution)/shard_map/ppermute | solution.py:277
  74.1 2.8 %collective-permute-start.35 = (f16[136,256]{1,0:T(8,128)(2,1)S(1)}, f16[136,256]{1,0:T(8,128)(2,1)S(1)}, u32[]{:S(2)}, u32[]{:S(2)}) collective-permute-start(f16[136,256]{1,0:T(8,128)(2,1)S(1)} %get-tuple-element.85), channel_id=1, source_target_pairs={{0,16},{1,17},{2,18},{3,19},{4,20},{5,21},{6,22},{7,23},{8,24},{9,... | collective-permute-start | bytes 208904 | tf_op jit(solution)/shard_map/ppermute | solution.py:277
  (77 shorter events, 13.9 us)
Async XLA Ops:
  2.5 8.2 %collective-permute-start = (bf16[2,720,128]{2,1,0:T(8,128)(2,1)S(1)}, bf16[2,720,128]{2,1,0:T(8,128)(2,1)S(1)}, u32[]{:S(2)}, u32[]{:S(2)}) collective-permute-start(bf16[2,720,128]{2,1,0:T(8,128)(2,1)S(1)} %get-tuple-element.45), channel_id=1, source_target_pairs={{0,1},{1,2},{2,3},{4,5},{5,6},{6,7},{8,9},{9,10},{10,11},{12,13},{... | collective-permute-start | bytes 1105928 | tf_op jit(solution)/shard_map/ppermute | solution.py:226
  4.9 5.8 %collective-permute-start.1 = (bf16[2,720,128]{2,1,0:T(8,128)(2,1)S(1)}, bf16[2,720,128]{2,1,0:T(8,128)(2,1)S(1)}, u32[]{:S(2)}, u32[]{:S(2)}) collective-permute-start(bf16[2,720,128]{2,1,0:T(8,128)(2,1)S(1)} %get-tuple-element.46), channel_id=1, source_target_pairs={{1,0},{2,1},{3,2},{5,4},{6,5},{7,6},{9,8},{10,9},{11,10},{13,12},{... | collective-permute-start | bytes 1105928 | tf_op jit(solution)/shard_map/ppermute | solution.py:227
  6.2 13.3 %collective-permute-start.7 = (bf16[720,128]{1,0:T(8,128)(2,1)S(1)}, bf16[720,128]{1,0:T(8,128)(2,1)S(1)}, u32[]{:S(2)}, u32[]{:S(2)}) collective-permute-start(bf16[720,128]{1,0:T(8,128)(2,1)S(1)} %get-tuple-element.54), channel_id=1, source_target_pairs={{0,24},{4,28},{8,16},{12,20},{16,8},{20,12},{24,0},{28,4},{1,25},{... | collective-permute-start | bytes 552968 | tf_op jit(solution)/shard_map/ppermute | solution.py:22
  13.3 6.6 %collective-permute-start.4 = (bf16[720,128]{1,0:T(8,128)(2,1)S(1)}, bf16[720,128]{1,0:T(8,128)(2,1)S(1)}, u32[]{:S(2)}, u32[]{:S(2)}) collective-permute-start(bf16[720,128]{1,0:T(8,128)(2,1)S(1)} %get-tuple-element.69.refs_0_), channel_id=1, source_target_pairs={{0,4},{4,0},{8,12},{12,8},{16,20},{20,16},{24,28},{28,24},{1,5},{5... | collective-permute-start | bytes 552968 | tf_op jit(solution)/shard_map/ppermute | solution.py:22
  14.9 7.5 %collective-permute-start.5 = (bf16[720,128]{1,0:T(8,128)(2,1)S(1)}, bf16[720,128]{1,0:T(8,128)(2,1)S(1)}, u32[]{:S(2)}, u32[]{:S(2)}) collective-permute-start(bf16[720,128]{1,0:T(8,128)(2,1)S(1)} %get-tuple-element.59.refs_0_), channel_id=1, source_target_pairs={{0,4},{4,0},{8,12},{12,8},{16,20},{20,16},{24,28},{28,24},{1,5},{5... | collective-permute-start | bytes 552968 | tf_op jit(solution)/shard_map/ppermute | solution.py:22
  15.4 8.5 %collective-permute-start.3 = (bf16[720,128]{1,0:T(8,128)(2,1)S(1)}, bf16[720,128]{1,0:T(8,128)(2,1)S(1)}, u32[]{:S(2)}, u32[]{:S(2)}) collective-permute-start(bf16[720,128]{1,0:T(8,128)(2,1)S(1)} %get-tuple-element.50), channel_id=1, source_target_pairs={{0,16},{4,20},{8,24},{12,28},{16,0},{20,4},{24,8},{28,12},{1,17},{... | collective-permute-start | bytes 552968 | tf_op jit(solution)/shard_map/ppermute | solution.py:22
  17.9 7.6 %collective-permute-start.23 = (bf16[720,128]{1,0:T(8,128)(2,1)S(1)}, bf16[720,128]{1,0:T(8,128)(2,1)S(1)}, u32[]{:S(2)}, u32[]{:S(2)}) collective-permute-start(bf16[720,128]{1,0:T(8,128)(2,1)S(1)} %get-tuple-element.70), channel_id=1, source_target_pairs={{0,8},{4,12},{8,0},{12,4},{16,24},{20,28},{24,16},{28,20},{1,9},{5... | collective-permute-start | bytes 552968 | tf_op jit(solution)/shard_map/ppermute | solution.py:22
  19.4 11.8 %collective-permute-start.11 = (bf16[720,128]{1,0:T(8,128)(2,1)S(1)}, bf16[720,128]{1,0:T(8,128)(2,1)S(1)}, u32[]{:S(2)}, u32[]{:S(2)}) collective-permute-start(bf16[720,128]{1,0:T(8,128)(2,1)S(1)} %get-tuple-element.60), channel_id=1, source_target_pairs={{0,8},{4,12},{8,0},{12,4},{16,24},{20,28},{24,16},{28,20},{1,9},{5... | collective-permute-start | bytes 552968 | tf_op jit(solution)/shard_map/ppermute | solution.py:22
  19.9 12.9 %collective-permute-start.9 = (bf16[720,128]{1,0:T(8,128)(2,1)S(1)}, bf16[720,128]{1,0:T(8,128)(2,1)S(1)}, u32[]{:S(2)}, u32[]{:S(2)}) collective-permute-start(bf16[720,128]{1,0:T(8,128)(2,1)S(1)} %get-tuple-element.57), channel_id=1, source_target_pairs={{0,24},{4,28},{8,16},{12,20},{16,8},{20,12},{24,0},{28,4},{1,25},{... | collective-permute-start | bytes 552968 | tf_op jit(solution)/shard_map/ppermute | solution.py:22
  22.4 11.2 %collective-permute-start.8 = (bf16[720,128]{1,0:T(8,128)(2,1)S(1)}, bf16[720,128]{1,0:T(8,128)(2,1)S(1)}, u32[]{:S(2)}, u32[]{:S(2)}) collective-permute-start(bf16[720,128]{1,0:T(8,128)(2,1)S(1)} %collective-permute-done.7.refs_6_.refs_12_), channel_id=1, source_target_pairs={{0,4},{4,0},{8,12},{12,8},{16,20},{20,16},{24,28},{28,24},{1,5},{5... | collective-permute-start | bytes 552968 | tf_op jit(solution)/shard_map/ppermute | solution.py:22
  23.9 9.7 %collective-permute-start.6 = (bf16[720,128]{1,0:T(8,128)(2,1)S(1)}, bf16[720,128]{1,0:T(8,128)(2,1)S(1)}, u32[]{:S(2)}, u32[]{:S(2)}) collective-permute-start(bf16[720,128]{1,0:T(8,128)(2,1)S(1)} %collective-permute-done.3.refs_4_.refs_8_), channel_id=1, source_target_pairs={{0,4},{4,0},{8,12},{12,8},{16,20},{20,16},{24,28},{28,24},{1,5},{5... | collective-permute-start | bytes 552968 | tf_op jit(solution)/shard_map/ppermute | solution.py:22
  25.5 16.8 %collective-permute-start.2 = (bf16[720,128]{1,0:T(8,128)(2,1)S(1)}, bf16[720,128]{1,0:T(8,128)(2,1)S(1)}, u32[]{:S(2)}, u32[]{:S(2)}) collective-permute-start(bf16[720,128]{1,0:T(8,128)(2,1)S(1)} %get-tuple-element.49), channel_id=1, source_target_pairs={{0,16},{4,20},{8,24},{12,28},{16,0},{20,4},{24,8},{28,12},{1,17},{... | collective-permute-start | bytes 552968 | tf_op jit(solution)/shard_map/ppermute | solution.py:22
  31.3 12.5 %collective-permute-start.28 = (bf16[720,128]{1,0:T(8,128)(2,1)S(1)}, bf16[720,128]{1,0:T(8,128)(2,1)S(1)}, u32[]{:S(2)}, u32[]{:S(2)}) collective-permute-start(bf16[720,128]{1,0:T(8,128)(2,1)S(1)} %collective-permute-done.23.refs_2_.refs_4_), channel_id=1, source_target_pairs={{0,4},{4,0},{8,12},{12,8},{16,20},{20,16},{24,28},{28,24},{1,5},{5... | collective-permute-start | bytes 552968 | tf_op jit(solution)/shard_map/ppermute | solution.py:22
  32.8 11.5 %collective-permute-start.16 = (bf16[720,128]{1,0:T(8,128)(2,1)S(1)}, bf16[720,128]{1,0:T(8,128)(2,1)S(1)}, u32[]{:S(2)}, u32[]{:S(2)}) collective-permute-start(bf16[720,128]{1,0:T(8,128)(2,1)S(1)} %collective-permute-done.11.refs_2_.refs_4_), channel_id=1, source_target_pairs={{0,4},{4,0},{8,12},{12,8},{16,20},{20,16},{24,28},{28,24},{1,5},{5... | collective-permute-start | bytes 552968 | tf_op jit(solution)/shard_map/ppermute | solution.py:22
  45.2 7.5 %collective-permute-start.20 = (bf16[720,128]{1,0:T(8,128)(2,1)S(1)}, bf16[720,128]{1,0:T(8,128)(2,1)S(1)}, u32[]{:S(2)}, u32[]{:S(2)}) collective-permute-start(bf16[720,128]{1,0:T(8,128)(2,1)S(1)} %collective-permute-done.9.refs_6_.refs_12_), channel_id=1, source_target_pairs={{0,4},{4,0},{8,12},{12,8},{16,20},{20,16},{24,28},{28,24},{1,5},{5... | collective-permute-start | bytes 552968 | tf_op jit(solution)/shard_map/ppermute | solution.py:22
  46.7 9.2 %collective-permute-start.18 = (bf16[720,128]{1,0:T(8,128)(2,1)S(1)}, bf16[720,128]{1,0:T(8,128)(2,1)S(1)}, u32[]{:S(2)}, u32[]{:S(2)}) collective-permute-start(bf16[720,128]{1,0:T(8,128)(2,1)S(1)} %collective-permute-done.2.refs_4_.refs_8_), channel_id=1, source_target_pairs={{0,4},{4,0},{8,12},{12,8},{16,20},{20,16},{24,28},{28,24},{1,5},{5... | collective-permute-start | bytes 552968 | tf_op jit(solution)/shard_map/ppermute | solution.py:22
  47.2 8.7 %collective-permute-start.22 = (bf16[720,128]{1,0:T(8,128)(2,1)S(1)}, bf16[720,128]{1,0:T(8,128)(2,1)S(1)}, u32[]{:S(2)}, u32[]{:S(2)}) collective-permute-start(bf16[720,128]{1,0:T(8,128)(2,1)S(1)} %get-tuple-element.69.refs_0_), channel_id=1, source_target_pairs={{0,1},{1,0},{2,3},{3,2},{4,5},{5,4},{6,7},{7,6},{8,9},{9,8},{10,11... | collective-permute-start | bytes 552968 | tf_op jit(solution)/shard_map/ppermute | solution.py:22
  47.2 9.2 %collective-permute-start.14 = (bf16[720,128]{1,0:T(8,128)(2,1)S(1)}, bf16[720,128]{1,0:T(8,128)(2,1)S(1)}, u32[]{:S(2)}, u32[]{:S(2)}) collective-permute-start(bf16[720,128]{1,0:T(8,128)(2,1)S(1)} %collective-permute-done.9.refs_6_.refs_12_), channel_id=1, source_target_pairs={{0,1},{1,0},{2,3},{3,2},{4,5},{5,4},{6,7},{7,6},{8,9},{9,8},{10,11... | collective-permute-start | bytes 552968 | tf_op jit(solution)/shard_map/ppermute | solution.py:22
  47.8 8.8 %collective-permute-start.13 = (bf16[720,128]{1,0:T(8,128)(2,1)S(1)}, bf16[720,128]{1,0:T(8,128)(2,1)S(1)}, u32[]{:S(2)}, u32[]{:S(2)}) collective-permute-start(bf16[720,128]{1,0:T(8,128)(2,1)S(1)} %collective-permute-done.2.refs_4_.refs_8_), channel_id=1, source_target_pairs={{0,1},{1,0},{2,3},{3,2},{4,5},{5,4},{6,7},{7,6},{8,9},{9,8},{10,11... | collective-permute-start | bytes 552968 | tf_op jit(solution)/shard_map/ppermute | solution.py:22
  62.4 10.5 %collective-permute-start.36 = (f16[136,256]{1,0:T(8,128)(2,1)S(1)}, f16[136,256]{1,0:T(8,128)(2,1)S(1)}, u32[]{:S(2)}, u32[]{:S(2)}) collective-permute-start(f16[136,256]{1,0:T(8,128)(2,1)S(1)} %get-tuple-element.84), channel_id=1, source_target_pairs={{0,18},{1,19},{2,16},{3,17},{4,22},{5,23},{6,20},{7,21},{8,26},{9,... | collective-permute-start | bytes 208904 | tf_op jit(solution)/shard_map/ppermute | solution.py:277
  67.3 6.9 %collective-permute-start.37 = (f16[136,256]{1,0:T(8,128)(2,1)S(1)}, f16[136,256]{1,0:T(8,128)(2,1)S(1)}, u32[]{:S(2)}, u32[]{:S(2)}) collective-permute-start(f16[136,256]{1,0:T(8,128)(2,1)S(1)} %get-tuple-element.83), channel_id=1, source_target_pairs={{0,24},{1,25},{2,26},{3,27},{4,28},{5,29},{6,30},{7,31},{8,16},{9,... | collective-permute-start | bytes 208904 | tf_op jit(solution)/shard_map/ppermute | solution.py:277
  68.4 8.6 %collective-permute-start.38 = (f16[136,256]{1,0:T(8,128)(2,1)S(1)}, f16[136,256]{1,0:T(8,128)(2,1)S(1)}, u32[]{:S(2)}, u32[]{:S(2)}) collective-permute-start(f16[136,256]{1,0:T(8,128)(2,1)S(1)} %get-tuple-element.82), channel_id=1, source_target_pairs={{0,26},{1,27},{2,24},{3,25},{4,30},{5,31},{6,28},{7,29},{8,18},{9,... | collective-permute-start | bytes 208904 | tf_op jit(solution)/shard_map/ppermute | solution.py:277
  70.6 6.4 %collective-permute-start.32 = (f16[136,256]{1,0:T(8,128)(2,1)S(1)}, f16[136,256]{1,0:T(8,128)(2,1)S(1)}, u32[]{:S(2)}, u32[]{:S(2)}) collective-permute-start(f16[136,256]{1,0:T(8,128)(2,1)S(1)} %get-tuple-element.81), channel_id=1, source_target_pairs={{0,2},{1,3},{2,0},{3,1},{4,6},{5,7},{6,4},{7,5},{8,10},{9,11},{10,... | collective-permute-start | bytes 208904 | tf_op jit(solution)/shard_map/ppermute | solution.py:277
  72.9 6.0 %collective-permute-start.34 = (f16[136,256]{1,0:T(8,128)(2,1)S(1)}, f16[136,256]{1,0:T(8,128)(2,1)S(1)}, u32[]{:S(2)}, u32[]{:S(2)}) collective-permute-start(f16[136,256]{1,0:T(8,128)(2,1)S(1)} %get-tuple-element.86), channel_id=1, source_target_pairs={{0,10},{1,11},{2,8},{3,9},{4,14},{5,15},{6,12},{7,13},{8,2},{9,3},... | collective-permute-start | bytes 208904 | tf_op jit(solution)/shard_map/ppermute | solution.py:277
  (15 other events, 49.7 us)

commit v4 on v3

v4 whole, which is shorter than its diff:
```python
import functools
import math

import jax
import jax.numpy as jnp
import numpy as np
from jax import lax
from jax.experimental import pallas as pl
from jax.experimental.pallas import tpu as pltpu
from jax.sharding import PartitionSpec as P

EXTRA = 8
VMEM_BYTES = 16 * 2**20
ANY = pl.BlockSpec(memory_space=pl.ANY)
HBM = pl.BlockSpec(memory_space=pltpu.HBM)
VMEM = pl.BlockSpec(memory_space=pltpu.VMEM)
UNIT = 18 * 10**8
QUICK = pl.CostEstimate(flops=1, bytes_accessed=1, transcendentals=0)
PARAMS = pltpu.CompilerParams(vmem_limit_bytes=VMEM_BYTES)


def flip(cells, axis, bits):
    count = lax.axis_size(axis)
    return lax.ppermute(cells, axis, [(i, i ^ bits) for i in range(count)])


def after(value, *earlier):
    return lax.optimization_barrier((value, *earlier))[0]


def row_factors(nlat, fields, nlon):
    cosine = np.cos(np.deg2rad(45.0 + 0.5 * (np.arange(nlat) + 0.5 - nlat / 2.0)))
    total = fields * nlon * cosine.sum()
    return [float(value) for value in np.sqrt(cosine) * total ** (-0.25)]


def chosen(values, at):
    value = jnp.float32(values[0])
    for n in range(1, len(values)):
        value = jnp.where(at == n, jnp.float32(values[n]), value)
    return value


def smooth_kernel(part, layers, edges, factors, x_hbm, lon_hbm, lat_hbm, *rest):
    if edges:
        inside_hbm, outside_hbm, *rest = rest
    *out_refs, x_ref, lon_ref, lat_ref, inside_ref, outside_ref, sems = rest
    sources = [(lon_hbm, lon_ref), (lat_hbm, lat_ref), (x_hbm, x_ref)]
    if edges:
        sources += [(inside_hbm, inside_ref), (outside_hbm, outside_ref)]
    copies = [pltpu.make_async_copy(a, b, sems.at[n]) for n, (a, b) in enumerate(sources)]
    for copy in copies:
        copy.start()
    for copy in copies:
        copy.wait()
    rows, nlon, snaps = x_ref.shape[1:]
    layer, band = lax.axis_index("snap") // 2, lax.axis_index("space")
    upper = band % 2 == 0
    inner = x_ref.shape[0] * (rows - 2)
    for j in reversed(range(layers)):
        n = part * layers + (layer ^ j)
        field, row = n // (rows - 2), 1 + n % (rows - 2)
        if edges:
            m = n - inner
            field = jnp.where(m < 0, field, m // 2)
            row = jnp.where(m < 0, row, (rows - 1) * (m % 2))
        up = x_ref[field, jnp.maximum(row - 1, 0)].astype(jnp.float32)
        down = x_ref[field, jnp.minimum(row + 1, rows - 1)].astype(jnp.float32)
        if edges:
            inside = inside_ref[field].astype(jnp.float32)
            outside = outside_ref[field].astype(jnp.float32)
            up = jnp.where(row == 0, jnp.where(upper, outside, inside), up)
            down = jnp.where(row == rows - 1, jnp.where(upper, inside, outside), down)
        x = x_ref[field, row].astype(jnp.float32)
        lon = jnp.broadcast_to(lon_ref[field, pl.ds(row, 1), :], (snaps, nlon)).T
        lat = jnp.broadcast_to(lat_ref[field, pl.ds(row, 1), :], (snaps, nlon)).T
        lon_part = pltpu.roll(x, 1, 0) + pltpu.roll(x, nlon - 1, 0) - 2.0 * x
        lat_part = up + down - 2.0 * x
        smooth = x + lon * lon_part + lat * lat_part
        factor = chosen(factors, band * rows + row)
        out_refs[j][...] = (smooth * factor).astype(jnp.bfloat16)


def scaled_part(part, layers, factors, cells, lon_coeff, lat_coeff, halo):
    fields, rows, nlon, snaps = cells.shape
    edge = (fields, nlon, snaps)
    out_shape = [jax.ShapeDtypeStruct((nlon, snaps), jnp.bfloat16)] * layers
    in_place = [pltpu.with_memory_space_constraint(v, pltpu.HBM) for v in (cells, lon_coeff, lat_coeff)]
    return pl.pallas_call(
        functools.partial(smooth_kernel, part, layers, bool(halo), factors),
        out_shape=out_shape,
        in_specs=[HBM] * 3 + [ANY] * len(halo),
        out_specs=[VMEM] * len(out_shape),
        scratch_shapes=[
            pltpu.VMEM(cells.shape, cells.dtype),
            pltpu.VMEM(lon_coeff.shape, lon_coeff.dtype),
            pltpu.VMEM(lat_coeff.shape, lat_coeff.dtype),
            pltpu.VMEM(edge, cells.dtype),
            pltpu.VMEM(edge, cells.dtype),
            pltpu.SemaphoreType.DMA((5,)),
        ],
        compiler_params=PARAMS,
        cost_estimate=QUICK,
        name="smooth_rows",
    )(*in_place, *halo)


def edges_kernel(x_hbm, inside_ref, outside_ref, sems):
    rows = x_hbm.shape[1]
    upper = lax.axis_index("space") % 2 == 0
    copies = [
        pltpu.make_async_copy(x_hbm.at[:, jnp.where(upper, a, b)], out_ref, sems.at[n])
        for n, (a, b, out_ref) in enumerate(
            [(rows - 1, 0, inside_ref), (0, rows - 1, outside_ref)]
        )
    ]
    for copy in copies:
        copy.start()
    for copy in copies:
        copy.wait()


def edges_of(cells):
    fields, _, nlon, snaps = cells.shape
    edge = jax.ShapeDtypeStruct((fields, nlon, snaps), cells.dtype)
    return pl.pallas_call(
        edges_kernel,
        out_shape=[edge, edge],
        in_specs=[HBM],
        out_specs=[VMEM, VMEM],
        scratch_shapes=[pltpu.SemaphoreType.DMA((2,))],
        compiler_params=PARAMS,
        cost_estimate=QUICK,
        name="band_edges",
    )(pltpu.with_memory_space_constraint(cells, pltpu.HBM))


def join_kernel(*refs):
    *pieces, out_ref = refs
    depth = pieces[0].shape[0]
    for n, piece in enumerate(pieces):
        out_ref[n * depth : (n + 1) * depth] = piece[...]


def join(pieces, cost=0.0):
    depth, snaps = pieces[0].shape
    return pl.pallas_call(
        join_kernel,
        out_shape=jax.ShapeDtypeStruct((len(pieces) * depth, snaps), jnp.bfloat16),
        in_specs=[VMEM] * len(pieces),
        out_specs=VMEM,
        compiler_params=PARAMS,
        cost_estimate=pl.CostEstimate(
            flops=1 + int(cost * UNIT), bytes_accessed=1, transcendentals=0
        ),
        name="join_pieces",
    )(*pieces)


def turn_kernel(places, depth, *refs):
    *arrays, out_ref = refs
    snaps = arrays[0].shape[1]
    at = [lax.broadcasted_iota(jnp.int32, (snaps, snaps), axis) for axis in (0, 1)]
    one = jnp.where(at[0] == at[1], 1.0, 0.0).astype(jnp.bfloat16)
    for n, (array, row) in enumerate(places):
        for side in range(2):
            piece = arrays[2 * array + side][pl.ds(row, depth)]
            turned = lax.dot_general(
                one, piece, (((1,), (1,)), ((), ())), preferred_element_type=jnp.float32
            )
            out_ref[n, side] = turned.astype(jnp.bfloat16)


def turned(arrays, places, depth):
    snaps = arrays[0].shape[1]
    return pl.pallas_call(
        functools.partial(turn_kernel, places, depth),
        out_shape=jax.ShapeDtypeStruct((len(places), 2, snaps, depth), jnp.bfloat16),
        in_specs=[VMEM] * len(arrays),
        out_specs=VMEM,
        compiler_params=PARAMS,
        cost_estimate=QUICK,
        name="turn_pieces",
    )(*arrays)


def product_kernel(layers, columns, share, places, *refs):
    parts = len(places)
    lefts, refs = refs[:parts], refs[parts:]
    *arrays, own_ref, out_ref, right, sems = refs
    depth, snaps = right.shape[2], arrays[0].shape[1]
    me, band = lax.axis_index("snap"), lax.axis_index("space")
    picks = columns * share
    for t in range(parts):
        for c in range(picks):
            i, g = c // share, c % share
            wanted = ((band ^ (2 * i)) * share + g) ^ me
            for j, (array, row) in enumerate(places[t]):
                for y in range(2):

                    @pl.when(wanted == 2 * j + y)
                    def _():
                        for side in range(2):
                            pltpu.make_async_copy(
                                arrays[4 * array + 2 * y + side].at[pl.ds(row, depth)],
                                right.at[t, side, :, pl.ds(c * snaps, snaps)],
                                sems.at[t, c, side],
                            ).start()

    for t in range(parts):
        for c in range(picks):
            for side in range(2):
                pltpu.make_async_copy(
                    arrays[0].at[pl.ds(0, depth)],
                    right.at[t, side, :, pl.ds(c * snaps, snaps)],
                    sems.at[t, c, side],
                ).wait()
    blocks, wide = [], share * snaps
    for j in range(layers):
        product = sum(
            jnp.dot(lefts[t][j, side], right[t, side], preferred_element_type=jnp.float32)
            for t in range(parts)
            for side in range(2)
        )
        for i in range(columns):
            blocks.append(product[:, i * wide : (i + 1) * wide])
    own_ref[...] = blocks[0]
    largest = functools.reduce(jnp.maximum, [jnp.abs(block) for block in blocks[1:]])
    largest = jnp.maximum(jnp.max(largest, axis=(0, 1), keepdims=True), 1e-30)
    power = jnp.ceil(jnp.log2(largest)) - 15.0
    scale = jnp.exp2(-power)
    for n, block in enumerate(blocks[1:]):
        out_ref[n, :snaps] = block * scale
        out_ref[n, snaps:] = jnp.broadcast_to(power, (EXTRA, block.shape[1]))


def block_products(layers, columns, share, lefts, arrays, places):
    parts = len(lefts)
    snaps, depth = lefts[0].shape[2:]
    wide = snaps * share
    return pl.pallas_call(
        functools.partial(product_kernel, layers, columns, share, places),
        out_shape=[
            jax.ShapeDtypeStruct((snaps, wide), jnp.float32),
            jax.ShapeDtypeStruct((layers * columns - 1, snaps + EXTRA, wide), jnp.float32),
        ],
        in_specs=[VMEM] * parts + [ANY] * len(arrays),
        out_specs=[VMEM, VMEM],
        scratch_shapes=[
            pltpu.VMEM((parts, 2, depth, columns * wide), jnp.bfloat16),
            pltpu.SemaphoreType.DMA((parts, columns * share, 2)),
        ],
        compiler_params=PARAMS,
        cost_estimate=QUICK,
        name="block_products",
    )(*lefts, *arrays)


def shards(snapshots, lon_coeff, lat_coeff):
    snaps, fields, rows, nlon = snapshots.shape
    groups, bands = lax.axis_size("snap"), lax.axis_size("space")
    layers, columns, share = groups // 2, bands // 2, groups // bands
    parts = fields * rows // layers
    inner_parts = fields * (rows - 2) // layers

    factors = row_factors(bands * rows, fields, nlon)
    cells = jnp.transpose(snapshots, (1, 2, 3, 0))
    inside, outside = edges_of(cells)
    scaled = [
        scaled_part(t, layers, factors, cells, lon_coeff, lat_coeff, ())
        for t in range(inner_parts)
    ]
    steps = [(i, i + 1) for i in range(1, bands - 1, 2)]
    halo = (
        flip(inside, "space", 1),
        lax.ppermute(outside, "space", steps + [(i, j) for j, i in steps]),
    )
    count = layers // 2
    scaled += [
        scaled_part(t, layers, factors, cells, lon_coeff, lat_coeff, halo)
        for t in range(inner_parts, parts)
    ]

    spans = [[(t, 0) for t in range(parts)]]
    own = join([scaled[t][0] for t in range(parts)])
    own_other = flip(own, "snap", 1)
    held, other = [own], [own_other]
    for j in range(1, count):
        near = flip(join([scaled[t][j] for t in range(parts)]), "snap", 2 * j)
        held.append(near)
        other.append(join([flip(near, "snap", 1)], 2.5))
        spans.append([(t, j) for t in range(parts)])
    before = own_other
    for t in range(parts):
        last = t == parts - 1
        far = [flip(scaled[t][j], "snap", 2 * j) for j in range(count, layers)]
        far = join(far, 1.9 if last else 1.3)
        sent = flip(after(far, before), "snap", 1)
        held.append(far)
        other.append(join([sent], 3.0) if last else sent)
        spans.append([(t, j) for j in range(count, layers)])
        before = before if last else sent
    late = [held[-1], before]
    held_too = [flip(after(array, *late), "space", 1) for array in held]
    places, lefts = [], []
    for t in range(parts):
        at = [(n, span) for n, span in enumerate(spans) if (t, span[-1][1]) in span]
        where = [(n, span.index((t, j)) * nlon) for j in range(layers) for n, span in at if (t, j) in span]
        places.append(where)
        used = [n for n, _ in at]
        arrays = [array for n in used for array in (held[n], held_too[n])]
        lefts.append(turned(arrays, [(used.index(n), row) for n, row in where], nlon))
    other_too = [flip(after(array, *late), "space", 1) for array in other[:-1]]
    other_too.append(flip(after(other[-1], *lefts), "space", 1))
    arrays = [array for arrays in zip(held, held_too, other, other_too) for array in arrays]
    total, blocks = block_products(layers, columns, share, lefts, arrays, places)

    blocks = blocks.astype(jnp.float16)
    order = [(j, i) for j in range(layers) for i in range(columns) if i or j]
    for j, i in sorted(order, key=lambda at: ((at[0] + at[1]) % 2, -(at[0] or layers - 1.5))):
        pairs = [
            (s * bands + b, (s ^ (2 * j)) * bands + (b ^ (2 * i)))
            for s in range(groups)
            for b in range(bands)
        ]
        block = lax.ppermute(blocks[j * columns + i - 1], ("snap", "space"), pairs)
        block = block.astype(jnp.float32)
        total += block[:snaps] * jnp.exp2(block[snaps : snaps + 1])
    return total


def solution(mesh):
    return jax.shard_map(
        shards,
        mesh=mesh,
        in_specs=(P("snap", None, "space", None), P(None, "space", None), P(None, "space", None)),
        out_specs=P("snap", "space"),
        check_vma=False,
    )
```

time: 80.5 us -> 77.3 us (0.960)
  starting transfers between devices: 43.9 us -> 36.9 us
  waiting for transfers between devices: 25.3 us -> 27.9 us
  Pallas kernels: 9.72 us -> 10.9 us
    ppermute x7, waiting for transfers between devices: 2.8 us -> 5.9 us  [shards(): block = lax.ppermute(blocks[j * columns + i - 1], ('snap', 'space'), pairs)]
    ppermute x2 -> x1, starting transfers between devices: 3.67 us -> 0.67 us  [shards(): lax.ppermute(outside, 'space', steps + [(i, j) for j, i in steps])]
    ppermute x30 -> x18, starting transfers between devices: 26.1 us -> 23.7 us  [flip(): return lax.ppermute(cells, axis, [(i, i ^ bits) for i in range(count)])]
    ppermute x7, starting transfers between devices: 14.1 us -> 12.6 us  [shards(): block = lax.ppermute(blocks[j * columns + i - 1], ('snap', 'space'), pairs)]
    pallas_call x6 -> x12, Pallas kernels: 9.72 us -> 10.9 us  [the longest x2 5.16 us: scaled_part(): pl.pallas_call(functools.partial(smooth_kernel, part, layers, bool(halo),...]
    ppermute x30 -> x18, waiting for transfers between devices: 22.5 us -> 22 us  [flip(): return lax.ppermute(cells, axis, [(i, i ^ bits) for i in range(count)])]
  transfers between devices with their start and end apart: 39 -> 26, of which waited for: 9 -> 10; matrix products, arithmetic and copies ran while one was open for 0% -> 0% of each run, Pallas kernels for 7% -> 9%
where the time goes in v4:
time: 77.3 us; the launch traced here: 77.1 us
  starting transfers between devices  36.9 us (48%)
  waiting for transfers between devices  27.9 us (36%)
  Pallas kernels  10.9 us (14%)
  other arithmetic  0.96 us (1%)
    ppermute x18, starting transfers between devices, flip(): return lax.ppermute(cells, axis, [(i, i ^ bits) for i in range(count)])  23.7 us
    ppermute x18, waiting for transfers between devices, flip(): return lax.ppermute(cells, axis, [(i, i ^ bits) for i in range(count)])  22 us
    ppermute x7, starting transfers between devices, shards(): block = lax.ppermute(blocks[j * columns + i - 1], ('snap', 'space'), pairs)  12.6 us
    ppermute x7, waiting for transfers between devices, shards(): block = lax.ppermute(blocks[j * columns + i - 1], ('snap', 'space'), pairs)  5.9 us
    pallas_call x2, Pallas kernels, scaled_part(): pl.pallas_call(functools.partial(smooth_kernel, part, layers, bool(halo),...  5.16 us
    pallas_call x1, Pallas kernels, block_products(): pl.pallas_call(functools.partial(product_kernel, layers, columns, share,...  3.13 us
  transfers between devices with their start and end apart: 26, of which 10 were waited for; matrix products, arithmetic and copies ran while one was open for 0% of the time, Pallas kernels for 9%

profile of v4, /device:TPU:0, one launch (start us, length us, event | category | flops | bytes accessed | tf_op | source)
XLA Modules:
  0.0 77.1 jit_solution(12173449725296263376)
XLA Ops:
  0.0 1.1 %band_edges.1 = (bf16[2,720,128]{2,1,0:T(8,128)(2,1)S(1)}, bf16[2,720,128]{2,1,0:T(8,128)(2,1)S(1)}) custom-call(bf16[2,4,720,128]{3,2,1,0:T(8,128)(2,1)} %bitcast.22), custom_call_target="tpu_custom_call" | custom-call | flops 1 | bytes 1 | tf_op jit(solution)/shard_map/band_edges/pallas_call | solution.py:126
  2.3 2.5 %smooth_rows.2 = (bf16[720,128]{1,0:T(8,128)(2,1)S(1)}, bf16[720,128]{1,0:T(8,128)(2,1)S(1)}, bf16[720,128]{1,0:T(8,128)(2,1)S(1)}, bf16[720,128]{1,0:T(8,128)(2,1)S(1)}) custom-call(bf16[2,4,720,128]{3,2,1,0:T(8,128)(2,1)} %bitcast.23, f32[2,4,720]{2,1,0:T(4,128)} %lon_hbm.3, f32[2,4,720]{2,1,0:T(4,128)} %lat_hbm.3), custom_call_target="tpu_custom_call" | custom-call | flops 1 | bytes 1 | tf_op jit(solution)/shard_map/smooth_rows/pallas_call | solution.py:89
  4.8 3.7 %collective-permute-start.4 = (bf16[720,128]{1,0:T(8,128)(2,1)S(1)}, bf16[720,128]{1,0:T(8,128)(2,1)S(1)}, u32[]{:S(2)}, u32[]{:S(2)}) collective-permute-start(bf16[720,128]{1,0:T(8,128)(2,1)S(1)} %get-tuple-element.33), channel_id=1, source_target_pairs={{0,16},{4,20},{8,24},{12,28},{16,0},{20,4},{24,8},{28,12},{1,17},{... | collective-permute-start | bytes 552968 | tf_op jit(solution)/shard_map/ppermute | solution.py:24
  8.5 1.3 %collective-permute-start.5 = (bf16[720,128]{1,0:T(8,128)(2,1)S(1)}, bf16[720,128]{1,0:T(8,128)(2,1)S(1)}, u32[]{:S(2)}, u32[]{:S(2)}) collective-permute-start(bf16[720,128]{1,0:T(8,128)(2,1)S(1)} %get-tuple-element.34), channel_id=1, source_target_pairs={{0,24},{4,28},{8,16},{12,20},{16,8},{20,12},{24,0},{28,4},{1,25},{... | collective-permute-start | bytes 552968 | tf_op jit(solution)/shard_map/ppermute | solution.py:24
  9.8 2.7 %smooth_rows.3 = (bf16[720,128]{1,0:T(8,128)(2,1)S(1)}, bf16[720,128]{1,0:T(8,128)(2,1)S(1)}, bf16[720,128]{1,0:T(8,128)(2,1)S(1)}, bf16[720,128]{1,0:T(8,128)(2,1)S(1)}) custom-call(bf16[2,4,720,128]{3,2,1,0:T(8,128)(2,1)} %bitcast.24, f32[2,4,720]{2,1,0:T(4,128)} %lon_hbm.3, f32[2,4,720]{2,1,0:T(4,128)} %lat_hbm.3, ...), custom_call_target="tpu_custom_call" | custom-call | flops 1 | bytes 1 | tf_op jit(solution)/shard_map/smooth_rows/pallas_call | solution.py:89
  12.6 1.6 %collective-permute-start.6 = (bf16[1440,128]{1,0:T(8,128)(2,1)S(1)}, bf16[1440,128]{1,0:T(8,128)(2,1)S(1)}, u32[]{:S(2)}, u32[]{:S(2)}) collective-permute-start(bf16[1440,128]{1,0:T(8,128)(2,1)S(1)} %join_pieces.6.refs_0_.refs_2_), channel_id=1, source_target_pairs={{0,4},{4,0},{8,12},{12,8},{16,20},{20,16},{24,28},{28,24},{1,5},{5... | collective-permute-start | bytes 1105928 | tf_op jit(solution)/shard_map/ppermute | solution.py:24
  14.5 2.8 %collective-permute-start.2 = (bf16[720,128]{1,0:T(8,128)(2,1)S(1)}, bf16[720,128]{1,0:T(8,128)(2,1)S(1)}, u32[]{:S(2)}, u32[]{:S(2)}) collective-permute-start(bf16[720,128]{1,0:T(8,128)(2,1)S(1)} %get-tuple-element.31), channel_id=1, source_target_pairs={{0,16},{4,20},{8,24},{12,28},{16,0},{20,4},{24,8},{28,12},{1,17},{... | collective-permute-start | bytes 552968 | tf_op jit(solution)/shard_map/ppermute | solution.py:24
  17.3 3.2 %collective-permute-done.4.refs_0_ = bf16[720,128]{1,0:T(8,128)(2,1)S(1)} collective-permute-done((bf16[720,128]{1,0:T(8,128)(2,1)S(1)}, bf16[720,128]{1,0:T(8,128)(2,1)S(1)}, u32[]{:S(2)}, u32[]{:S(2)}) %collective-permute-start.4) | collective-permute-done | bytes 184352 | tf_op jit(solution)/shard_map/ppermute | solution.py:24
  20.4 5.2 %collective-permute-start.3 = (bf16[720,128]{1,0:T(8,128)(2,1)S(1)}, bf16[720,128]{1,0:T(8,128)(2,1)S(1)}, u32[]{:S(2)}, u32[]{:S(2)}) collective-permute-start(bf16[720,128]{1,0:T(8,128)(2,1)S(1)} %get-tuple-element.32), channel_id=1, source_target_pairs={{0,24},{4,28},{8,16},{12,20},{16,8},{20,12},{24,0},{28,4},{1,25},{... | collective-permute-start | bytes 552968 | tf_op jit(solution)/shard_map/ppermute | solution.py:24
  25.7 1.6 %collective-permute-start.7 = (bf16[1440,128]{1,0:T(8,128)(2,1)S(1)}, bf16[1440,128]{1,0:T(8,128)(2,1)S(1)}, u32[]{:S(2)}, u32[]{:S(2)}) collective-permute-start(bf16[1440,128]{1,0:T(8,128)(2,1)S(1)} %join_pieces.8.refs_4_.refs_10_), channel_id=1, source_target_pairs={{0,4},{4,0},{8,12},{12,8},{16,20},{20,16},{24,28},{28,24},{1,5},{5... | collective-permute-start | bytes 1105928 | tf_op jit(solution)/shard_map/ppermute | solution.py:24
  27.3 5.5 %collective-permute-done.9.refs_2_.refs_6_ = bf16[1440,128]{1,0:T(8,128)(2,1)S(1)} collective-permute-done((bf16[1440,128]{1,0:T(8,128)(2,1)S(1)}, bf16[1440,128]{1,0:T(8,128)(2,1)S(1)}, u32[]{:S(2)}, u32[]{:S(2)}) %collective-permute-start.9) | collective-permute-done | bytes 368672 | tf_op jit(solution)/shard_map/ppermute | solution.py:24
  33.5 2.7 %collective-permute-done.2.refs_0_ = bf16[720,128]{1,0:T(8,128)(2,1)S(1)} collective-permute-done((bf16[720,128]{1,0:T(8,128)(2,1)S(1)}, bf16[720,128]{1,0:T(8,128)(2,1)S(1)}, u32[]{:S(2)}, u32[]{:S(2)}) %collective-permute-start.2) | collective-permute-done | bytes 184352 | tf_op jit(solution)/shard_map/ppermute | solution.py:24
  36.3 2.8 %collective-permute-start.8 = (bf16[1440,128]{1,0:T(8,128)(2,1)S(1)}, bf16[1440,128]{1,0:T(8,128)(2,1)S(1)}, u32[]{:S(2)}, u32[]{:S(2)}) collective-permute-start(bf16[1440,128]{1,0:T(8,128)(2,1)S(1)} %join_pieces.6.refs_0_.refs_2_), channel_id=1, source_target_pairs={{0,1},{1,0},{2,3},{3,2},{4,5},{5,4},{6,7},{7,6},{8,9},{9,8},{10,11... | collective-permute-start | bytes 1105928 | tf_op jit(solution)/shard_map/ppermute | solution.py:24
  39.6 1.5 %collective-permute-start.17 = (bf16[1440,128]{1,0:T(8,128)(2,1)S(1)}, bf16[1440,128]{1,0:T(8,128)(2,1)S(1)}, u32[]{:S(2)}, u32[]{:S(2)}) collective-permute-start(bf16[1440,128]{1,0:T(8,128)(2,1)S(1)} %join_pieces.7.refs_4_.refs_14_), channel_id=1, source_target_pairs={{0,4},{4,0},{8,12},{12,8},{16,20},{20,16},{24,28},{28,24},{1,5},{5... | collective-permute-start | bytes 1105928 | tf_op jit(solution)/shard_map/ppermute | solution.py:24
  41.2 3.1 %collective-permute-done.14.refs_0_ = bf16[1440,128]{1,0:T(8,128)(2,1)S(1)} collective-permute-done((bf16[1440,128]{1,0:T(8,128)(2,1)S(1)}, bf16[1440,128]{1,0:T(8,128)(2,1)S(1)}, u32[]{:S(2)}, u32[]{:S(2)}) %collective-permute-start.14) | collective-permute-done | bytes 368672 | tf_op jit(solution)/shard_map/ppermute | solution.py:24
  46.1 5.8 %collective-permute-done.17.refs_0_ = bf16[1440,128]{1,0:T(8,128)(2,1)S(1)} collective-permute-done((bf16[1440,128]{1,0:T(8,128)(2,1)S(1)}, bf16[1440,128]{1,0:T(8,128)(2,1)S(1)}, u32[]{:S(2)}, u32[]{:S(2)}) %collective-permute-start.17) | collective-permute-done | bytes 368672 | tf_op jit(solution)/shard_map/ppermute | solution.py:24
  52.7 1.6 %collective-permute-done.18.refs_17_ = bf16[1440,128]{1,0:T(8,128)(2,1)S(1)} collective-permute-done((bf16[1440,128]{1,0:T(8,128)(2,1)S(1)}, bf16[1440,128]{1,0:T(8,128)(2,1)S(1)}, u32[]{:S(2)}, u32[]{:S(2)}) %collective-permute-start.18) | collective-permute-done | bytes 368672 | tf_op jit(solution)/shard_map/ppermute | solution.py:24
  54.3 3.1 %block_products.1 = (f32[128,256]{1,0:T(8,128)S(1)}, f32[7,136,256]{2,1,0:T(8,128)S(1)}) custom-call(bf16[4,2,128,720]{3,2,1,0:T(8,128)(2,1)S(1)} %turn_pieces.2.refs_0_, bf16[4,2,128,720]{3,2,1,0:T(8,128)(2,1)S(1)} %turn_pieces.3.refs_1_, bf16[1440,128]{1,0:T(8,128)(2,1)S(1)} %join_pieces.6.refs_0_.refs_2_, ...), custom_call_target="tpu_custom_call" | custom-call | flops 1 | bytes 1 | tf_op jit(solution)/shard_map/block_products/pallas_call | solution.py:241
  57.7 1.9 %collective-permute-start.19 = (f16[136,256]{1,0:T(8,128)(2,1)S(1)}, f16[136,256]{1,0:T(8,128)(2,1)S(1)}, u32[]{:S(2)}, u32[]{:S(2)}) collective-permute-start(f16[136,256]{1,0:T(8,128)(2,1)S(1)} %get-tuple-element.49), channel_id=1, source_target_pairs={{0,26},{1,27},{2,24},{3,25},{4,30},{5,31},{6,28},{7,29},{8,18},{9,... | collective-permute-start | bytes 208904 | tf_op jit(solution)/shard_map/ppermute | solution.py:326
  59.6 4.8 %collective-permute-start.25 = (f16[136,256]{1,0:T(8,128)(2,1)S(1)}, f16[136,256]{1,0:T(8,128)(2,1)S(1)}, u32[]{:S(2)}, u32[]{:S(2)}) collective-permute-start(f16[136,256]{1,0:T(8,128)(2,1)S(1)} %get-tuple-element.50), channel_id=1, source_target_pairs={{0,8},{1,9},{2,10},{3,11},{4,12},{5,13},{6,14},{7,15},{8,0},{9,1},... | collective-permute-start | bytes 208904 | tf_op jit(solution)/shard_map/ppermute | solution.py:326
  65.2 3.0 %collective-permute-start.22 = (f16[136,256]{1,0:T(8,128)(2,1)S(1)}, f16[136,256]{1,0:T(8,128)(2,1)S(1)}, u32[]{:S(2)}, u32[]{:S(2)}) collective-permute-start(f16[136,256]{1,0:T(8,128)(2,1)S(1)} %get-tuple-element.53), channel_id=1, source_target_pairs={{0,24},{1,25},{2,26},{3,27},{4,28},{5,29},{6,30},{7,31},{8,16},{9,... | collective-permute-start | bytes 208904 | tf_op jit(solution)/shard_map/ppermute | solution.py:326
  68.2 1.4 %collective-permute-start.21 = (f16[136,256]{1,0:T(8,128)(2,1)S(1)}, f16[136,256]{1,0:T(8,128)(2,1)S(1)}, u32[]{:S(2)}, u32[]{:S(2)}) collective-permute-start(f16[136,256]{1,0:T(8,128)(2,1)S(1)} %get-tuple-element.54), channel_id=1, source_target_pairs={{0,10},{1,11},{2,8},{3,9},{4,14},{5,15},{6,12},{7,13},{8,2},{9,3},... | collective-permute-start | bytes 208904 | tf_op jit(solution)/shard_map/ppermute | solution.py:326
  70.3 2.7 %collective-permute-done.24 = f16[136,256]{1,0:T(8,128)(2,1)S(1)} collective-permute-done((f16[136,256]{1,0:T(8,128)(2,1)S(1)}, f16[136,256]{1,0:T(8,128)(2,1)S(1)}, u32[]{:S(2)}, u32[]{:S(2)}) %collective-permute-start.24) | collective-permute-done | bytes 69664 | tf_op jit(solution)/shard_map/ppermute | solution.py:326
  74.0 2.4 %collective-permute-done.20 = f16[136,256]{1,0:T(8,128)(2,1)S(1)} collective-permute-done((f16[136,256]{1,0:T(8,128)(2,1)S(1)}, f16[136,256]{1,0:T(8,128)(2,1)S(1)}, u32[]{:S(2)}, u32[]{:S(2)}) %collective-permute-start.20) | collective-permute-done | bytes 69664 | tf_op jit(solution)/shard_map/ppermute | solution.py:326
  (57 shorter events, 8.9 us)
Async XLA Ops:
  1.1 8.7 %collective-permute-start = (bf16[2,720,128]{2,1,0:T(8,128)(2,1)S(1)}, bf16[2,720,128]{2,1,0:T(8,128)(2,1)S(1)}, u32[]{:S(2)}, u32[]{:S(2)}) collective-permute-start(bf16[2,720,128]{2,1,0:T(8,128)(2,1)S(1)} %get-tuple-element.28), channel_id=1, source_target_pairs={{0,1},{1,0},{2,3},{3,2},{4,5},{5,4},{6,7},{7,6},{8,9},{9,8},{10,11... | collective-permute-start | bytes 1105928 | tf_op jit(solution)/shard_map/ppermute | solution.py:24
  1.6 8.2 %collective-permute-start.1 = (bf16[2,720,128]{2,1,0:T(8,128)(2,1)S(1)}, bf16[2,720,128]{2,1,0:T(8,128)(2,1)S(1)}, u32[]{:S(2)}, u32[]{:S(2)}) collective-permute-start(bf16[2,720,128]{2,1,0:T(8,128)(2,1)S(1)} %get-tuple-element.29), channel_id=1, source_target_pairs={{1,2},{2,1},{5,6},{6,5},{9,10},{10,9},{13,14},{14,13},{17,18},{18,... | collective-permute-start | bytes 1105928 | tf_op jit(solution)/shard_map/ppermute | solution.py:276
  4.8 15.7 %collective-permute-start.4 = (bf16[720,128]{1,0:T(8,128)(2,1)S(1)}, bf16[720,128]{1,0:T(8,128)(2,1)S(1)}, u32[]{:S(2)}, u32[]{:S(2)}) collective-permute-start(bf16[720,128]{1,0:T(8,128)(2,1)S(1)} %get-tuple-element.33), channel_id=1, source_target_pairs={{0,16},{4,20},{8,24},{12,28},{16,0},{20,4},{24,8},{28,12},{1,17},{... | collective-permute-start | bytes 552968 | tf_op jit(solution)/shard_map/ppermute | solution.py:24
  8.5 17.2 %collective-permute-start.5 = (bf16[720,128]{1,0:T(8,128)(2,1)S(1)}, bf16[720,128]{1,0:T(8,128)(2,1)S(1)}, u32[]{:S(2)}, u32[]{:S(2)}) collective-permute-start(bf16[720,128]{1,0:T(8,128)(2,1)S(1)} %get-tuple-element.34), channel_id=1, source_target_pairs={{0,24},{4,28},{8,16},{12,20},{16,8},{20,12},{24,0},{28,4},{1,25},{... | collective-permute-start | bytes 552968 | tf_op jit(solution)/shard_map/ppermute | solution.py:24
  12.6 13.1 %collective-permute-start.6 = (bf16[1440,128]{1,0:T(8,128)(2,1)S(1)}, bf16[1440,128]{1,0:T(8,128)(2,1)S(1)}, u32[]{:S(2)}, u32[]{:S(2)}) collective-permute-start(bf16[1440,128]{1,0:T(8,128)(2,1)S(1)} %join_pieces.6.refs_0_.refs_2_), channel_id=1, source_target_pairs={{0,4},{4,0},{8,12},{12,8},{16,20},{20,16},{24,28},{28,24},{1,5},{5... | collective-permute-start | bytes 1105928 | tf_op jit(solution)/shard_map/ppermute | solution.py:24
  14.2 18.6 %collective-permute-start.9 = (bf16[1440,128]{1,0:T(8,128)(2,1)S(1)}, bf16[1440,128]{1,0:T(8,128)(2,1)S(1)}, u32[]{:S(2)}, u32[]{:S(2)}) collective-permute-start(bf16[1440,128]{1,0:T(8,128)(2,1)S(1)} %join_pieces.9), channel_id=1, source_target_pairs={{0,8},{4,12},{8,0},{12,4},{16,24},{20,28},{24,16},{28,20},{1,9},{5... | collective-permute-start | bytes 1105928 | tf_op jit(solution)/shard_map/ppermute | solution.py:24
  14.5 21.7 %collective-permute-start.2 = (bf16[720,128]{1,0:T(8,128)(2,1)S(1)}, bf16[720,128]{1,0:T(8,128)(2,1)S(1)}, u32[]{:S(2)}, u32[]{:S(2)}) collective-permute-start(bf16[720,128]{1,0:T(8,128)(2,1)S(1)} %get-tuple-element.31), channel_id=1, source_target_pairs={{0,16},{4,20},{8,24},{12,28},{16,0},{20,4},{24,8},{28,12},{1,17},{... | collective-permute-start | bytes 552968 | tf_op jit(solution)/shard_map/ppermute | solution.py:24
  20.4 15.7 %collective-permute-start.3 = (bf16[720,128]{1,0:T(8,128)(2,1)S(1)}, bf16[720,128]{1,0:T(8,128)(2,1)S(1)}, u32[]{:S(2)}, u32[]{:S(2)}) collective-permute-start(bf16[720,128]{1,0:T(8,128)(2,1)S(1)} %get-tuple-element.32), channel_id=1, source_target_pairs={{0,24},{4,28},{8,16},{12,20},{16,8},{20,12},{24,0},{28,4},{1,25},{... | collective-permute-start | bytes 552968 | tf_op jit(solution)/shard_map/ppermute | solution.py:24
  25.7 10.6 %collective-permute-start.7 = (bf16[1440,128]{1,0:T(8,128)(2,1)S(1)}, bf16[1440,128]{1,0:T(8,128)(2,1)S(1)}, u32[]{:S(2)}, u32[]{:S(2)}) collective-permute-start(bf16[1440,128]{1,0:T(8,128)(2,1)S(1)} %join_pieces.8.refs_4_.refs_10_), channel_id=1, source_target_pairs={{0,4},{4,0},{8,12},{12,8},{16,20},{20,16},{24,28},{28,24},{1,5},{5... | collective-permute-start | bytes 1105928 | tf_op jit(solution)/shard_map/ppermute | solution.py:24
  32.8 11.5 %collective-permute-start.14 = (bf16[1440,128]{1,0:T(8,128)(2,1)S(1)}, bf16[1440,128]{1,0:T(8,128)(2,1)S(1)}, u32[]{:S(2)}, u32[]{:S(2)}) collective-permute-start(bf16[1440,128]{1,0:T(8,128)(2,1)S(1)} %collective-permute-done.9.refs_2_.refs_6_), channel_id=1, source_target_pairs={{0,4},{4,0},{8,12},{12,8},{16,20},{20,16},{24,28},{28,24},{1,5},{5... | collective-permute-start | bytes 1105928 | tf_op jit(solution)/shard_map/ppermute | solution.py:24
  36.3 8.1 %collective-permute-start.8 = (bf16[1440,128]{1,0:T(8,128)(2,1)S(1)}, bf16[1440,128]{1,0:T(8,128)(2,1)S(1)}, u32[]{:S(2)}, u32[]{:S(2)}) collective-permute-start(bf16[1440,128]{1,0:T(8,128)(2,1)S(1)} %join_pieces.6.refs_0_.refs_2_), channel_id=1, source_target_pairs={{0,1},{1,0},{2,3},{3,2},{4,5},{5,4},{6,7},{7,6},{8,9},{9,8},{10,11... | collective-permute-start | bytes 1105928 | tf_op jit(solution)/shard_map/ppermute | solution.py:24
  39.2 5.8 %collective-permute-start.12 = (bf16[1440,128]{1,0:T(8,128)(2,1)S(1)}, bf16[1440,128]{1,0:T(8,128)(2,1)S(1)}, u32[]{:S(2)}, u32[]{:S(2)}) collective-permute-start(bf16[1440,128]{1,0:T(8,128)(2,1)S(1)} %join_pieces.7.refs_4_.refs_14_), channel_id=1, source_target_pairs={{0,1},{1,0},{2,3},{3,2},{4,5},{5,4},{6,7},{7,6},{8,9},{9,8},{10,11... | collective-permute-start | bytes 1105928 | tf_op jit(solution)/shard_map/ppermute | solution.py:24
  39.6 12.2 %collective-permute-start.17 = (bf16[1440,128]{1,0:T(8,128)(2,1)S(1)}, bf16[1440,128]{1,0:T(8,128)(2,1)S(1)}, u32[]{:S(2)}, u32[]{:S(2)}) collective-permute-start(bf16[1440,128]{1,0:T(8,128)(2,1)S(1)} %join_pieces.7.refs_4_.refs_14_), channel_id=1, source_target_pairs={{0,4},{4,0},{8,12},{12,8},{16,20},{20,16},{24,28},{28,24},{1,5},{5... | collective-permute-start | bytes 1105928 | tf_op jit(solution)/shard_map/ppermute | solution.py:24
  44.3 7.6 %collective-permute-start.11 = (bf16[1440,128]{1,0:T(8,128)(2,1)S(1)}, bf16[1440,128]{1,0:T(8,128)(2,1)S(1)}, u32[]{:S(2)}, u32[]{:S(2)}) collective-permute-start(bf16[1440,128]{1,0:T(8,128)(2,1)S(1)} %join_pieces.8.refs_4_.refs_10_), channel_id=1, source_target_pairs={{0,1},{1,0},{2,3},{3,2},{4,5},{5,4},{6,7},{7,6},{8,9},{9,8},{10,11... | collective-permute-start | bytes 1105928 | tf_op jit(solution)/shard_map/ppermute | solution.py:24
  44.4 8.3 %collective-permute-start.13 = (bf16[1440,128]{1,0:T(8,128)(2,1)S(1)}, bf16[1440,128]{1,0:T(8,128)(2,1)S(1)}, u32[]{:S(2)}, u32[]{:S(2)}) collective-permute-start(bf16[1440,128]{1,0:T(8,128)(2,1)S(1)} %collective-permute-done.6.refs_4_), channel_id=1, source_target_pairs={{0,1},{1,0},{2,3},{3,2},{4,5},{5,4},{6,7},{7,6},{8,9},{9,8},{10,11... | collective-permute-start | bytes 1105928 | tf_op jit(solution)/shard_map/ppermute | solution.py:24
  44.9 7.8 %collective-permute-start.15 = (bf16[1440,128]{1,0:T(8,128)(2,1)S(1)}, bf16[1440,128]{1,0:T(8,128)(2,1)S(1)}, u32[]{:S(2)}, u32[]{:S(2)}) collective-permute-start(bf16[1440,128]{1,0:T(8,128)(2,1)S(1)} %join_pieces.10.refs_8_), channel_id=1, source_target_pairs={{0,1},{1,0},{2,3},{3,2},{4,5},{5,4},{6,7},{7,6},{8,9},{9,8},{10,11... | collective-permute-start | bytes 1105928 | tf_op jit(solution)/shard_map/ppermute | solution.py:24
  45.0 7.7 %collective-permute-start.16 = (bf16[1440,128]{1,0:T(8,128)(2,1)S(1)}, bf16[1440,128]{1,0:T(8,128)(2,1)S(1)}, u32[]{:S(2)}, u32[]{:S(2)}) collective-permute-start(bf16[1440,128]{1,0:T(8,128)(2,1)S(1)} %collective-permute-done.7.refs_12_), channel_id=1, source_target_pairs={{0,1},{1,0},{2,3},{3,2},{4,5},{5,4},{6,7},{7,6},{8,9},{9,8},{10,11... | collective-permute-start | bytes 1105928 | tf_op jit(solution)/shard_map/ppermute | solution.py:24
  57.7 10.5 %collective-permute-start.19 = (f16[136,256]{1,0:T(8,128)(2,1)S(1)}, f16[136,256]{1,0:T(8,128)(2,1)S(1)}, u32[]{:S(2)}, u32[]{:S(2)}) collective-permute-start(f16[136,256]{1,0:T(8,128)(2,1)S(1)} %get-tuple-element.49), channel_id=1, source_target_pairs={{0,26},{1,27},{2,24},{3,25},{4,30},{5,31},{6,28},{7,29},{8,18},{9,... | collective-permute-start | bytes 208904 | tf_op jit(solution)/shard_map/ppermute | solution.py:326
  59.6 10.1 %collective-permute-start.25 = (f16[136,256]{1,0:T(8,128)(2,1)S(1)}, f16[136,256]{1,0:T(8,128)(2,1)S(1)}, u32[]{:S(2)}, u32[]{:S(2)}) collective-permute-start(f16[136,256]{1,0:T(8,128)(2,1)S(1)} %get-tuple-element.50), channel_id=1, source_target_pairs={{0,8},{1,9},{2,10},{3,11},{4,12},{5,13},{6,14},{7,15},{8,0},{9,1},... | collective-permute-start | bytes 208904 | tf_op jit(solution)/shard_map/ppermute | solution.py:326
  64.3 8.6 %collective-permute-start.24 = (f16[136,256]{1,0:T(8,128)(2,1)S(1)}, f16[136,256]{1,0:T(8,128)(2,1)S(1)}, u32[]{:S(2)}, u32[]{:S(2)}) collective-permute-start(f16[136,256]{1,0:T(8,128)(2,1)S(1)} %get-tuple-element.51), channel_id=1, source_target_pairs={{0,18},{1,19},{2,16},{3,17},{4,22},{5,23},{6,20},{7,21},{8,26},{9,... | collective-permute-start | bytes 208904 | tf_op jit(solution)/shard_map/ppermute | solution.py:326
  64.3 8.7 %collective-permute-start.23 = (f16[136,256]{1,0:T(8,128)(2,1)S(1)}, f16[136,256]{1,0:T(8,128)(2,1)S(1)}, u32[]{:S(2)}, u32[]{:S(2)}) collective-permute-start(f16[136,256]{1,0:T(8,128)(2,1)S(1)} %get-tuple-element.52), channel_id=1, source_target_pairs={{0,2},{1,3},{2,0},{3,1},{4,6},{5,7},{6,4},{7,5},{8,10},{9,11},{10,... | collective-permute-start | bytes 208904 | tf_op jit(solution)/shard_map/ppermute | solution.py:326
  65.2 7.9 %collective-permute-start.22 = (f16[136,256]{1,0:T(8,128)(2,1)S(1)}, f16[136,256]{1,0:T(8,128)(2,1)S(1)}, u32[]{:S(2)}, u32[]{:S(2)}) collective-permute-start(f16[136,256]{1,0:T(8,128)(2,1)S(1)} %get-tuple-element.53), channel_id=1, source_target_pairs={{0,24},{1,25},{2,26},{3,27},{4,28},{5,29},{6,30},{7,31},{8,16},{9,... | collective-permute-start | bytes 208904 | tf_op jit(solution)/shard_map/ppermute | solution.py:326
  68.2 5.8 %collective-permute-start.21 = (f16[136,256]{1,0:T(8,128)(2,1)S(1)}, f16[136,256]{1,0:T(8,128)(2,1)S(1)}, u32[]{:S(2)}, u32[]{:S(2)}) collective-permute-start(f16[136,256]{1,0:T(8,128)(2,1)S(1)} %get-tuple-element.54), channel_id=1, source_target_pairs={{0,10},{1,11},{2,8},{3,9},{4,14},{5,15},{6,12},{7,13},{8,2},{9,3},... | collective-permute-start | bytes 208904 | tf_op jit(solution)/shard_map/ppermute | solution.py:326
  69.6 6.7 %collective-permute-start.20 = (f16[136,256]{1,0:T(8,128)(2,1)S(1)}, f16[136,256]{1,0:T(8,128)(2,1)S(1)}, u32[]{:S(2)}, u32[]{:S(2)}) collective-permute-start(f16[136,256]{1,0:T(8,128)(2,1)S(1)} %get-tuple-element.55), channel_id=1, source_target_pairs={{0,16},{1,17},{2,18},{3,19},{4,20},{5,21},{6,22},{7,23},{8,24},{9,... | collective-permute-start | bytes 208904 | tf_op jit(solution)/shard_map/ppermute | solution.py:326
  (2 other events, 7.5 us)

commit v5 on v4

--- a/solution.py
+++ b/solution.py
@@ -14,6 +14,7 @@
 ANY = pl.BlockSpec(memory_space=pl.ANY)
 HBM = pl.BlockSpec(memory_space=pltpu.HBM)
 VMEM = pl.BlockSpec(memory_space=pltpu.VMEM)
+FAR, FAR_LAST, NEAR_OTHER, FAR_OTHER, FAR_LAST_OTHER = 1.1, 2.2, 4.0, 0.5, 3.0
 UNIT = 18 * 10**8
 QUICK = pl.CostEstimate(flops=1, bytes_accessed=1, transcendentals=0)
 PARAMS = pltpu.CompilerParams(vmem_limit_bytes=VMEM_BYTES)
@@ -187,7 +188,7 @@
 def product_kernel(layers, columns, share, places, *refs):
     parts = len(places)
     lefts, refs = refs[:parts], refs[parts:]
-    *arrays, own_ref, out_ref, right, sems = refs
+    *arrays, own_ref, out_ref, right = refs
     depth, snaps = right.shape[2], arrays[0].shape[1]
     me, band = lax.axis_index("snap"), lax.axis_index("space")
     picks = columns * share
@@ -201,29 +202,24 @@
                     @pl.when(wanted == 2 * j + y)
                     def _():
                         for side in range(2):
-                            pltpu.make_async_copy(
-                                arrays[4 * array + 2 * y + side].at[pl.ds(row, depth)],
-                                right.at[t, side, :, pl.ds(c * snaps, snaps)],
-                                sems.at[t, c, side],
-                            ).start()
-
-    for t in range(parts):
-        for c in range(picks):
-            for side in range(2):
-                pltpu.make_async_copy(
-                    arrays[0].at[pl.ds(0, depth)],
-                    right.at[t, side, :, pl.ds(c * snaps, snaps)],
-                    sems.at[t, c, side],
-                ).wait()
-    blocks, wide = [], share * snaps
-    for j in range(layers):
-        product = sum(
-            jnp.dot(lefts[t][j, side], right[t, side], preferred_element_type=jnp.float32)
-            for t in range(parts)
-            for side in range(2)
+                            piece = arrays[4 * array + 2 * y + side][pl.ds(row, depth)]
+                            right[t, side, :, c * snaps : (c + 1) * snaps] = piece
+
+    product = sum(
+        jnp.dot(
+            lefts[t][:, side].reshape(layers * snaps, depth),
+            right[t, side],
+            preferred_element_type=jnp.float32,
         )
-        for i in range(columns):
-            blocks.append(product[:, i * wide : (i + 1) * wide])
+        for t in range(parts)
+        for side in range(2)
+    )
+    wide = share * snaps
+    blocks = [
+        product[j * snaps : (j + 1) * snaps, i * wide : (i + 1) * wide]
+        for j in range(layers)
+        for i in range(columns)
+    ]
     own_ref[...] = blocks[0]
     largest = functools.reduce(jnp.maximum, [jnp.abs(block) for block in blocks[1:]])
     largest = jnp.maximum(jnp.max(largest, axis=(0, 1), keepdims=True), 1e-30)
@@ -244,11 +240,10 @@
             jax.ShapeDtypeStruct((snaps, wide), jnp.float32),
             jax.ShapeDtypeStruct((layers * columns - 1, snaps + EXTRA, wide), jnp.float32),
         ],
-        in_specs=[VMEM] * parts + [ANY] * len(arrays),
+        in_specs=[VMEM] * (parts + len(arrays)),
         out_specs=[VMEM, VMEM],
         scratch_shapes=[
             pltpu.VMEM((parts, 2, depth, columns * wide), jnp.bfloat16),
-            pltpu.SemaphoreType.DMA((parts, columns * share, 2)),
         ],
         compiler_params=PARAMS,
         cost_estimate=QUICK,
@@ -288,16 +283,16 @@
     for j in range(1, count):
         near = flip(join([scaled[t][j] for t in range(parts)]), "snap", 2 * j)
         held.append(near)
-        other.append(join([flip(near, "snap", 1)], 2.5))
+        other.append(join([flip(near, "snap", 1)], NEAR_OTHER))
         spans.append([(t, j) for t in range(parts)])
     before = own_other
     for t in range(parts):
         last = t == parts - 1
         far = [flip(scaled[t][j], "snap", 2 * j) for j in range(count, layers)]
-        far = join(far, 1.9 if last else 1.3)
+        far = join(far, FAR_LAST if last else FAR)
         sent = flip(after(far, before), "snap", 1)
         held.append(far)
-        other.append(join([sent], 3.0) if last else sent)
+        other.append(join([sent], FAR_LAST_OTHER if last else FAR_OTHER))
         spans.append([(t, j) for j in range(count, layers)])
         before = before if last else sent
     late = [held[-1], before]
@@ -317,7 +312,7 @@
 
     blocks = blocks.astype(jnp.float16)
     order = [(j, i) for j in range(layers) for i in range(columns) if i or j]
-    for j, i in sorted(order, key=lambda at: ((at[0] + at[1]) % 2, -(at[0] or layers - 1.5))):
+    for j, i in sorted(order, key=lambda at: (1, (at[0] + 1) % layers) if sum(at) % 2 else (0, -at[0])):
         pairs = [
             (s * bands + b, (s ^ (2 * j)) * bands + (b ^ (2 * i)))
             for s in range(groups)

time: 77.3 us -> 75.5 us (0.977)
  waiting for transfers between devices: 27.9 us -> 26.1 us
    ppermute x7, waiting for transfers between devices: 5.9 us -> 4.11 us  [shards(): block = lax.ppermute(blocks[j * columns + i - 1], ('snap', 'space'), pairs)]
where the time goes in v5:
time: 75.5 us; the launch traced here: 75.3 us
  starting transfers between devices  37.3 us (49%)
  waiting for transfers between devices  26.1 us (35%)
  Pallas kernels  10.6 us (14%)
  other arithmetic  0.96 us (1%)
    ppermute x18, starting transfers between devices, flip(): return lax.ppermute(cells, axis, [(i, i ^ bits) for i in range(count)])  23.7 us
    ppermute x18, waiting for transfers between devices, flip(): return lax.ppermute(cells, axis, [(i, i ^ bits) for i in range(count)])  22 us
    ppermute x7, starting transfers between devices, shards(): block = lax.ppermute(blocks[j * columns + i - 1], ('snap', 'space'), pairs)  12.9 us
    pallas_call x2, Pallas kernels, scaled_part(): pl.pallas_call(functools.partial(smooth_kernel, part, layers, bool(halo),...  5.16 us
    ppermute x7, waiting for transfers between devices, shards(): block = lax.ppermute(blocks[j * columns + i - 1], ('snap', 'space'), pairs)  4.11 us
    pallas_call x1, Pallas kernels, block_products(): pl.pallas_call(functools.partial(product_kernel, layers, columns, share,...  2.75 us
  transfers between devices with their start and end apart: 26, of which 10 were waited for; matrix products, arithmetic and copies ran while one was open for 0% of the time, Pallas kernels for 9%

profile of v5, /device:TPU:0, one launch (start us, length us, event | category | flops | bytes accessed | tf_op | source)
XLA Modules:
  0.0 75.3 jit_solution(12325837804752442471)
XLA Ops:
  0.0 1.1 %band_edges.1 = (bf16[2,720,128]{2,1,0:T(8,128)(2,1)S(1)}, bf16[2,720,128]{2,1,0:T(8,128)(2,1)S(1)}) custom-call(bf16[2,4,720,128]{3,2,1,0:T(8,128)(2,1)} %bitcast.22), custom_call_target="tpu_custom_call" | custom-call | flops 1 | bytes 1 | tf_op jit(solution)/shard_map/band_edges/pallas_call | solution.py:127
  2.3 2.5 %smooth_rows.2 = (bf16[720,128]{1,0:T(8,128)(2,1)S(1)}, bf16[720,128]{1,0:T(8,128)(2,1)S(1)}, bf16[720,128]{1,0:T(8,128)(2,1)S(1)}, bf16[720,128]{1,0:T(8,128)(2,1)S(1)}) custom-call(bf16[2,4,720,128]{3,2,1,0:T(8,128)(2,1)} %bitcast.23, f32[2,4,720]{2,1,0:T(4,128)} %lon_hbm.3, f32[2,4,720]{2,1,0:T(4,128)} %lat_hbm.3), custom_call_target="tpu_custom_call" | custom-call | flops 1 | bytes 1 | tf_op jit(solution)/shard_map/smooth_rows/pallas_call | solution.py:90
  4.8 3.7 %collective-permute-start.4 = (bf16[720,128]{1,0:T(8,128)(2,1)S(1)}, bf16[720,128]{1,0:T(8,128)(2,1)S(1)}, u32[]{:S(2)}, u32[]{:S(2)}) collective-permute-start(bf16[720,128]{1,0:T(8,128)(2,1)S(1)} %get-tuple-element.33), channel_id=1, source_target_pairs={{0,16},{4,20},{8,24},{12,28},{16,0},{20,4},{24,8},{28,12},{1,17},{... | collective-permute-start | bytes 552968 | tf_op jit(solution)/shard_map/ppermute | solution.py:25
  8.5 1.3 %collective-permute-start.5 = (bf16[720,128]{1,0:T(8,128)(2,1)S(1)}, bf16[720,128]{1,0:T(8,128)(2,1)S(1)}, u32[]{:S(2)}, u32[]{:S(2)}) collective-permute-start(bf16[720,128]{1,0:T(8,128)(2,1)S(1)} %get-tuple-element.34), channel_id=1, source_target_pairs={{0,24},{4,28},{8,16},{12,20},{16,8},{20,12},{24,0},{28,4},{1,25},{... | collective-permute-start | bytes 552968 | tf_op jit(solution)/shard_map/ppermute | solution.py:25
  9.8 2.7 %smooth_rows.3 = (bf16[720,128]{1,0:T(8,128)(2,1)S(1)}, bf16[720,128]{1,0:T(8,128)(2,1)S(1)}, bf16[720,128]{1,0:T(8,128)(2,1)S(1)}, bf16[720,128]{1,0:T(8,128)(2,1)S(1)}) custom-call(bf16[2,4,720,128]{3,2,1,0:T(8,128)(2,1)} %bitcast.24, f32[2,4,720]{2,1,0:T(4,128)} %lon_hbm.3, f32[2,4,720]{2,1,0:T(4,128)} %lat_hbm.3, ...), custom_call_target="tpu_custom_call" | custom-call | flops 1 | bytes 1 | tf_op jit(solution)/shard_map/smooth_rows/pallas_call | solution.py:90
  12.6 1.6 %collective-permute-start.6 = (bf16[1440,128]{1,0:T(8,128)(2,1)S(1)}, bf16[1440,128]{1,0:T(8,128)(2,1)S(1)}, u32[]{:S(2)}, u32[]{:S(2)}) collective-permute-start(bf16[1440,128]{1,0:T(8,128)(2,1)S(1)} %join_pieces.7.refs_0_.refs_2_), channel_id=1, source_target_pairs={{0,4},{4,0},{8,12},{12,8},{16,20},{20,16},{24,28},{28,24},{1,5},{5... | collective-permute-start | bytes 1105928 | tf_op jit(solution)/shard_map/ppermute | solution.py:25
  14.5 2.8 %collective-permute-start.2 = (bf16[720,128]{1,0:T(8,128)(2,1)S(1)}, bf16[720,128]{1,0:T(8,128)(2,1)S(1)}, u32[]{:S(2)}, u32[]{:S(2)}) collective-permute-start(bf16[720,128]{1,0:T(8,128)(2,1)S(1)} %get-tuple-element.31), channel_id=1, source_target_pairs={{0,16},{4,20},{8,24},{12,28},{16,0},{20,4},{24,8},{28,12},{1,17},{... | collective-permute-start | bytes 552968 | tf_op jit(solution)/shard_map/ppermute | solution.py:25
  17.3 3.2 %collective-permute-done.4.refs_0_ = bf16[720,128]{1,0:T(8,128)(2,1)S(1)} collective-permute-done((bf16[720,128]{1,0:T(8,128)(2,1)S(1)}, bf16[720,128]{1,0:T(8,128)(2,1)S(1)}, u32[]{:S(2)}, u32[]{:S(2)}) %collective-permute-start.4) | collective-permute-done | bytes 184352 | tf_op jit(solution)/shard_map/ppermute | solution.py:25
  20.4 5.2 %collective-permute-start.3 = (bf16[720,128]{1,0:T(8,128)(2,1)S(1)}, bf16[720,128]{1,0:T(8,128)(2,1)S(1)}, u32[]{:S(2)}, u32[]{:S(2)}) collective-permute-start(bf16[720,128]{1,0:T(8,128)(2,1)S(1)} %get-tuple-element.32), channel_id=1, source_target_pairs={{0,24},{4,28},{8,16},{12,20},{16,8},{20,12},{24,0},{28,4},{1,25},{... | collective-permute-start | bytes 552968 | tf_op jit(solution)/shard_map/ppermute | solution.py:25
  25.7 1.6 %collective-permute-start.7 = (bf16[1440,128]{1,0:T(8,128)(2,1)S(1)}, bf16[1440,128]{1,0:T(8,128)(2,1)S(1)}, u32[]{:S(2)}, u32[]{:S(2)}) collective-permute-start(bf16[1440,128]{1,0:T(8,128)(2,1)S(1)} %join_pieces.9.refs_4_.refs_10_), channel_id=1, source_target_pairs={{0,4},{4,0},{8,12},{12,8},{16,20},{20,16},{24,28},{28,24},{1,5},{5... | collective-permute-start | bytes 1105928 | tf_op jit(solution)/shard_map/ppermute | solution.py:25
  27.3 5.5 %collective-permute-done.9.refs_2_.refs_6_ = bf16[1440,128]{1,0:T(8,128)(2,1)S(1)} collective-permute-done((bf16[1440,128]{1,0:T(8,128)(2,1)S(1)}, bf16[1440,128]{1,0:T(8,128)(2,1)S(1)}, u32[]{:S(2)}, u32[]{:S(2)}) %collective-permute-start.9) | collective-permute-done | bytes 368672 | tf_op jit(solution)/shard_map/ppermute | solution.py:25
  33.5 2.7 %collective-permute-done.2.refs_0_ = bf16[720,128]{1,0:T(8,128)(2,1)S(1)} collective-permute-done((bf16[720,128]{1,0:T(8,128)(2,1)S(1)}, bf16[720,128]{1,0:T(8,128)(2,1)S(1)}, u32[]{:S(2)}, u32[]{:S(2)}) %collective-permute-start.2) | collective-permute-done | bytes 184352 | tf_op jit(solution)/shard_map/ppermute | solution.py:25
  36.3 2.8 %collective-permute-start.8 = (bf16[1440,128]{1,0:T(8,128)(2,1)S(1)}, bf16[1440,128]{1,0:T(8,128)(2,1)S(1)}, u32[]{:S(2)}, u32[]{:S(2)}) collective-permute-start(bf16[1440,128]{1,0:T(8,128)(2,1)S(1)} %join_pieces.7.refs_0_.refs_2_), channel_id=1, source_target_pairs={{0,1},{1,0},{2,3},{3,2},{4,5},{5,4},{6,7},{7,6},{8,9},{9,8},{10,11... | collective-permute-start | bytes 1105928 | tf_op jit(solution)/shard_map/ppermute | solution.py:25
  39.6 1.5 %collective-permute-start.17 = (bf16[1440,128]{1,0:T(8,128)(2,1)S(1)}, bf16[1440,128]{1,0:T(8,128)(2,1)S(1)}, u32[]{:S(2)}, u32[]{:S(2)}) collective-permute-start(bf16[1440,128]{1,0:T(8,128)(2,1)S(1)} %join_pieces.8.refs_4_.refs_14_), channel_id=1, source_target_pairs={{0,4},{4,0},{8,12},{12,8},{16,20},{20,16},{24,28},{28,24},{1,5},{5... | collective-permute-start | bytes 1105928 | tf_op jit(solution)/shard_map/ppermute | solution.py:25
  41.2 3.1 %collective-permute-done.14.refs_0_ = bf16[1440,128]{1,0:T(8,128)(2,1)S(1)} collective-permute-done((bf16[1440,128]{1,0:T(8,128)(2,1)S(1)}, bf16[1440,128]{1,0:T(8,128)(2,1)S(1)}, u32[]{:S(2)}, u32[]{:S(2)}) %collective-permute-start.14) | collective-permute-done | bytes 368672 | tf_op jit(solution)/shard_map/ppermute | solution.py:25
  46.1 5.7 %collective-permute-done.17.refs_0_ = bf16[1440,128]{1,0:T(8,128)(2,1)S(1)} collective-permute-done((bf16[1440,128]{1,0:T(8,128)(2,1)S(1)}, bf16[1440,128]{1,0:T(8,128)(2,1)S(1)}, u32[]{:S(2)}, u32[]{:S(2)}) %collective-permute-start.17) | collective-permute-done | bytes 368672 | tf_op jit(solution)/shard_map/ppermute | solution.py:25
  52.7 1.6 %collective-permute-done.18.refs_17_ = bf16[1440,128]{1,0:T(8,128)(2,1)S(1)} collective-permute-done((bf16[1440,128]{1,0:T(8,128)(2,1)S(1)}, bf16[1440,128]{1,0:T(8,128)(2,1)S(1)}, u32[]{:S(2)}, u32[]{:S(2)}) %collective-permute-start.18) | collective-permute-done | bytes 368672 | tf_op jit(solution)/shard_map/ppermute | solution.py:25
  54.3 2.8 %block_products.1 = (f32[128,256]{1,0:T(8,128)S(1)}, f32[7,136,256]{2,1,0:T(8,128)S(1)}) custom-call(bf16[4,2,128,720]{3,2,1,0:T(8,128)(2,1)S(1)} %turn_pieces.2.refs_0_, bf16[4,2,128,720]{3,2,1,0:T(8,128)(2,1)S(1)} %turn_pieces.3.refs_1_, bf16[1440,128]{1,0:T(8,128)(2,1)S(1)} %join_pieces.7.refs_0_.refs_2_, ...), custom_call_target="tpu_custom_call" | custom-call | flops 1 | bytes 1 | tf_op jit(solution)/shard_map/block_products/pallas_call | solution.py:237
  57.3 1.9 %collective-permute-start.19 = (f16[136,256]{1,0:T(8,128)(2,1)S(1)}, f16[136,256]{1,0:T(8,128)(2,1)S(1)}, u32[]{:S(2)}, u32[]{:S(2)}) collective-permute-start(f16[136,256]{1,0:T(8,128)(2,1)S(1)} %get-tuple-element.49), channel_id=1, source_target_pairs={{0,26},{1,27},{2,24},{3,25},{4,30},{5,31},{6,28},{7,29},{8,18},{9,... | collective-permute-start | bytes 208904 | tf_op jit(solution)/shard_map/ppermute | solution.py:321
  59.2 4.3 %collective-permute-start.25 = (f16[136,256]{1,0:T(8,128)(2,1)S(1)}, f16[136,256]{1,0:T(8,128)(2,1)S(1)}, u32[]{:S(2)}, u32[]{:S(2)}) collective-permute-start(f16[136,256]{1,0:T(8,128)(2,1)S(1)} %get-tuple-element.50), channel_id=1, source_target_pairs={{0,18},{1,19},{2,16},{3,17},{4,22},{5,23},{6,20},{7,21},{8,26},{9,... | collective-permute-start | bytes 208904 | tf_op jit(solution)/shard_map/ppermute | solution.py:321
  64.8 3.0 %collective-permute-start.22 = (f16[136,256]{1,0:T(8,128)(2,1)S(1)}, f16[136,256]{1,0:T(8,128)(2,1)S(1)}, u32[]{:S(2)}, u32[]{:S(2)}) collective-permute-start(f16[136,256]{1,0:T(8,128)(2,1)S(1)} %get-tuple-element.53), channel_id=1, source_target_pairs={{0,24},{1,25},{2,26},{3,27},{4,28},{5,29},{6,30},{7,31},{8,16},{9,... | collective-permute-start | bytes 208904 | tf_op jit(solution)/shard_map/ppermute | solution.py:321
  67.8 1.4 %collective-permute-start.21 = (f16[136,256]{1,0:T(8,128)(2,1)S(1)}, f16[136,256]{1,0:T(8,128)(2,1)S(1)}, u32[]{:S(2)}, u32[]{:S(2)}) collective-permute-start(f16[136,256]{1,0:T(8,128)(2,1)S(1)} %get-tuple-element.54), channel_id=1, source_target_pairs={{0,10},{1,11},{2,8},{3,9},{4,14},{5,15},{6,12},{7,13},{8,2},{9,3},... | collective-permute-start | bytes 208904 | tf_op jit(solution)/shard_map/ppermute | solution.py:321
  70.4 2.3 %collective-permute-done.22 = f16[136,256]{1,0:T(8,128)(2,1)S(1)} collective-permute-done((f16[136,256]{1,0:T(8,128)(2,1)S(1)}, f16[136,256]{1,0:T(8,128)(2,1)S(1)}, u32[]{:S(2)}, u32[]{:S(2)}) %collective-permute-start.22) | collective-permute-done | bytes 69664 | tf_op jit(solution)/shard_map/ppermute | solution.py:321
  72.7 1.0 %collective-permute-done.21 = f16[136,256]{1,0:T(8,128)(2,1)S(1)} collective-permute-done((f16[136,256]{1,0:T(8,128)(2,1)S(1)}, f16[136,256]{1,0:T(8,128)(2,1)S(1)}, u32[]{:S(2)}, u32[]{:S(2)}) %collective-permute-start.21) | collective-permute-done | bytes 69664 | tf_op jit(solution)/shard_map/ppermute | solution.py:321
  (58 shorter events, 9.7 us)
Async XLA Ops:
  1.1 8.7 %collective-permute-start = (bf16[2,720,128]{2,1,0:T(8,128)(2,1)S(1)}, bf16[2,720,128]{2,1,0:T(8,128)(2,1)S(1)}, u32[]{:S(2)}, u32[]{:S(2)}) collective-permute-start(bf16[2,720,128]{2,1,0:T(8,128)(2,1)S(1)} %get-tuple-element.28), channel_id=1, source_target_pairs={{0,1},{1,0},{2,3},{3,2},{4,5},{5,4},{6,7},{7,6},{8,9},{9,8},{10,11... | collective-permute-start | bytes 1105928 | tf_op jit(solution)/shard_map/ppermute | solution.py:25
  1.6 8.2 %collective-permute-start.1 = (bf16[2,720,128]{2,1,0:T(8,128)(2,1)S(1)}, bf16[2,720,128]{2,1,0:T(8,128)(2,1)S(1)}, u32[]{:S(2)}, u32[]{:S(2)}) collective-permute-start(bf16[2,720,128]{2,1,0:T(8,128)(2,1)S(1)} %get-tuple-element.29), channel_id=1, source_target_pairs={{1,2},{2,1},{5,6},{6,5},{9,10},{10,9},{13,14},{14,13},{17,18},{18,... | collective-permute-start | bytes 1105928 | tf_op jit(solution)/shard_map/ppermute | solution.py:271
  4.8 15.7 %collective-permute-start.4 = (bf16[720,128]{1,0:T(8,128)(2,1)S(1)}, bf16[720,128]{1,0:T(8,128)(2,1)S(1)}, u32[]{:S(2)}, u32[]{:S(2)}) collective-permute-start(bf16[720,128]{1,0:T(8,128)(2,1)S(1)} %get-tuple-element.33), channel_id=1, source_target_pairs={{0,16},{4,20},{8,24},{12,28},{16,0},{20,4},{24,8},{28,12},{1,17},{... | collective-permute-start | bytes 552968 | tf_op jit(solution)/shard_map/ppermute | solution.py:25
  8.5 17.2 %collective-permute-start.5 = (bf16[720,128]{1,0:T(8,128)(2,1)S(1)}, bf16[720,128]{1,0:T(8,128)(2,1)S(1)}, u32[]{:S(2)}, u32[]{:S(2)}) collective-permute-start(bf16[720,128]{1,0:T(8,128)(2,1)S(1)} %get-tuple-element.34), channel_id=1, source_target_pairs={{0,24},{4,28},{8,16},{12,20},{16,8},{20,12},{24,0},{28,4},{1,25},{... | collective-permute-start | bytes 552968 | tf_op jit(solution)/shard_map/ppermute | solution.py:25
  12.6 13.1 %collective-permute-start.6 = (bf16[1440,128]{1,0:T(8,128)(2,1)S(1)}, bf16[1440,128]{1,0:T(8,128)(2,1)S(1)}, u32[]{:S(2)}, u32[]{:S(2)}) collective-permute-start(bf16[1440,128]{1,0:T(8,128)(2,1)S(1)} %join_pieces.7.refs_0_.refs_2_), channel_id=1, source_target_pairs={{0,4},{4,0},{8,12},{12,8},{16,20},{20,16},{24,28},{28,24},{1,5},{5... | collective-permute-start | bytes 1105928 | tf_op jit(solution)/shard_map/ppermute | solution.py:25
  14.2 18.6 %collective-permute-start.9 = (bf16[1440,128]{1,0:T(8,128)(2,1)S(1)}, bf16[1440,128]{1,0:T(8,128)(2,1)S(1)}, u32[]{:S(2)}, u32[]{:S(2)}) collective-permute-start(bf16[1440,128]{1,0:T(8,128)(2,1)S(1)} %join_pieces.10), channel_id=1, source_target_pairs={{0,8},{4,12},{8,0},{12,4},{16,24},{20,28},{24,16},{28,20},{1,9},{5... | collective-permute-start | bytes 1105928 | tf_op jit(solution)/shard_map/ppermute | solution.py:25
  14.5 21.7 %collective-permute-start.2 = (bf16[720,128]{1,0:T(8,128)(2,1)S(1)}, bf16[720,128]{1,0:T(8,128)(2,1)S(1)}, u32[]{:S(2)}, u32[]{:S(2)}) collective-permute-start(bf16[720,128]{1,0:T(8,128)(2,1)S(1)} %get-tuple-element.31), channel_id=1, source_target_pairs={{0,16},{4,20},{8,24},{12,28},{16,0},{20,4},{24,8},{28,12},{1,17},{... | collective-permute-start | bytes 552968 | tf_op jit(solution)/shard_map/ppermute | solution.py:25
  20.4 15.7 %collective-permute-start.3 = (bf16[720,128]{1,0:T(8,128)(2,1)S(1)}, bf16[720,128]{1,0:T(8,128)(2,1)S(1)}, u32[]{:S(2)}, u32[]{:S(2)}) collective-permute-start(bf16[720,128]{1,0:T(8,128)(2,1)S(1)} %get-tuple-element.32), channel_id=1, source_target_pairs={{0,24},{4,28},{8,16},{12,20},{16,8},{20,12},{24,0},{28,4},{1,25},{... | collective-permute-start | bytes 552968 | tf_op jit(solution)/shard_map/ppermute | solution.py:25
  25.7 10.6 %collective-permute-start.7 = (bf16[1440,128]{1,0:T(8,128)(2,1)S(1)}, bf16[1440,128]{1,0:T(8,128)(2,1)S(1)}, u32[]{:S(2)}, u32[]{:S(2)}) collective-permute-start(bf16[1440,128]{1,0:T(8,128)(2,1)S(1)} %join_pieces.9.refs_4_.refs_10_), channel_id=1, source_target_pairs={{0,4},{4,0},{8,12},{12,8},{16,20},{20,16},{24,28},{28,24},{1,5},{5... | collective-permute-start | bytes 1105928 | tf_op jit(solution)/shard_map/ppermute | solution.py:25
  32.8 11.5 %collective-permute-start.14 = (bf16[1440,128]{1,0:T(8,128)(2,1)S(1)}, bf16[1440,128]{1,0:T(8,128)(2,1)S(1)}, u32[]{:S(2)}, u32[]{:S(2)}) collective-permute-start(bf16[1440,128]{1,0:T(8,128)(2,1)S(1)} %collective-permute-done.9.refs_2_.refs_6_), channel_id=1, source_target_pairs={{0,4},{4,0},{8,12},{12,8},{16,20},{20,16},{24,28},{28,24},{1,5},{5... | collective-permute-start | bytes 1105928 | tf_op jit(solution)/shard_map/ppermute | solution.py:25
  36.3 8.1 %collective-permute-start.8 = (bf16[1440,128]{1,0:T(8,128)(2,1)S(1)}, bf16[1440,128]{1,0:T(8,128)(2,1)S(1)}, u32[]{:S(2)}, u32[]{:S(2)}) collective-permute-start(bf16[1440,128]{1,0:T(8,128)(2,1)S(1)} %join_pieces.7.refs_0_.refs_2_), channel_id=1, source_target_pairs={{0,1},{1,0},{2,3},{3,2},{4,5},{5,4},{6,7},{7,6},{8,9},{9,8},{10,11... | collective-permute-start | bytes 1105928 | tf_op jit(solution)/shard_map/ppermute | solution.py:25
  39.1 5.8 %collective-permute-start.10 = (bf16[1440,128]{1,0:T(8,128)(2,1)S(1)}, bf16[1440,128]{1,0:T(8,128)(2,1)S(1)}, u32[]{:S(2)}, u32[]{:S(2)}) collective-permute-start(bf16[1440,128]{1,0:T(8,128)(2,1)S(1)} %collective-permute-done.9.refs_2_.refs_6_), channel_id=1, source_target_pairs={{0,1},{1,0},{2,3},{3,2},{4,5},{5,4},{6,7},{7,6},{8,9},{9,8},{10,11... | collective-permute-start | bytes 1105928 | tf_op jit(solution)/shard_map/ppermute | solution.py:25
  39.2 5.8 %collective-permute-start.12 = (bf16[1440,128]{1,0:T(8,128)(2,1)S(1)}, bf16[1440,128]{1,0:T(8,128)(2,1)S(1)}, u32[]{:S(2)}, u32[]{:S(2)}) collective-permute-start(bf16[1440,128]{1,0:T(8,128)(2,1)S(1)} %join_pieces.8.refs_4_.refs_14_), channel_id=1, source_target_pairs={{0,1},{1,0},{2,3},{3,2},{4,5},{5,4},{6,7},{7,6},{8,9},{9,8},{10,11... | collective-permute-start | bytes 1105928 | tf_op jit(solution)/shard_map/ppermute | solution.py:25
  39.6 12.2 %collective-permute-start.17 = (bf16[1440,128]{1,0:T(8,128)(2,1)S(1)}, bf16[1440,128]{1,0:T(8,128)(2,1)S(1)}, u32[]{:S(2)}, u32[]{:S(2)}) collective-permute-start(bf16[1440,128]{1,0:T(8,128)(2,1)S(1)} %join_pieces.8.refs_4_.refs_14_), channel_id=1, source_target_pairs={{0,4},{4,0},{8,12},{12,8},{16,20},{20,16},{24,28},{28,24},{1,5},{5... | collective-permute-start | bytes 1105928 | tf_op jit(solution)/shard_map/ppermute | solution.py:25
  44.3 8.3 %collective-permute-start.16 = (bf16[1440,128]{1,0:T(8,128)(2,1)S(1)}, bf16[1440,128]{1,0:T(8,128)(2,1)S(1)}, u32[]{:S(2)}, u32[]{:S(2)}) collective-permute-start(bf16[1440,128]{1,0:T(8,128)(2,1)S(1)} %join_pieces.12.refs_12_), channel_id=1, source_target_pairs={{0,1},{1,0},{2,3},{3,2},{4,5},{5,4},{6,7},{7,6},{8,9},{9,8},{10,11... | collective-permute-start | bytes 1105928 | tf_op jit(solution)/shard_map/ppermute | solution.py:25
  44.4 7.5 %collective-permute-start.11 = (bf16[1440,128]{1,0:T(8,128)(2,1)S(1)}, bf16[1440,128]{1,0:T(8,128)(2,1)S(1)}, u32[]{:S(2)}, u32[]{:S(2)}) collective-permute-start(bf16[1440,128]{1,0:T(8,128)(2,1)S(1)} %join_pieces.9.refs_4_.refs_10_), channel_id=1, source_target_pairs={{0,1},{1,0},{2,3},{3,2},{4,5},{5,4},{6,7},{7,6},{8,9},{9,8},{10,11... | collective-permute-start | bytes 1105928 | tf_op jit(solution)/shard_map/ppermute | solution.py:25
  44.9 7.8 %collective-permute-start.13 = (bf16[1440,128]{1,0:T(8,128)(2,1)S(1)}, bf16[1440,128]{1,0:T(8,128)(2,1)S(1)}, u32[]{:S(2)}, u32[]{:S(2)}) collective-permute-start(bf16[1440,128]{1,0:T(8,128)(2,1)S(1)} %collective-permute-done.6.refs_4_), channel_id=1, source_target_pairs={{0,1},{1,0},{2,3},{3,2},{4,5},{5,4},{6,7},{7,6},{8,9},{9,8},{10,11... | collective-permute-start | bytes 1105928 | tf_op jit(solution)/shard_map/ppermute | solution.py:25
  45.0 7.7 %collective-permute-start.15 = (bf16[1440,128]{1,0:T(8,128)(2,1)S(1)}, bf16[1440,128]{1,0:T(8,128)(2,1)S(1)}, u32[]{:S(2)}, u32[]{:S(2)}) collective-permute-start(bf16[1440,128]{1,0:T(8,128)(2,1)S(1)} %join_pieces.11.refs_8_), channel_id=1, source_target_pairs={{0,1},{1,0},{2,3},{3,2},{4,5},{5,4},{6,7},{7,6},{8,9},{9,8},{10,11... | collective-permute-start | bytes 1105928 | tf_op jit(solution)/shard_map/ppermute | solution.py:25
  57.3 10.5 %collective-permute-start.19 = (f16[136,256]{1,0:T(8,128)(2,1)S(1)}, f16[136,256]{1,0:T(8,128)(2,1)S(1)}, u32[]{:S(2)}, u32[]{:S(2)}) collective-permute-start(f16[136,256]{1,0:T(8,128)(2,1)S(1)} %get-tuple-element.49), channel_id=1, source_target_pairs={{0,26},{1,27},{2,24},{3,25},{4,30},{5,31},{6,28},{7,29},{8,18},{9,... | collective-permute-start | bytes 208904 | tf_op jit(solution)/shard_map/ppermute | solution.py:321
  59.2 10.0 %collective-permute-start.25 = (f16[136,256]{1,0:T(8,128)(2,1)S(1)}, f16[136,256]{1,0:T(8,128)(2,1)S(1)}, u32[]{:S(2)}, u32[]{:S(2)}) collective-permute-start(f16[136,256]{1,0:T(8,128)(2,1)S(1)} %get-tuple-element.50), channel_id=1, source_target_pairs={{0,18},{1,19},{2,16},{3,17},{4,22},{5,23},{6,20},{7,21},{8,26},{9,... | collective-permute-start | bytes 208904 | tf_op jit(solution)/shard_map/ppermute | solution.py:321
  63.5 6.8 %collective-permute-start.24 = (f16[136,256]{1,0:T(8,128)(2,1)S(1)}, f16[136,256]{1,0:T(8,128)(2,1)S(1)}, u32[]{:S(2)}, u32[]{:S(2)}) collective-permute-start(f16[136,256]{1,0:T(8,128)(2,1)S(1)} %get-tuple-element.51), channel_id=1, source_target_pairs={{0,8},{1,9},{2,10},{3,11},{4,12},{5,13},{6,14},{7,15},{8,0},{9,1},... | collective-permute-start | bytes 208904 | tf_op jit(solution)/shard_map/ppermute | solution.py:321
  63.9 6.4 %collective-permute-start.23 = (f16[136,256]{1,0:T(8,128)(2,1)S(1)}, f16[136,256]{1,0:T(8,128)(2,1)S(1)}, u32[]{:S(2)}, u32[]{:S(2)}) collective-permute-start(f16[136,256]{1,0:T(8,128)(2,1)S(1)} %get-tuple-element.52), channel_id=1, source_target_pairs={{0,2},{1,3},{2,0},{3,1},{4,6},{5,7},{6,4},{7,5},{8,10},{9,11},{10,... | collective-permute-start | bytes 208904 | tf_op jit(solution)/shard_map/ppermute | solution.py:321
  64.8 7.8 %collective-permute-start.22 = (f16[136,256]{1,0:T(8,128)(2,1)S(1)}, f16[136,256]{1,0:T(8,128)(2,1)S(1)}, u32[]{:S(2)}, u32[]{:S(2)}) collective-permute-start(f16[136,256]{1,0:T(8,128)(2,1)S(1)} %get-tuple-element.53), channel_id=1, source_target_pairs={{0,24},{1,25},{2,26},{3,27},{4,28},{5,29},{6,30},{7,31},{8,16},{9,... | collective-permute-start | bytes 208904 | tf_op jit(solution)/shard_map/ppermute | solution.py:321
  67.8 5.9 %collective-permute-start.21 = (f16[136,256]{1,0:T(8,128)(2,1)S(1)}, f16[136,256]{1,0:T(8,128)(2,1)S(1)}, u32[]{:S(2)}, u32[]{:S(2)}) collective-permute-start(f16[136,256]{1,0:T(8,128)(2,1)S(1)} %get-tuple-element.54), channel_id=1, source_target_pairs={{0,10},{1,11},{2,8},{3,9},{4,14},{5,15},{6,12},{7,13},{8,2},{9,3},... | collective-permute-start | bytes 208904 | tf_op jit(solution)/shard_map/ppermute | solution.py:321
  (2 other events, 7.0 us)

commit v6 on v5

--- a/solution.py
+++ b/solution.py
@@ -14,7 +14,7 @@
 ANY = pl.BlockSpec(memory_space=pl.ANY)
 HBM = pl.BlockSpec(memory_space=pltpu.HBM)
 VMEM = pl.BlockSpec(memory_space=pltpu.VMEM)
-FAR, FAR_LAST, NEAR_OTHER, FAR_OTHER, FAR_LAST_OTHER = 1.1, 2.2, 4.0, 0.5, 3.0
+FAR, FAR_LAST, NEAR_OTHER, FAR_OTHER, FAR_LAST_OTHER = 1.1, 2.2, 4.0, 0.5, 3.6
 UNIT = 18 * 10**8
 QUICK = pl.CostEstimate(flops=1, bytes_accessed=1, transcendentals=0)
 PARAMS = pltpu.CompilerParams(vmem_limit_bytes=VMEM_BYTES)
@@ -187,7 +187,8 @@
 
 def product_kernel(layers, columns, share, places, *refs):
     parts = len(places)
-    lefts, refs = refs[:parts], refs[parts:]
+    near_ref, *far_refs = refs[: 1 + parts]
+    refs = refs[1 + parts :]
     *arrays, own_ref, out_ref, right = refs
     depth, snaps = right.shape[2], arrays[0].shape[1]
     me, band = lax.axis_index("snap"), lax.axis_index("space")
@@ -205,9 +206,12 @@
                             piece = arrays[4 * array + 2 * y + side][pl.ds(row, depth)]
                             right[t, side, :, c * snaps : (c + 1) * snaps] = piece
 
+    near = near_ref.shape[0] // parts
     product = sum(
         jnp.dot(
-            lefts[t][:, side].reshape(layers * snaps, depth),
+            jnp.concatenate(
+                [near_ref[t * near : (t + 1) * near, side], far_refs[t][:, side]], axis=0
+            ).reshape(layers * snaps, depth),
             right[t, side],
             preferred_element_type=jnp.float32,
         )
@@ -231,7 +235,7 @@
 
 
 def block_products(layers, columns, share, lefts, arrays, places):
-    parts = len(lefts)
+    parts = len(places)
     snaps, depth = lefts[0].shape[2:]
     wide = snaps * share
     return pl.pallas_call(
@@ -240,7 +244,7 @@
             jax.ShapeDtypeStruct((snaps, wide), jnp.float32),
             jax.ShapeDtypeStruct((layers * columns - 1, snaps + EXTRA, wide), jnp.float32),
         ],
-        in_specs=[VMEM] * (parts + len(arrays)),
+        in_specs=[VMEM] * (1 + parts + len(arrays)),
         out_specs=[VMEM, VMEM],
         scratch_shapes=[
             pltpu.VMEM((parts, 2, depth, columns * wide), jnp.bfloat16),
@@ -276,7 +280,6 @@
         for t in range(inner_parts, parts)
     ]
 
-    spans = [[(t, 0) for t in range(parts)]]
     own = join([scaled[t][0] for t in range(parts)])
     own_other = flip(own, "snap", 1)
     held, other = [own], [own_other]
@@ -284,7 +287,6 @@
         near = flip(join([scaled[t][j] for t in range(parts)]), "snap", 2 * j)
         held.append(near)
         other.append(join([flip(near, "snap", 1)], NEAR_OTHER))
-        spans.append([(t, j) for t in range(parts)])
     before = own_other
     for t in range(parts):
         last = t == parts - 1
@@ -293,18 +295,18 @@
         sent = flip(after(far, before), "snap", 1)
         held.append(far)
         other.append(join([sent], FAR_LAST_OTHER if last else FAR_OTHER))
-        spans.append([(t, j) for j in range(count, layers)])
         before = before if last else sent
     late = [held[-1], before]
     held_too = [flip(after(array, *late), "space", 1) for array in held]
-    places, lefts = [], []
+    places = [
+        [(j, t * nlon) for j in range(count)] + [(count + t, n * nlon) for n in range(layers - count)]
+        for t in range(parts)
+    ]
+    arrays = [array for pair in zip(held[:count], held_too) for array in pair]
+    lefts = [turned(arrays, [at for t in range(parts) for at in places[t][:count]], nlon)]
     for t in range(parts):
-        at = [(n, span) for n, span in enumerate(spans) if (t, span[-1][1]) in span]
-        where = [(n, span.index((t, j)) * nlon) for j in range(layers) for n, span in at if (t, j) in span]
-        places.append(where)
-        used = [n for n, _ in at]
-        arrays = [array for n in used for array in (held[n], held_too[n])]
-        lefts.append(turned(arrays, [(used.index(n), row) for n, row in where], nlon))
+        arrays = [held[count + t], held_too[count + t]]
+        lefts.append(turned(arrays, [(0, n * nlon) for n in range(layers - count)], nlon))
     other_too = [flip(after(array, *late), "space", 1) for array in other[:-1]]
     other_too.append(flip(after(other[-1], *lefts), "space", 1))
     arrays = [array for arrays in zip(held, held_too, other, other_too) for array in arrays]

time: 75.5 us -> 75.7 us (level)
    pallas_call x2 -> x3, Pallas kernels: 1.38 us -> 1.56 us  [turned(): pl.pallas_call(functools.partial(turn_kernel, places, depth), out_shape=j...]
  transfers between devices with their start and end apart: 26 -> 26, of which waited for: 10 -> 11; matrix products, arithmetic and copies ran while one was open for 0% -> 0% of each run, Pallas kernels for 9% -> 9%
where the time goes in v6:
time: 75.7 us; the launch traced here: 75.5 us
  starting transfers between devices  37.5 us (50%)
  waiting for transfers between devices  25.9 us (34%)
  Pallas kernels  10.8 us (14%)
  other arithmetic  0.96 us (1%)
    ppermute x18, starting transfers between devices, flip(): return lax.ppermute(cells, axis, [(i, i ^ bits) for i in range(count)])  23.8 us
    ppermute x18, waiting for transfers between devices, flip(): return lax.ppermute(cells, axis, [(i, i ^ bits) for i in range(count)])  21.8 us
    ppermute x7, starting transfers between devices, shards(): block = lax.ppermute(blocks[j * columns + i - 1], ('snap', 'space'), pairs)  13 us
    pallas_call x2, Pallas kernels, scaled_part(): pl.pallas_call(functools.partial(smooth_kernel, part, layers, bool(halo),...  5.16 us
    ppermute x7, waiting for transfers between devices, shards(): block = lax.ppermute(blocks[j * columns + i - 1], ('snap', 'space'), pairs)  4.07 us
    pallas_call x1, Pallas kernels, block_products(): pl.pallas_call(functools.partial(product_kernel, layers, columns, share,...  2.75 us
    pallas_call x3, Pallas kernels, turned(): pl.pallas_call(functools.partial(turn_kernel, places, depth), out_shape=j...  1.56 us
  transfers between devices with their start and end apart: 26, of which 11 were waited for; matrix products, arithmetic and copies ran while one was open for 0% of the time, Pallas kernels for 9%

profile of v6, /device:TPU:0, one launch (start us, length us, event | category | flops | bytes accessed | tf_op | source)
XLA Modules:
  0.0 75.5 jit_solution(5771192981486178906)
XLA Ops:
  0.0 1.1 %band_edges.1 = (bf16[2,720,128]{2,1,0:T(8,128)(2,1)S(1)}, bf16[2,720,128]{2,1,0:T(8,128)(2,1)S(1)}) custom-call(bf16[2,4,720,128]{3,2,1,0:T(8,128)(2,1)} %bitcast.22), custom_call_target="tpu_custom_call" | custom-call | flops 1 | bytes 1 | tf_op jit(solution)/shard_map/band_edges/pallas_call | solution.py:127
  2.3 2.5 %smooth_rows.2 = (bf16[720,128]{1,0:T(8,128)(2,1)S(1)}, bf16[720,128]{1,0:T(8,128)(2,1)S(1)}, bf16[720,128]{1,0:T(8,128)(2,1)S(1)}, bf16[720,128]{1,0:T(8,128)(2,1)S(1)}) custom-call(bf16[2,4,720,128]{3,2,1,0:T(8,128)(2,1)} %bitcast.23, f32[2,4,720]{2,1,0:T(4,128)} %lon_hbm.3, f32[2,4,720]{2,1,0:T(4,128)} %lat_hbm.3), custom_call_target="tpu_custom_call" | custom-call | flops 1 | bytes 1 | tf_op jit(solution)/shard_map/smooth_rows/pallas_call | solution.py:90
  4.8 3.7 %collective-permute-start.4 = (bf16[720,128]{1,0:T(8,128)(2,1)S(1)}, bf16[720,128]{1,0:T(8,128)(2,1)S(1)}, u32[]{:S(2)}, u32[]{:S(2)}) collective-permute-start(bf16[720,128]{1,0:T(8,128)(2,1)S(1)} %get-tuple-element.33), channel_id=1, source_target_pairs={{0,16},{4,20},{8,24},{12,28},{16,0},{20,4},{24,8},{28,12},{1,17},{... | collective-permute-start | bytes 552968 | tf_op jit(solution)/shard_map/ppermute | solution.py:25
  8.5 1.3 %collective-permute-start.5 = (bf16[720,128]{1,0:T(8,128)(2,1)S(1)}, bf16[720,128]{1,0:T(8,128)(2,1)S(1)}, u32[]{:S(2)}, u32[]{:S(2)}) collective-permute-start(bf16[720,128]{1,0:T(8,128)(2,1)S(1)} %get-tuple-element.34), channel_id=1, source_target_pairs={{0,24},{4,28},{8,16},{12,20},{16,8},{20,12},{24,0},{28,4},{1,25},{... | collective-permute-start | bytes 552968 | tf_op jit(solution)/shard_map/ppermute | solution.py:25
  9.8 2.7 %smooth_rows.3 = (bf16[720,128]{1,0:T(8,128)(2,1)S(1)}, bf16[720,128]{1,0:T(8,128)(2,1)S(1)}, bf16[720,128]{1,0:T(8,128)(2,1)S(1)}, bf16[720,128]{1,0:T(8,128)(2,1)S(1)}) custom-call(bf16[2,4,720,128]{3,2,1,0:T(8,128)(2,1)} %bitcast.24, f32[2,4,720]{2,1,0:T(4,128)} %lon_hbm.3, f32[2,4,720]{2,1,0:T(4,128)} %lat_hbm.3, ...), custom_call_target="tpu_custom_call" | custom-call | flops 1 | bytes 1 | tf_op jit(solution)/shard_map/smooth_rows/pallas_call | solution.py:90
  12.6 1.6 %collective-permute-start.6 = (bf16[1440,128]{1,0:T(8,128)(2,1)S(1)}, bf16[1440,128]{1,0:T(8,128)(2,1)S(1)}, u32[]{:S(2)}, u32[]{:S(2)}) collective-permute-start(bf16[1440,128]{1,0:T(8,128)(2,1)S(1)} %join_pieces.7.refs_0_.refs_3_), channel_id=1, source_target_pairs={{0,4},{4,0},{8,12},{12,8},{16,20},{20,16},{24,28},{28,24},{1,5},{5... | collective-permute-start | bytes 1105928 | tf_op jit(solution)/shard_map/ppermute | solution.py:25
  14.5 2.8 %collective-permute-start.2 = (bf16[720,128]{1,0:T(8,128)(2,1)S(1)}, bf16[720,128]{1,0:T(8,128)(2,1)S(1)}, u32[]{:S(2)}, u32[]{:S(2)}) collective-permute-start(bf16[720,128]{1,0:T(8,128)(2,1)S(1)} %get-tuple-element.31), channel_id=1, source_target_pairs={{0,16},{4,20},{8,24},{12,28},{16,0},{20,4},{24,8},{28,12},{1,17},{... | collective-permute-start | bytes 552968 | tf_op jit(solution)/shard_map/ppermute | solution.py:25
  17.3 3.2 %collective-permute-done.4.refs_0_ = bf16[720,128]{1,0:T(8,128)(2,1)S(1)} collective-permute-done((bf16[720,128]{1,0:T(8,128)(2,1)S(1)}, bf16[720,128]{1,0:T(8,128)(2,1)S(1)}, u32[]{:S(2)}, u32[]{:S(2)}) %collective-permute-start.4) | collective-permute-done | bytes 184352 | tf_op jit(solution)/shard_map/ppermute | solution.py:25
  20.4 5.2 %collective-permute-start.3 = (bf16[720,128]{1,0:T(8,128)(2,1)S(1)}, bf16[720,128]{1,0:T(8,128)(2,1)S(1)}, u32[]{:S(2)}, u32[]{:S(2)}) collective-permute-start(bf16[720,128]{1,0:T(8,128)(2,1)S(1)} %get-tuple-element.32), channel_id=1, source_target_pairs={{0,24},{4,28},{8,16},{12,20},{16,8},{20,12},{24,0},{28,4},{1,25},{... | collective-permute-start | bytes 552968 | tf_op jit(solution)/shard_map/ppermute | solution.py:25
  25.7 1.6 %collective-permute-start.7 = (bf16[1440,128]{1,0:T(8,128)(2,1)S(1)}, bf16[1440,128]{1,0:T(8,128)(2,1)S(1)}, u32[]{:S(2)}, u32[]{:S(2)}) collective-permute-start(bf16[1440,128]{1,0:T(8,128)(2,1)S(1)} %join_pieces.9.refs_0_.refs_11_), channel_id=1, source_target_pairs={{0,4},{4,0},{8,12},{12,8},{16,20},{20,16},{24,28},{28,24},{1,5},{5... | collective-permute-start | bytes 1105928 | tf_op jit(solution)/shard_map/ppermute | solution.py:25
  27.3 5.5 %collective-permute-done.9.refs_2_.refs_7_ = bf16[1440,128]{1,0:T(8,128)(2,1)S(1)} collective-permute-done((bf16[1440,128]{1,0:T(8,128)(2,1)S(1)}, bf16[1440,128]{1,0:T(8,128)(2,1)S(1)}, u32[]{:S(2)}, u32[]{:S(2)}) %collective-permute-start.9) | collective-permute-done | bytes 368672 | tf_op jit(solution)/shard_map/ppermute | solution.py:25
  33.5 2.7 %collective-permute-done.2.refs_0_ = bf16[720,128]{1,0:T(8,128)(2,1)S(1)} collective-permute-done((bf16[720,128]{1,0:T(8,128)(2,1)S(1)}, bf16[720,128]{1,0:T(8,128)(2,1)S(1)}, u32[]{:S(2)}, u32[]{:S(2)}) %collective-permute-start.2) | collective-permute-done | bytes 184352 | tf_op jit(solution)/shard_map/ppermute | solution.py:25
  36.3 2.8 %collective-permute-start.11 = (bf16[1440,128]{1,0:T(8,128)(2,1)S(1)}, bf16[1440,128]{1,0:T(8,128)(2,1)S(1)}, u32[]{:S(2)}, u32[]{:S(2)}) collective-permute-start(bf16[1440,128]{1,0:T(8,128)(2,1)S(1)} %join_pieces.9.refs_0_.refs_11_), channel_id=1, source_target_pairs={{0,1},{1,0},{2,3},{3,2},{4,5},{5,4},{6,7},{7,6},{8,9},{9,8},{10,11... | collective-permute-start | bytes 1105928 | tf_op jit(solution)/shard_map/ppermute | solution.py:25
  39.2 1.5 %collective-permute-start.17 = (bf16[1440,128]{1,0:T(8,128)(2,1)S(1)}, bf16[1440,128]{1,0:T(8,128)(2,1)S(1)}, u32[]{:S(2)}, u32[]{:S(2)}) collective-permute-start(bf16[1440,128]{1,0:T(8,128)(2,1)S(1)} %join_pieces.8.refs_0_.refs_15_), channel_id=1, source_target_pairs={{0,4},{4,0},{8,12},{12,8},{16,20},{20,16},{24,28},{28,24},{1,5},{5... | collective-permute-start | bytes 1105928 | tf_op jit(solution)/shard_map/ppermute | solution.py:25
  40.7 3.6 %collective-permute-done.14.refs_0_ = bf16[1440,128]{1,0:T(8,128)(2,1)S(1)} collective-permute-done((bf16[1440,128]{1,0:T(8,128)(2,1)S(1)}, bf16[1440,128]{1,0:T(8,128)(2,1)S(1)}, u32[]{:S(2)}, u32[]{:S(2)}) %collective-permute-start.14) | collective-permute-done | bytes 368672 | tf_op jit(solution)/shard_map/ppermute | solution.py:25
  46.4 5.5 %collective-permute-done.17.refs_0_ = bf16[1440,128]{1,0:T(8,128)(2,1)S(1)} collective-permute-done((bf16[1440,128]{1,0:T(8,128)(2,1)S(1)}, bf16[1440,128]{1,0:T(8,128)(2,1)S(1)}, u32[]{:S(2)}, u32[]{:S(2)}) %collective-permute-start.17) | collective-permute-done | bytes 368672 | tf_op jit(solution)/shard_map/ppermute | solution.py:25
  54.5 2.8 %block_products.1 = (f32[128,256]{1,0:T(8,128)S(1)}, f32[7,136,256]{2,1,0:T(8,128)S(1)}) custom-call(bf16[4,2,128,720]{3,2,1,0:T(8,128)(2,1)S(1)} %turn_pieces.3.refs_0_, bf16[2,2,128,720]{3,2,1,0:T(8,128)(2,1)S(1)} %turn_pieces.4.refs_1_, bf16[2,2,128,720]{3,2,1,0:T(8,128)(2,1)S(1)} %turn_pieces.5.refs_2_, ...), custom_call_target="tpu_custom_call" | custom-call | flops 1 | bytes 1 | tf_op jit(solution)/shard_map/block_products/pallas_call | solution.py:241
  57.4 1.5 %collective-permute-start.19 = (f16[136,256]{1,0:T(8,128)(2,1)S(1)}, f16[136,256]{1,0:T(8,128)(2,1)S(1)}, u32[]{:S(2)}, u32[]{:S(2)}) collective-permute-start(f16[136,256]{1,0:T(8,128)(2,1)S(1)} %get-tuple-element.49), channel_id=1, source_target_pairs={{0,26},{1,27},{2,24},{3,25},{4,30},{5,31},{6,28},{7,29},{8,18},{9,... | collective-permute-start | bytes 208904 | tf_op jit(solution)/shard_map/ppermute | solution.py:323
  58.9 4.7 %collective-permute-start.25 = (f16[136,256]{1,0:T(8,128)(2,1)S(1)}, f16[136,256]{1,0:T(8,128)(2,1)S(1)}, u32[]{:S(2)}, u32[]{:S(2)}) collective-permute-start(f16[136,256]{1,0:T(8,128)(2,1)S(1)} %get-tuple-element.50), channel_id=1, source_target_pairs={{0,18},{1,19},{2,16},{3,17},{4,22},{5,23},{6,20},{7,21},{8,26},{9,... | collective-permute-start | bytes 208904 | tf_op jit(solution)/shard_map/ppermute | solution.py:323
  65.0 3.0 %collective-permute-start.22 = (f16[136,256]{1,0:T(8,128)(2,1)S(1)}, f16[136,256]{1,0:T(8,128)(2,1)S(1)}, u32[]{:S(2)}, u32[]{:S(2)}) collective-permute-start(f16[136,256]{1,0:T(8,128)(2,1)S(1)} %get-tuple-element.53), channel_id=1, source_target_pairs={{0,24},{1,25},{2,26},{3,27},{4,28},{5,29},{6,30},{7,31},{8,16},{9,... | collective-permute-start | bytes 208904 | tf_op jit(solution)/shard_map/ppermute | solution.py:323
  67.9 1.4 %collective-permute-start.21 = (f16[136,256]{1,0:T(8,128)(2,1)S(1)}, f16[136,256]{1,0:T(8,128)(2,1)S(1)}, u32[]{:S(2)}, u32[]{:S(2)}) collective-permute-start(f16[136,256]{1,0:T(8,128)(2,1)S(1)} %get-tuple-element.54), channel_id=1, source_target_pairs={{0,10},{1,11},{2,8},{3,9},{4,14},{5,15},{6,12},{7,13},{8,2},{9,3},... | collective-permute-start | bytes 208904 | tf_op jit(solution)/shard_map/ppermute | solution.py:323
  69.4 1.0 %collective-permute-start.20 = (f16[136,256]{1,0:T(8,128)(2,1)S(1)}, f16[136,256]{1,0:T(8,128)(2,1)S(1)}, u32[]{:S(2)}, u32[]{:S(2)}) collective-permute-start(f16[136,256]{1,0:T(8,128)(2,1)S(1)} %get-tuple-element.55), channel_id=1, source_target_pairs={{0,16},{1,17},{2,18},{3,19},{4,20},{5,21},{6,22},{7,23},{8,24},{9,... | collective-permute-start | bytes 208904 | tf_op jit(solution)/shard_map/ppermute | solution.py:323
  70.6 2.1 %collective-permute-done.22 = f16[136,256]{1,0:T(8,128)(2,1)S(1)} collective-permute-done((f16[136,256]{1,0:T(8,128)(2,1)S(1)}, f16[136,256]{1,0:T(8,128)(2,1)S(1)}, u32[]{:S(2)}, u32[]{:S(2)}) %collective-permute-start.22) | collective-permute-done | bytes 69664 | tf_op jit(solution)/shard_map/ppermute | solution.py:323
  72.7 1.2 %collective-permute-done.21 = f16[136,256]{1,0:T(8,128)(2,1)S(1)} collective-permute-done((f16[136,256]{1,0:T(8,128)(2,1)S(1)}, f16[136,256]{1,0:T(8,128)(2,1)S(1)}, u32[]{:S(2)}, u32[]{:S(2)}) %collective-permute-start.21) | collective-permute-done | bytes 69664 | tf_op jit(solution)/shard_map/ppermute | solution.py:323
  (59 shorter events, 10.2 us)
Async XLA Ops:
  1.1 8.7 %collective-permute-start = (bf16[2,720,128]{2,1,0:T(8,128)(2,1)S(1)}, bf16[2,720,128]{2,1,0:T(8,128)(2,1)S(1)}, u32[]{:S(2)}, u32[]{:S(2)}) collective-permute-start(bf16[2,720,128]{2,1,0:T(8,128)(2,1)S(1)} %get-tuple-element.28), channel_id=1, source_target_pairs={{0,1},{1,0},{2,3},{3,2},{4,5},{5,4},{6,7},{7,6},{8,9},{9,8},{10,11... | collective-permute-start | bytes 1105928 | tf_op jit(solution)/shard_map/ppermute | solution.py:25
  1.6 8.2 %collective-permute-start.1 = (bf16[2,720,128]{2,1,0:T(8,128)(2,1)S(1)}, bf16[2,720,128]{2,1,0:T(8,128)(2,1)S(1)}, u32[]{:S(2)}, u32[]{:S(2)}) collective-permute-start(bf16[2,720,128]{2,1,0:T(8,128)(2,1)S(1)} %get-tuple-element.29), channel_id=1, source_target_pairs={{1,2},{2,1},{5,6},{6,5},{9,10},{10,9},{13,14},{14,13},{17,18},{18,... | collective-permute-start | bytes 1105928 | tf_op jit(solution)/shard_map/ppermute | solution.py:275
  4.8 15.7 %collective-permute-start.4 = (bf16[720,128]{1,0:T(8,128)(2,1)S(1)}, bf16[720,128]{1,0:T(8,128)(2,1)S(1)}, u32[]{:S(2)}, u32[]{:S(2)}) collective-permute-start(bf16[720,128]{1,0:T(8,128)(2,1)S(1)} %get-tuple-element.33), channel_id=1, source_target_pairs={{0,16},{4,20},{8,24},{12,28},{16,0},{20,4},{24,8},{28,12},{1,17},{... | collective-permute-start | bytes 552968 | tf_op jit(solution)/shard_map/ppermute | solution.py:25
  8.5 17.2 %collective-permute-start.5 = (bf16[720,128]{1,0:T(8,128)(2,1)S(1)}, bf16[720,128]{1,0:T(8,128)(2,1)S(1)}, u32[]{:S(2)}, u32[]{:S(2)}) collective-permute-start(bf16[720,128]{1,0:T(8,128)(2,1)S(1)} %get-tuple-element.34), channel_id=1, source_target_pairs={{0,24},{4,28},{8,16},{12,20},{16,8},{20,12},{24,0},{28,4},{1,25},{... | collective-permute-start | bytes 552968 | tf_op jit(solution)/shard_map/ppermute | solution.py:25
  12.6 13.1 %collective-permute-start.6 = (bf16[1440,128]{1,0:T(8,128)(2,1)S(1)}, bf16[1440,128]{1,0:T(8,128)(2,1)S(1)}, u32[]{:S(2)}, u32[]{:S(2)}) collective-permute-start(bf16[1440,128]{1,0:T(8,128)(2,1)S(1)} %join_pieces.7.refs_0_.refs_3_), channel_id=1, source_target_pairs={{0,4},{4,0},{8,12},{12,8},{16,20},{20,16},{24,28},{28,24},{1,5},{5... | collective-permute-start | bytes 1105928 | tf_op jit(solution)/shard_map/ppermute | solution.py:25
  14.2 18.6 %collective-permute-start.9 = (bf16[1440,128]{1,0:T(8,128)(2,1)S(1)}, bf16[1440,128]{1,0:T(8,128)(2,1)S(1)}, u32[]{:S(2)}, u32[]{:S(2)}) collective-permute-start(bf16[1440,128]{1,0:T(8,128)(2,1)S(1)} %join_pieces.10), channel_id=1, source_target_pairs={{0,8},{4,12},{8,0},{12,4},{16,24},{20,28},{24,16},{28,20},{1,9},{5... | collective-permute-start | bytes 1105928 | tf_op jit(solution)/shard_map/ppermute | solution.py:25
  14.5 21.7 %collective-permute-start.2 = (bf16[720,128]{1,0:T(8,128)(2,1)S(1)}, bf16[720,128]{1,0:T(8,128)(2,1)S(1)}, u32[]{:S(2)}, u32[]{:S(2)}) collective-permute-start(bf16[720,128]{1,0:T(8,128)(2,1)S(1)} %get-tuple-element.31), channel_id=1, source_target_pairs={{0,16},{4,20},{8,24},{12,28},{16,0},{20,4},{24,8},{28,12},{1,17},{... | collective-permute-start | bytes 552968 | tf_op jit(solution)/shard_map/ppermute | solution.py:25
  20.4 15.7 %collective-permute-start.3 = (bf16[720,128]{1,0:T(8,128)(2,1)S(1)}, bf16[720,128]{1,0:T(8,128)(2,1)S(1)}, u32[]{:S(2)}, u32[]{:S(2)}) collective-permute-start(bf16[720,128]{1,0:T(8,128)(2,1)S(1)} %get-tuple-element.32), channel_id=1, source_target_pairs={{0,24},{4,28},{8,16},{12,20},{16,8},{20,12},{24,0},{28,4},{1,25},{... | collective-permute-start | bytes 552968 | tf_op jit(solution)/shard_map/ppermute | solution.py:25
  25.7 10.6 %collective-permute-start.7 = (bf16[1440,128]{1,0:T(8,128)(2,1)S(1)}, bf16[1440,128]{1,0:T(8,128)(2,1)S(1)}, u32[]{:S(2)}, u32[]{:S(2)}) collective-permute-start(bf16[1440,128]{1,0:T(8,128)(2,1)S(1)} %join_pieces.9.refs_0_.refs_11_), channel_id=1, source_target_pairs={{0,4},{4,0},{8,12},{12,8},{16,20},{20,16},{24,28},{28,24},{1,5},{5... | collective-permute-start | bytes 1105928 | tf_op jit(solution)/shard_map/ppermute | solution.py:25
  32.8 11.5 %collective-permute-start.14 = (bf16[1440,128]{1,0:T(8,128)(2,1)S(1)}, bf16[1440,128]{1,0:T(8,128)(2,1)S(1)}, u32[]{:S(2)}, u32[]{:S(2)}) collective-permute-start(bf16[1440,128]{1,0:T(8,128)(2,1)S(1)} %collective-permute-done.9.refs_2_.refs_7_), channel_id=1, source_target_pairs={{0,4},{4,0},{8,12},{12,8},{16,20},{20,16},{24,28},{28,24},{1,5},{5... | collective-permute-start | bytes 1105928 | tf_op jit(solution)/shard_map/ppermute | solution.py:25
  36.3 9.1 %collective-permute-start.11 = (bf16[1440,128]{1,0:T(8,128)(2,1)S(1)}, bf16[1440,128]{1,0:T(8,128)(2,1)S(1)}, u32[]{:S(2)}, u32[]{:S(2)}) collective-permute-start(bf16[1440,128]{1,0:T(8,128)(2,1)S(1)} %join_pieces.9.refs_0_.refs_11_), channel_id=1, source_target_pairs={{0,1},{1,0},{2,3},{3,2},{4,5},{5,4},{6,7},{7,6},{8,9},{9,8},{10,11... | collective-permute-start | bytes 1105928 | tf_op jit(solution)/shard_map/ppermute | solution.py:25
  39.1 5.8 %collective-permute-start.12 = (bf16[1440,128]{1,0:T(8,128)(2,1)S(1)}, bf16[1440,128]{1,0:T(8,128)(2,1)S(1)}, u32[]{:S(2)}, u32[]{:S(2)}) collective-permute-start(bf16[1440,128]{1,0:T(8,128)(2,1)S(1)} %join_pieces.8.refs_0_.refs_15_), channel_id=1, source_target_pairs={{0,1},{1,0},{2,3},{3,2},{4,5},{5,4},{6,7},{7,6},{8,9},{9,8},{10,11... | collective-permute-start | bytes 1105928 | tf_op jit(solution)/shard_map/ppermute | solution.py:25
  39.2 12.7 %collective-permute-start.17 = (bf16[1440,128]{1,0:T(8,128)(2,1)S(1)}, bf16[1440,128]{1,0:T(8,128)(2,1)S(1)}, u32[]{:S(2)}, u32[]{:S(2)}) collective-permute-start(bf16[1440,128]{1,0:T(8,128)(2,1)S(1)} %join_pieces.8.refs_0_.refs_15_), channel_id=1, source_target_pairs={{0,4},{4,0},{8,12},{12,8},{16,20},{20,16},{24,28},{28,24},{1,5},{5... | collective-permute-start | bytes 1105928 | tf_op jit(solution)/shard_map/ppermute | solution.py:25
  44.3 8.8 %collective-permute-start.16 = (bf16[1440,128]{1,0:T(8,128)(2,1)S(1)}, bf16[1440,128]{1,0:T(8,128)(2,1)S(1)}, u32[]{:S(2)}, u32[]{:S(2)}) collective-permute-start(bf16[1440,128]{1,0:T(8,128)(2,1)S(1)} %join_pieces.12.refs_13_), channel_id=1, source_target_pairs={{0,1},{1,0},{2,3},{3,2},{4,5},{5,4},{6,7},{7,6},{8,9},{9,8},{10,11... | collective-permute-start | bytes 1105928 | tf_op jit(solution)/shard_map/ppermute | solution.py:25
  44.4 7.5 %collective-permute-start.8 = (bf16[1440,128]{1,0:T(8,128)(2,1)S(1)}, bf16[1440,128]{1,0:T(8,128)(2,1)S(1)}, u32[]{:S(2)}, u32[]{:S(2)}) collective-permute-start(bf16[1440,128]{1,0:T(8,128)(2,1)S(1)} %join_pieces.7.refs_0_.refs_3_), channel_id=1, source_target_pairs={{0,1},{1,0},{2,3},{3,2},{4,5},{5,4},{6,7},{7,6},{8,9},{9,8},{10,11... | collective-permute-start | bytes 1105928 | tf_op jit(solution)/shard_map/ppermute | solution.py:25
  44.9 7.0 %collective-permute-start.10 = (bf16[1440,128]{1,0:T(8,128)(2,1)S(1)}, bf16[1440,128]{1,0:T(8,128)(2,1)S(1)}, u32[]{:S(2)}, u32[]{:S(2)}) collective-permute-start(bf16[1440,128]{1,0:T(8,128)(2,1)S(1)} %collective-permute-done.9.refs_2_.refs_7_), channel_id=1, source_target_pairs={{0,1},{1,0},{2,3},{3,2},{4,5},{5,4},{6,7},{7,6},{8,9},{9,8},{10,11... | collective-permute-start | bytes 1105928 | tf_op jit(solution)/shard_map/ppermute | solution.py:25
  45.4 7.7 %collective-permute-start.13 = (bf16[1440,128]{1,0:T(8,128)(2,1)S(1)}, bf16[1440,128]{1,0:T(8,128)(2,1)S(1)}, u32[]{:S(2)}, u32[]{:S(2)}) collective-permute-start(bf16[1440,128]{1,0:T(8,128)(2,1)S(1)} %collective-permute-done.6.refs_5_), channel_id=1, source_target_pairs={{0,1},{1,0},{2,3},{3,2},{4,5},{5,4},{6,7},{7,6},{8,9},{9,8},{10,11... | collective-permute-start | bytes 1105928 | tf_op jit(solution)/shard_map/ppermute | solution.py:25
  57.4 10.5 %collective-permute-start.19 = (f16[136,256]{1,0:T(8,128)(2,1)S(1)}, f16[136,256]{1,0:T(8,128)(2,1)S(1)}, u32[]{:S(2)}, u32[]{:S(2)}) collective-permute-start(f16[136,256]{1,0:T(8,128)(2,1)S(1)} %get-tuple-element.49), channel_id=1, source_target_pairs={{0,26},{1,27},{2,24},{3,25},{4,30},{5,31},{6,28},{7,29},{8,18},{9,... | collective-permute-start | bytes 208904 | tf_op jit(solution)/shard_map/ppermute | solution.py:323
  58.9 10.5 %collective-permute-start.25 = (f16[136,256]{1,0:T(8,128)(2,1)S(1)}, f16[136,256]{1,0:T(8,128)(2,1)S(1)}, u32[]{:S(2)}, u32[]{:S(2)}) collective-permute-start(f16[136,256]{1,0:T(8,128)(2,1)S(1)} %get-tuple-element.50), channel_id=1, source_target_pairs={{0,18},{1,19},{2,16},{3,17},{4,22},{5,23},{6,20},{7,21},{8,26},{9,... | collective-permute-start | bytes 208904 | tf_op jit(solution)/shard_map/ppermute | solution.py:323
  63.6 6.8 %collective-permute-start.24 = (f16[136,256]{1,0:T(8,128)(2,1)S(1)}, f16[136,256]{1,0:T(8,128)(2,1)S(1)}, u32[]{:S(2)}, u32[]{:S(2)}) collective-permute-start(f16[136,256]{1,0:T(8,128)(2,1)S(1)} %get-tuple-element.51), channel_id=1, source_target_pairs={{0,8},{1,9},{2,10},{3,11},{4,12},{5,13},{6,14},{7,15},{8,0},{9,1},... | collective-permute-start | bytes 208904 | tf_op jit(solution)/shard_map/ppermute | solution.py:323
  64.1 6.4 %collective-permute-start.23 = (f16[136,256]{1,0:T(8,128)(2,1)S(1)}, f16[136,256]{1,0:T(8,128)(2,1)S(1)}, u32[]{:S(2)}, u32[]{:S(2)}) collective-permute-start(f16[136,256]{1,0:T(8,128)(2,1)S(1)} %get-tuple-element.52), channel_id=1, source_target_pairs={{0,2},{1,3},{2,0},{3,1},{4,6},{5,7},{6,4},{7,5},{8,10},{9,11},{10,... | collective-permute-start | bytes 208904 | tf_op jit(solution)/shard_map/ppermute | solution.py:323
  65.0 7.7 %collective-permute-start.22 = (f16[136,256]{1,0:T(8,128)(2,1)S(1)}, f16[136,256]{1,0:T(8,128)(2,1)S(1)}, u32[]{:S(2)}, u32[]{:S(2)}) collective-permute-start(f16[136,256]{1,0:T(8,128)(2,1)S(1)} %get-tuple-element.53), channel_id=1, source_target_pairs={{0,24},{1,25},{2,26},{3,27},{4,28},{5,29},{6,30},{7,31},{8,16},{9,... | collective-permute-start | bytes 208904 | tf_op jit(solution)/shard_map/ppermute | solution.py:323
  67.9 6.0 %collective-permute-start.21 = (f16[136,256]{1,0:T(8,128)(2,1)S(1)}, f16[136,256]{1,0:T(8,128)(2,1)S(1)}, u32[]{:S(2)}, u32[]{:S(2)}) collective-permute-start(f16[136,256]{1,0:T(8,128)(2,1)S(1)} %get-tuple-element.54), channel_id=1, source_target_pairs={{0,10},{1,11},{2,8},{3,9},{4,14},{5,15},{6,12},{7,13},{8,2},{9,3},... | collective-permute-start | bytes 208904 | tf_op jit(solution)/shard_map/ppermute | solution.py:323
  69.4 5.3 %collective-permute-start.20 = (f16[136,256]{1,0:T(8,128)(2,1)S(1)}, f16[136,256]{1,0:T(8,128)(2,1)S(1)}, u32[]{:S(2)}, u32[]{:S(2)}) collective-permute-start(f16[136,256]{1,0:T(8,128)(2,1)S(1)} %get-tuple-element.55), channel_id=1, source_target_pairs={{0,16},{1,17},{2,18},{3,19},{4,20},{5,21},{6,22},{7,23},{8,24},{9,... | collective-permute-start | bytes 208904 | tf_op jit(solution)/shard_map/ppermute | solution.py:323
  (2 other events, 3.6 us)
